TPU v7x, 256 devices: a whole 4x4x8 slice. The times are simulated.
256 devices in a mesh: leaf: 64 (over x, z, core), sub: 4 (over y).
Axes of the slice: x: 4, y: 4, z: 8, core: 2. Of those that a mesh axis runs over, the one named last changes fastest.
Arguments:
- vectors: bfloat16 [16, 524288], P(None, ('leaf', 'sub')), may hold values from -6 to 6
- leaf_size: int32 [8192], P(('leaf', 'sub')), may hold values from 1 to 64, 393216 in all
- leaf_basis: bfloat16 [8192, 4096], P(('leaf', 'sub')), may hold values from -0.75 to 0.75
- near_blocks: bfloat16 [8192, 3, 4096], P(('leaf', 'sub')), may hold values from -0.4375 to 0.4375
- leaf_links: int32 [8192, 8], P(('leaf', 'sub')), may hold values from 0 to 8191, as said below
- leaf_coupling: bfloat16 [8192, 8, 4096], P(('leaf', 'sub')), may hold values from -0.25 to 0.25
- leaf_transfer: bfloat16 [8192, 4096], P(('leaf', 'sub')), may hold values from -0.1875 to 0.1875
- node_transfer: bfloat16 [128, 4096], replicated, may hold values from -0.5 to 0.5
- node_links: int32 [128, 3], replicated, may hold values from 1 to 127, as said below
- node_coupling: bfloat16 [128, 3, 4096], replicated, may hold values from -0.4375 to 0.4375
Outputs:
- product: bfloat16 [16, 524288], P(None, ('leaf', 'sub'))
Inputs may be any that keep to these rules, and one draw needn't show every extreme that they name: `leaf_size`: the sizes sum to 393216 and some leaf is full. `leaf_links`: the partners of leaf l lie in its branch (index // 128 equal to l // 128), and in the branch's cyclic order of leaves none is l or adjacent to l. `node_links`: for rows k from 8 on, every partner is a node of k's level that in the level's cyclic order is neither k nor adjacent to k; rows under 8 are not read.
All inputs are finite; a program needn't handle non-finite values. No bound on the sum of `leaf_size` on one device may be relied on, other than what follows from the above.
Results may differ from a plain program's by a relative error of at most 0.0055.
Values may be sent and summed in bfloat16 or wider, within the bound.
No kernel may reach another device: no remote copies, remote signals or barrier semaphores. Data moves between devices by JAX's collectives and lax.ppermute only.
A program may use at most 64 MiB of HBM per device.

v0:
```python
import jax
import jax.numpy as jnp
from jax import lax
from jax.sharding import PartitionSpec as P

LEAF_PTS = 64
RANK = 64


highest = lax.Precision.HIGHEST


def padded_2(cells, sides, width):
    for axis, dim in sides:
        count = lax.axis_size(axis)
        ends = count - 1
        head = lax.slice_in_dim(cells, 0, width, axis=dim)
        tail = lax.slice_in_dim(cells, cells.shape[dim] - width, cells.shape[dim], axis=dim)
        cells = jnp.concatenate(
            [
                lax.ppermute(tail, axis, [(i, (i + 1) % count) for i in range(ends)]),
                cells,
                lax.ppermute(head, axis, [((i + 1) % count, i) for i in range(ends)]),
            ],
            axis=dim,
        )
    return cells


def from_partner(block, axis, stride):
    count = lax.axis_size(axis)
    route = []
    for low in range(count):
        high = low | 1 << stride
        if high != low and high < count:
            route += [(low, high), (high, low)]
    return lax.ppermute(block, axis, route)


def ancestor_sum(level_rows, node_id, level_size, node_links, node_coupling):
    partners = node_links[node_id] - level_size
    gathered = jnp.take(level_rows, partners, axis=0)
    matrices = node_coupling[node_id].astype(jnp.float32).reshape(-1, RANK, RANK)
    return jnp.einsum("ckr,crs->ks", gathered, matrices, precision=highest)


def descend(coupled_map, ascending, branch, branches, node_transfer):
    downward = coupled_map[ascending[0]]
    for level_size in ascending[1:]:
        node_id = level_size + branch // (branches // level_size)
        transfer = node_transfer[node_id].astype(jnp.float32).reshape(RANK, RANK)
        downward = coupled_map[level_size] + jnp.dot(downward, transfer.T, precision=highest)
    return downward


def body(
    vectors,
    leaf_size,
    leaf_basis,
    near_blocks,
    leaf_links,
    leaf_coupling,
    leaf_transfer,
    node_transfer,
    node_links,
    node_coupling,
):
    leaf_count = leaf_size.shape[0]
    columns = vectors.shape[0]
    point_span = leaf_count * LEAF_PTS
    present = lax.broadcasted_iota(jnp.int32, (leaf_count, LEAF_PTS), 1) < leaf_size[:, None]
    masked = jnp.where(present.reshape(1, point_span), vectors, jnp.zeros_like(vectors))
    padded = padded_2(masked, ((("leaf", "sub"), 1),), LEAF_PTS)
    blocks = near_blocks.reshape(leaf_count, 3, LEAF_PTS, LEAF_PTS)
    near_field = jnp.zeros((columns, leaf_count, LEAF_PTS), jnp.float32)
    for neighbour in range(3):
        shifted = padded[:, neighbour * LEAF_PTS : neighbour * LEAF_PTS + point_span].reshape(
            columns, leaf_count, LEAF_PTS
        )
        near_field = near_field + jnp.einsum(
            "lpq,klq->klp", blocks[:, neighbour], shifted, preferred_element_type=jnp.float32
        )
    basis_mats = leaf_basis.reshape(leaf_count, LEAF_PTS, RANK)
    own_points = masked.reshape(columns, leaf_count, LEAF_PTS)
    coeffs = jnp.einsum(
        "klp,lpr->lkr", own_points, basis_mats, preferred_element_type=jnp.float32
    ).astype(jnp.bfloat16)
    transfers = leaf_transfer.reshape(leaf_count, RANK, RANK)
    partial_sum = jnp.einsum("lkr,lrs->ks", coeffs, transfers, preferred_element_type=jnp.float32)
    gathered = lax.all_gather(coeffs, "sub", axis=0, tiled=True)
    branch = lax.axis_index("leaf")
    branches = lax.axis_size("leaf")
    first_leaf = branch * lax.axis_size("sub") * leaf_count
    picked = jnp.take(gathered, leaf_links - first_leaf, axis=0)
    coupling = leaf_coupling.reshape(leaf_count, leaf_links.shape[1], RANK, RANK)
    linked = jnp.einsum("lckr,lcrs->lks", picked, coupling, preferred_element_type=jnp.float32)
    ascending = []
    level_size = 8
    while level_size <= branches:
        ascending.append(level_size)
        level_size = level_size * 2
    coupled_map = {}
    current = lax.psum(partial_sum, "sub")
    for level_size in ascending[::-1]:
        stride = branches // level_size
        level_all = lax.all_gather(current[None], "leaf", axis=0, tiled=True)
        grouped = level_all.reshape(level_size, stride, columns, RANK)
        level_rows = lax.dynamic_index_in_dim(grouped, branch % stride, 1, keepdims=False)
        node_id = level_size + branch // stride
        coupled_map[level_size] = ancestor_sum(
            level_rows, node_id, level_size, node_links, node_coupling
        )
        if level_size > 8:
            sibling = from_partner(current, "leaf", stride.bit_length() - 1)
            own_matrix = node_transfer[node_id].astype(jnp.float32).reshape(RANK, RANK)
            other_matrix = (
                node_transfer[jnp.bitwise_xor(node_id, 1)].astype(jnp.float32).reshape(RANK, RANK)
            )
            current = jnp.dot(current, own_matrix, precision=highest) + jnp.dot(
                sibling, other_matrix, precision=highest
            )
    downward = descend(coupled_map, ascending, branch, branches, node_transfer).astype(jnp.bfloat16)
    far_field = (
        linked + jnp.einsum("ks,lrs->lkr", downward, transfers, preferred_element_type=jnp.float32)
    ).astype(jnp.bfloat16)
    expanded = jnp.einsum("lkr,lpr->klp", far_field, basis_mats, preferred_element_type=jnp.float32)
    combined = jnp.where(present[None], near_field + expanded, jnp.zeros_like(expanded))
    return combined.astype(jnp.bfloat16).reshape(columns, point_span)


def solution(mesh):
    placed = (
        P(None, ("leaf", "sub")),
        P(("leaf", "sub")),
        P(("leaf", "sub"), None),
        P(("leaf", "sub"), None, None),
        P(("leaf", "sub"), None),
        P(("leaf", "sub"), None, None),
        P(("leaf", "sub"), None),
        P(),
        P(),
        P(),
    )
    return jax.shard_map(
        body, mesh=mesh, in_specs=placed, out_specs=P(None, ("leaf", "sub")), check_vma=False
    )
```

profile of v0, /device:TPU:1, one launch (start us, length us, event | category | flops | bytes accessed | tf_op | source)
XLA Modules:
  0.0 296.9 jit_solution(9834771245900300150)
XLA Ops:
  0.8 0.9 broadcast_select_fusion
  2.4 6.0 %collective-permute-start.1 = (bf16[16,64]{1,0:T(8,128)(2,1)}, bf16[16,64]{1,0:T(8,128)(2,1)}, u32[]{:S(2)}, u32[]{:S(2)}) collective-permute-start(bf16[16,64]{1,0:T(8,128)(2,1)} %get-tuple-element.23), channel_id=1, source_target_pairs={{1,0},{2,1},{3,2},{4,3},{5,4},{6,5},{7,6},{8,7},{9,8},{10,9},{11,1... | collective-permute-start | bytes 6152 | tf_op jit(solution)/shard_map/ppermute | solution.py:23
  8.4 1.9 collective-permute-start
  10.5 1.5 reshape.235
  12.0 1.5 reshape.237
  14.0 9.9 %psum.7 = f32[16,64]{1,0:T(8,128)} all-reduce(f32[16,64]{1,0:T(8,128)S(1)} %convolution_bitcast_fusion.6), channel_id=1, replica_groups=mesh['leaf'=64,'sub'=4] {'sub'}, use_global_device_ids=true, to_apply=%region_0.1 | all-reduce | flops 1024 | bytes 8192 | tf_op jit(solution)/shard_map/psum | solution.py:103
  23.9 1.8 collective-permute-start.2
  25.7 10.5 %all_gather.15 = bf16[128,16,64]{2,1,0:T(8,128)(2,1)S(1)} all-gather(bf16[32,16,64]{2,1,0:T(8,128)(2,1)S(1)} %convolution_convert_fusion), channel_id=1, replica_groups=mesh['leaf'=64,'sub'=4] {'sub'}, dimensions={0}, use_global_device_ids=true | all-gather | bytes 327680 | tf_op jit(solution)/shard_map/all_gather | solution.py:90
  36.2 61.1 %all-gather = f32[1024,64]{1,0:T(8,128)} all-gather(f32[16,64]{1,0:T(8,128)} %psum.7), channel_id=2, replica_groups=mesh['leaf'=64,'sub'=4] {'leaf'}, dimensions={0}, use_global_device_ids=true | all-gather | bytes 266240 | tf_op jit(solution)/shard_map/all_gather | solution.py:106
  100.9 2.5 reshape.232
  103.8 6.9 %reshape.236 = bf16[32,8,64,64]{3,2,1,0:T(8,128)(2,1)} reshape(bf16[32,8,4096]{2,1,0:T(8,128)(2,1)} %param.15) | data formatting | bytes 4194304 | tf_op jit(solution)/shard_map/reshape | solution.py:95
  111.0 2.5 dynamic-slice_reduce_fusion
  113.5 0.9 reshape.238
  114.9 1.9 dynamic-slice_reduce_fusion.4
  116.9 0.8 reshape.239
  117.6 1.4 fusion.41
  119.1 1.2 pad_clamp_fusion.2
  120.2 1.3 pad_clamp_fusion.1
  121.5 1.8 gather_fusion
  123.3 1.7 gather_fusion.1
  125.1 3.6 %convolution_bitcast_fusion.1 = f32[32,16,64]{2,1,0:T(8,128)S(1)} fusion(bf16[32,8,64,64]{3,2,1,0:T(8,128)(2,1)} %reshape.236, bf16[32,8,16,64]{3,2,1,0:T(8,128)(2,1)} %bitcast.92, pred[32,8]{1,0:T(8,128)(4,1)S(1)} %copy.24), kind=kOutput, calls=%fused_computation.8 | convolution fusion | flops 33816576 | bytes 2752768 | tf_op jit(solution)/shard_map/lckr,lcrs->lks/dot_general | solution.py:96
  128.7 0.9 convolution_bitcast_fusion.5
  135.8 0.8 pad_maximum_fusion
  137.8 0.8 convolution_add_fusion.8
  138.6 48.9 %all-gather.1 = f32[1024,64]{1,0:T(8,128)S(1)} all-gather(f32[16,64]{1,0:T(8,128)S(1)} %convolution_add_fusion.8), channel_id=3, replica_groups=mesh['leaf'=64,'sub'=4] {'leaf'}, dimensions={0}, use_global_device_ids=true | all-gather | bytes 266240 | tf_op jit(solution)/shard_map/all_gather | solution.py:106
  188.3 1.0 convolution_bitcast_fusion.4
  190.0 0.8 convolution_add_fusion.7
  190.8 49.5 %all-gather.2 = f32[1024,64]{1,0:T(8,128)S(1)} all-gather(f32[16,64]{1,0:T(8,128)S(1)} %convolution_add_fusion.7), channel_id=4, replica_groups=mesh['leaf'=64,'sub'=4] {'leaf'}, dimensions={0}, use_global_device_ids=true | all-gather | bytes 266240 | tf_op jit(solution)/shard_map/all_gather | solution.py:106
  242.0 1.8 collective-permute-done.4
  243.9 49.8 %all-gather.3 = f32[1024,64]{1,0:T(8,128)S(1)} all-gather(f32[16,64]{1,0:T(8,128)S(1)} %convolution_add_fusion.6), channel_id=5, replica_groups=mesh['leaf'=64,'sub'=4] {'leaf'}, dimensions={0}, use_global_device_ids=true | all-gather | bytes 266240 | tf_op jit(solution)/shard_map/all_gather | solution.py:106
  295.2 0.8 fusion.4
  296.1 0.8 reshape.251
  (101 shorter events, 18.8 us)
Async XLA Ops:
  0.7 9.6 %copy-start.10 = (pred[32,64]{1,0:T(8,128)(4,1)}, pred[32,64]{1,0:T(8,128)(4,1)S(1)}, u32[]{:S(2)}) copy-start(pred[32,64]{1,0:T(8,128)(4,1)S(1)} %iota_compare_fusion) | copy-start | bytes 6148
  1.7 22.2 %copy-start = (bf16[16,2048]{1,0:T(8,128)(2,1)}, bf16[16,2048]{1,0:T(8,128)(2,1)S(1)}, u32[]{:S(2)}) copy-start(bf16[16,2048]{1,0:T(8,128)(2,1)S(1)} %broadcast_select_fusion) | copy-start | bytes 196612
  2.4 133.4 %collective-permute-start.1 = (bf16[16,64]{1,0:T(8,128)(2,1)}, bf16[16,64]{1,0:T(8,128)(2,1)}, u32[]{:S(2)}, u32[]{:S(2)}) collective-permute-start(bf16[16,64]{1,0:T(8,128)(2,1)} %get-tuple-element.23), channel_id=1, source_target_pairs={{1,0},{2,1},{3,2},{4,3},{5,4},{6,5},{7,6},{8,7},{9,8},{10,9},{11,1... | collective-permute-start | bytes 6152 | tf_op jit(solution)/shard_map/ppermute | solution.py:23
  8.4 127.4 %collective-permute-start = (bf16[16,64]{1,0:T(8,128)(2,1)}, bf16[16,64]{1,0:T(8,128)(2,1)}, u32[]{:S(2)}, u32[]{:S(2)}) collective-permute-start(bf16[16,64]{1,0:T(8,128)(2,1)} %get-tuple-element.24), channel_id=1, source_target_pairs={{0,1},{1,2},{2,3},{3,4},{4,5},{5,6},{6,7},{7,8},{8,9},{9,10},{10,1... | collective-permute-start | bytes 6152 | tf_op jit(solution)/shard_map/ppermute | solution.py:21
  10.5 86.8 %copy-start.16 = (s32[128,3]{0,1:T(4,128)S(1)}, s32[128,3]{0,1:T(4,128)}, u32[]{:S(2)}) copy-start(s32[128,3]{0,1:T(4,128)} %param.18) | copy-start | bytes 4612
  23.9 113.9 %collective-permute-start.2 = (f32[16,64]{1,0:T(8,128)}, f32[16,64]{1,0:T(8,128)}, u32[]{:S(2)}, u32[]{:S(2)}) collective-permute-start(f32[16,64]{1,0:T(8,128)} %psum.7), channel_id=1, source_target_pairs={{0,4},{4,0},{8,12},{12,8},{16,20},{20,16},{24,28},{28,24},{32,36},... | collective-permute-start | bytes 12296 | tf_op jit(solution)/shard_map/ppermute | solution.py:37
  103.8 6.9 %copy-start.18 = (s32[32,8]{0,1:T(8,128)S(1)}, s32[32,8]{0,1:T(8,128)}, u32[]{:S(2)}) copy-start(s32[32,8]{0,1:T(8,128)} %param.14) | copy-start | bytes 3076
  125.0 3.7 %copy-start.21 = (pred[3]{0:T(512)(128)(4,1)S(1)}, pred[3]{0:T(512)(128)(4,1)}, u32[]{:S(2)}) copy-start(pred[3]{0:T(512)(128)(4,1)} %compare_and_fusion.4) | copy-start | bytes 13
  125.0 4.6 %copy-start.22 = (s32[3]{0:T(128)S(1)}, s32[3]{0:T(128)}, u32[]{:S(2)}) copy-start(s32[3]{0:T(128)} %fusion.34) | copy-start | bytes 40
  125.0 5.2 %copy-start.7 = (bf16[3,4096]{1,0:T(4,128)(2,1)S(1)}, bf16[3,4096]{1,0:T(4,128)(2,1)}, u32[]{:S(2)}) copy-start(bf16[3,4096]{1,0:T(4,128)(2,1)} %get-tuple-element.6) | copy-start | bytes 73732
  125.0 5.9 %copy-start.15 = (bf16[4096]{0:T(1024)(128)(2,1)S(1)}, bf16[4096]{0:T(1024)(128)(2,1)}, u32[]{:S(2)}) copy-start(bf16[4096]{0:T(1024)(128)(2,1)} %get-tuple-element.12) | copy-start | bytes 24580
  125.0 7.3 %copy-start.14 = (bf16[4096]{0:T(1024)(128)(2,1)S(1)}, bf16[4096]{0:T(1024)(128)(2,1)}, u32[]{:S(2)}) copy-start(bf16[4096]{0:T(1024)(128)(2,1)} %get-tuple-element.11) | copy-start | bytes 24580
  125.0 8.0 %copy-start.13 = (bf16[4096]{0:T(1024)(128)(2,1)S(1)}, bf16[4096]{0:T(1024)(128)(2,1)}, u32[]{:S(2)}) copy-start(bf16[4096]{0:T(1024)(128)(2,1)} %get-tuple-element.10) | copy-start | bytes 24580
  125.1 9.4 %copy-start.12 = (bf16[4096]{0:T(1024)(128)(2,1)S(1)}, bf16[4096]{0:T(1024)(128)(2,1)}, u32[]{:S(2)}) copy-start(bf16[4096]{0:T(1024)(128)(2,1)} %get-tuple-element.14) | copy-start | bytes 24580
  125.1 10.7 %copy-start.1 = (bf16[16,2048]{1,0:T(8,128)(2,1)S(1)}, bf16[16,2048]{1,0:T(8,128)(2,1)}, u32[]{:S(2)}) copy-start(bf16[16,2048]{1,0:T(8,128)(2,1)} %copy-done) | copy-start | bytes 196612
  136.9 0.9 copy-start.9
  136.9 50.6 %copy-start.4 = (bf16[64,64]{1,0:T(8,128)(2,1)S(1)}, bf16[64,64]{1,0:T(8,128)(2,1)}, u32[]{:S(2)}) copy-start(bf16[64,64]{1,0:T(8,128)(2,1)} %reshape.243) | copy-start | bytes 24580
  137.3 103.6 %copy-start.6 = (bf16[64,64]{1,0:T(8,128)(2,1)S(1)}, bf16[64,64]{1,0:T(8,128)(2,1)}, u32[]{:S(2)}) copy-start(bf16[64,64]{1,0:T(8,128)(2,1)} %reshape.247) | copy-start | bytes 24580
  137.3 104.4 %copy-start.3 = (bf16[3,64,64]{2,1,0:T(8,128)(2,1)S(1)}, bf16[3,64,64]{2,1,0:T(8,128)(2,1)}, u32[]{:S(2)}) copy-start(bf16[3,64,64]{2,1,0:T(8,128)(2,1)} %reshape.246) | copy-start | bytes 73732
  137.3 104.4 %copy-start.20 = (pred[3]{0:T(512)(128)(4,1)S(1)}, pred[3]{0:T(512)(128)(4,1)}, u32[]{:S(2)}) copy-start(pred[3]{0:T(512)(128)(4,1)} %get-tuple-element.26) | copy-start | bytes 13
  137.3 106.5 %copy-start.8 = (bf16[64,64]{1,0:T(8,128)(2,1)S(1)}, bf16[64,64]{1,0:T(8,128)(2,1)}, u32[]{:S(2)}) copy-start(bf16[64,64]{1,0:T(8,128)(2,1)} %reshape.248) | copy-start | bytes 24580
  137.4 157.1 %copy-start.2 = (bf16[3,64,64]{2,1,0:T(8,128)(2,1)S(1)}, bf16[3,64,64]{2,1,0:T(8,128)(2,1)}, u32[]{:S(2)}) copy-start(bf16[3,64,64]{2,1,0:T(8,128)(2,1)} %reshape.250) | copy-start | bytes 73732
  137.4 157.1 %copy-start.19 = (pred[3]{0:T(512)(128)(4,1)S(1)}, pred[3]{0:T(512)(128)(4,1)}, u32[]{:S(2)}) copy-start(pred[3]{0:T(512)(128)(4,1)} %get-tuple-element.25) | copy-start | bytes 13
  137.4 157.5 %copy-start.5 = (bf16[64,64]{1,0:T(8,128)(2,1)S(1)}, bf16[64,64]{1,0:T(8,128)(2,1)}, u32[]{:S(2)}) copy-start(bf16[64,64]{1,0:T(8,128)(2,1)} %reshape.243) | copy-start | bytes 24580
  137.4 157.6 %copy-start.17 = (f32[16,64]{1,0:T(8,128)S(1)}, f32[16,64]{1,0:T(8,128)}, u32[]{:S(2)}) copy-start(f32[16,64]{1,0:T(8,128)} %convolution_bitcast_fusion.5) | copy-start | bytes 12292
  137.4 157.8 %copy-start.11 = (pred[32,64]{1,0:T(8,128)(4,1)S(1)}, pred[32,64]{1,0:T(8,128)(4,1)}, u32[]{:S(2)}) copy-start(pred[32,64]{1,0:T(8,128)(4,1)} %copy-done.10) | copy-start | bytes 6148
  187.5 2.5 collective-permute-start.3
  240.4 3.4 %collective-permute-start.4 = (f32[16,64]{1,0:T(8,128)S(1)}, f32[16,64]{1,0:T(8,128)S(1)}, u32[]{:S(2)}, u32[]{:S(2)}) collective-permute-start(f32[16,64]{1,0:T(8,128)S(1)} %convolution_add_fusion.7), channel_id=1, source_target_pairs={{0,16},{16,0},{4,20},{20,4},{8,24},{24,8},{12,28},{28,12},{32,48},... | collective-permute-start | bytes 12296 | tf_op jit(solution)/shard_map/ppermute | solution.py:37
where the time goes:
time: 298 us; the launch traced here: 297 us
  blocking collectives  230 us (77%)
  local copies, waits for them, and re-layouts  32.2 us (11%)
  matrix products  12.4 us (4%)
  starting transfers between devices  10.2 us (3%)
  other arithmetic  9.37 us (3%)
    all_gather x4, blocking collectives, body(): level_all = lax.all_gather(current[None], 'leaf', axis=0, tiled=True)  209 us
    all_gather x1, blocking collectives, body(): gathered = lax.all_gather(coeffs, 'sub', axis=0, tiled=True)  10.5 us
    psum x1, blocking collectives, body(): current = lax.psum(partial_sum, 'sub')  9.95 us
    reshape x1, local copies, waits for them, and re-layouts, body(): leaf_coupling.reshape(leaf_count, leaf_links.shape[1], RANK, RANK)  6.92 us
    ppermute x1, starting transfers between devices, padded_2(): lax.ppermute(head, axis, [((i + 1) % count, i) for i in range(ends)])  6.02 us
  transfers between devices with their start and end apart: 5, of which 2 were waited for; matrix products, arithmetic and copies ran while one was open for 16% of the time, Pallas kernels for 0%

commit v1 on v0

v1 whole, which is shorter than its diff:
```python
import jax
import jax.numpy as jnp
from jax import lax
from jax.experimental import pallas as pl
from jax.experimental.pallas import tpu as pltpu
from jax.sharding import PartitionSpec as P

F32, BF16, I32 = jnp.float32, jnp.bfloat16, jnp.int32
TILES = 16
COEFF = 16 * 128
PAYLOAD = 19 * 128


def iota(shape, dim):
    return lax.broadcasted_iota(I32, shape, dim)


def dot(a, b):
    return jnp.dot(a, b, preferred_element_type=F32)


def dot_t(a, b):
    return lax.dot_general(a, b, (((1,), (1,)), ((), ())), preferred_element_type=F32)


def swap(x):
    return pltpu.roll(x, 64, 1)


def low_half(rows):
    return iota((rows, 128), 1) < 64


def tile(ref, j):
    return ref[:, 128 * j : 128 * j + 128]


def pieces(x):
    high = x.astype(BF16)
    return high, (x - high.astype(F32)).astype(BF16)


def split_map():
    row = iota((512, 128), 0)
    rank = row & 63
    target = (rank & 1) * 256 + (rank >> 1) * 8 + (row >> 6) - iota((512, 128), 1)
    return jnp.concatenate(
        [jnp.where(target == 128 * q, 1.0, 0.0).astype(BF16) for q in range(4)], axis=1
    )


def present(size_ref, j):
    lane = iota((16, 128), 1)
    limit = jnp.where(lane < 64, size_ref[2 * j], size_ref[2 * j + 1])
    return (lane & 63) < limit


def upward_kernel(size_ref, x_ref, basis_ref, transfer_ref, pay_ref, masked_ref, cross_ref, map_ref):
    lo = low_half(16)
    for j in range(TILES):
        kept = jnp.where(present(size_ref, j), tile(x_ref, j).astype(F32), 0.0)
        masked_ref[:, 128 * j : 128 * j + 128] = kept.astype(BF16)
    map_ref[...] = split_map()
    points = jnp.concatenate([masked_ref[:, 512 * g : 512 * g + 512] for g in range(4)], axis=0)
    spread = dot(points, map_ref[...]).astype(BF16)
    member = iota((16, 256), 1) & 7
    picks = [jnp.where(member == m, 1.0, 0.0).astype(BF16) for m in range(8)]
    for g in range(4):
        halves = [spread[16 * g : 16 * g + 16, 256 * h : 256 * h + 256] for h in range(2)]
        rows = jnp.concatenate([halves[h] * picks[m] for m in range(8) for h in range(2)], axis=0)
        out = dot(rows, basis_ref[g])
        for q in range(4):
            a0, a1, b0, b1 = [out[64 * q + 16 * n : 64 * q + 16 * n + 16] for n in range(4)]
            coeff = jnp.where(lo, a0 + swap(a1), swap(b0) + b1)
            j = 4 * g + q
            pay_ref[:, 128 * j : 128 * j + 128] = coeff.astype(BF16)
    coeffs = jnp.concatenate([pay_ref[:, 512 * g : 512 * g + 512] for g in range(4)], axis=0)
    spread = dot(coeffs, map_ref[...]).astype(BF16)
    total = jnp.zeros((32, 128), F32)
    for g in range(4):
        rows = jnp.concatenate(
            [spread[16 * g : 16 * g + 16, 256 * h : 256 * h + 256] for h in range(2)], axis=0
        )
        total = total + dot(rows, transfer_ref[g])
    share = jnp.where(lo, total[:16] + swap(total[16:]), swap(total[:16]) + total[16:])
    high = share.astype(BF16).astype(F32)
    pay_ref[:, COEFF : COEFF + 128] = jnp.where(lo, high, share - high).astype(BF16)
    first, last = tile(masked_ref, 0), tile(masked_ref, 15)
    pay_ref[:, COEFF + 128 : COEFF + 256] = first
    pay_ref[:, COEFF + 256 : COEFF + 384] = last
    at_start = lax.axis_index("sub") == 0
    cross_ref[...] = jnp.where(at_start, first.astype(F32), last.astype(F32)).astype(BF16)


def parity_rows(raw, count):
    even = (iota((count, 128), 0) & 1) == 0
    return jnp.where(low_half(count) == even, raw, swap(raw))


def prepare_kernel(
    masked_ref, near_ref, basis_ref, transfer_ref, nodes_ref, coupling_ref,
    field_ref, edge_ref, basis_out, transfer_out, nodes_out, coupled_out, map_out,
    sides_ref, near_f32, sums_ref, coupling_buf, coupling_sem,
):
    branch = lax.axis_index("leaf")
    own = [64 + branch, 32 + (branch >> 1), 16 + (branch >> 2), 8 + (branch >> 3)]
    copies = [
        pltpu.make_async_copy(coupling_ref.at[own[n]], coupling_buf.at[n], coupling_sem.at[n])
        for n in range(4)
    ]
    for copy in copies:
        copy.start()
    lo = low_half(16)
    map_out[...] = split_map()
    row, col = iota((512, 256), 0), iota((512, 256), 1)
    plain = jnp.where(((row >> 6) == (col & 7)) & (((row & 63) >> 1) == (col >> 3)), 1.0, 0.0).astype(BF16)
    member = (iota((512, 128), 0) >> 6) & 1
    own_half = (member == 0) == (iota((512, 128), 1) < 64)
    for g in range(4):
        for source, target in ((basis_ref, basis_out), (transfer_ref, transfer_out)):
            rows = parity_rows(dot(plain, source[g]), 512)
            target[512 * g : 512 * g + 512] = jnp.where(own_half, rows, 0.0).astype(BF16)

    def node_group(g, _):
        rows = parity_rows(dot(plain, nodes_ref[g + 2]), 512).astype(BF16)
        nodes_out[pl.ds(pl.multiple_of(g * 512, 512), 512), :] = rows
        return 0

    lax.fori_loop(0, 14, node_group, 0)

    sides_ref[0] = jnp.zeros((32, 128), BF16)
    sides_ref[33] = jnp.zeros((32, 128), BF16)
    for j in range(TILES):
        x = tile(masked_ref, j).astype(F32)
        y = swap(x)
        sides_ref[2 * j + 1, 0:16, :] = jnp.where(lo, x, 0.0).astype(BF16)
        sides_ref[2 * j + 1, 16:32, :] = jnp.where(lo, 0.0, y).astype(BF16)
        sides_ref[2 * j + 2, 0:16, :] = jnp.where(lo, y, 0.0).astype(BF16)
        sides_ref[2 * j + 2, 16:32, :] = jnp.where(lo, 0.0, x).astype(BF16)
    near_f32[...] = jnp.zeros((2, 128, 128), F32)
    which = iota((32, 128), 1) & 3

    def stage(slot, get):
        for i in range(32):
            near_f32[slot, 4 * i : 4 * i + 3, :] = get(i).astype(F32)
        return near_f32[slot].astype(BF16)

    def near_leaf(leaf, slot):
        block = stage(slot, lambda i: near_ref[leaf, i])
        out = dot_t(sides_ref[pl.ds(leaf, 3)].reshape(96, 128), block)
        near = jnp.where(which == 0, out[:32], jnp.where(which == 1, out[32:64], out[64:]))
        high, low = pieces(near)
        start = pl.multiple_of(leaf * 16, 16)
        for h in range(2):
            sums_ref[0, pl.ds(start, 16), 128 * h : 128 * h + 128] = high[16 * h : 16 * h + 16]
            sums_ref[1, pl.ds(start, 16), 128 * h : 128 * h + 128] = low[16 * h : 16 * h + 16]
        return block

    row, col = iota((64, 128), 0), iota((64, 128), 1)
    half = iota((64, 128), 1) < 64

    def edge(block, s):
        pick = jnp.where(((row >> 1) == (col >> 2)) & ((col & 3) == s), 1.0, 0.0).astype(BF16)
        return parity_rows(dot(pick, block), 64)

    zeros = jnp.zeros((64, 128), BF16)
    edge_ref[0, 0:64, :] = jnp.where(half, 0.0, edge(near_leaf(0, 0), 0)).astype(BF16)
    edge_ref[0, 64:128, :] = zeros
    edge_ref[1, 0:64, :] = zeros
    edge_ref[1, 64:128, :] = jnp.where(half, edge(near_leaf(31, 1), 2), 0.0).astype(BF16)

    def near_pair(n, _):
        near_leaf(2 * n + 1, 0)
        near_leaf(2 * n + 2, 1)
        return 0

    lax.fori_loop(0, 15, near_pair, 0)
    row, col = iota((256, 128), 0), iota((256, 128), 1)
    gather = jnp.where((col & 63) == ((row >> 7) + 2 * ((row & 127) >> 2)), 1.0, 0.0)
    gather = jnp.where((row & 3) == 3, 0.0, gather).astype(BF16)
    fields = dot(sums_ref[0], gather) + dot(sums_ref[1], gather)
    for j in range(TILES):
        field_ref[:, 128 * j : 128 * j + 128] = jnp.where(
            lo, fields[32 * j : 32 * j + 16], fields[32 * j + 16 : 32 * j + 32]
        )

    for copy in copies:
        copy.wait()
    row, col = iota((256, 128), 0), iota((256, 128), 1)
    order = jnp.where(((row >> 6) == (col & 3)) & (((row & 63) >> 1) == (col >> 2)), 1.0, 0.0).astype(BF16)

    def node(n):
        return nodes_out[pl.ds(pl.multiple_of((own[n] - 16) * 64, 64), 64), :]

    def both(x):
        x = x.astype(F32)
        return jnp.concatenate([jnp.where(half, x, 0.0), jnp.where(half, 0.0, x)], axis=0).astype(BF16)

    chain = [None]
    carried = (node(0), None)
    for n in range(1, 4):
        high, low = carried
        parts = [both(high)] + ([both(low)] if low is not None else [])
        chain.append(jnp.concatenate(parts, axis=0))
        if n < 3:
            below = node(n)
            longer = dot(high[:, :64], below)
            if low is not None:
                longer = longer + dot(low[:, :64], below)
            carried = pieces(longer)
    lo256 = low_half(256)
    for n in range(4):
        block = stage(n & 1, lambda i: coupling_buf[n, i])
        if n == 0:
            rows = jnp.where(lo256, parity_rows(dot(order, block), 256), 0.0)
        else:
            both_parts = dot_t(block, chain[n])
            summed = both_parts[:, :128]
            if n > 1:
                summed = summed + both_parts[:, 128:]
            high, low = pieces(summed)
            rows = jnp.where(
                lo256, parity_rows(dot(order, high), 256), parity_rows(dot(order, low), 256)
            )
        coupled_out[256 * n : 256 * n + 256, :] = rows.astype(BF16)


def message_kernel(own_ref, one_ref, two_ref, three_ref, out_ref):
    total = (
        own_ref[...].astype(F32) + one_ref[...].astype(F32)
        + two_ref[...].astype(F32) + three_ref[...].astype(F32)
    )
    total = total + swap(total)
    packed = jnp.where(low_half(8), total[:8], total[8:]).astype(BF16)
    for n in range(64):
        out_ref[n] = packed


def downward_kernel(
    size_ref, links_ref, node_links_ref, own_ref, one_ref, two_ref, three_ref, cross_ref, message_ref,
    coupling_ref, field_ref, edge_ref, basis_ref, transfer_ref, nodes_ref, coupled_ref, map_ref,
    out_ref,
    coeff_ref, picked_ref, spread_ref, linked_ref, table_ref,
):
    branch, sub = lax.axis_index("leaf"), lax.axis_index("sub")
    lo = low_half(16)
    lo8 = low_half(8)
    lo32 = low_half(32)

    pairs = []
    for q in range(32):
        one, two = message_ref[2 * q].astype(F32), message_ref[2 * q + 1].astype(F32)
        one_s, two_s = swap(one), swap(two)
        pairs.append(
            jnp.concatenate([jnp.where(lo8, one, two_s), jnp.where(lo8, one_s, two)], axis=0).astype(BF16)
        )
        first = jnp.concatenate([jnp.where(lo8, one, one_s), jnp.where(lo8, one_s, one)], axis=0)
        second = jnp.concatenate([jnp.where(lo8, two, two_s), jnp.where(lo8, two_s, two)], axis=0)
        zeros = jnp.zeros((16, 128), BF16)
        table_ref[64 + 2 * q] = jnp.concatenate([first.astype(BF16), zeros], axis=0)
        table_ref[65 + 2 * q] = jnp.concatenate([second.astype(BF16), zeros], axis=0)

    def weights(q):
        return nodes_ref[128 * (q - 8) : 128 * (q - 8) + 128, :]

    size = 32
    while size >= 8:
        parents = []
        for q in range(size, 2 * size):
            a = dot(pairs[q - size], weights(q))
            if size < 32:
                a = a[:16] + a[16:]
            high, low = pieces(a)
            parents.append(jnp.concatenate([high, low], axis=0))
            table_ref[q] = parents[-1]
        pairs = [
            jnp.where(lo32, parents[2 * q].astype(F32), parents[2 * q + 1].astype(F32)).astype(BF16)
            for q in range(size // 2)
        ]
        size = size // 2
    sources = []
    for n in range(4):
        own = (64 >> n) + (branch >> n)
        a, b, c = [table_ref[node_links_ref[own, m]].astype(F32) for m in range(3)]
        sources += [jnp.where(lo32, a, b).astype(BF16), jnp.where(lo32, c, 0.0).astype(BF16)]
    down = dot(jnp.concatenate(sources, axis=1), coupled_ref[...])
    down = down[:16] + down[16:]
    down = (down + swap(down)).astype(BF16)
    inherited = dot_t(down, transfer_ref[...])

    for d, ref in enumerate((own_ref, one_ref, two_ref, three_ref)):
        for j in range(TILES):
            x = tile(ref, j).astype(F32)
            y = swap(x)
            coeff_ref[32 * d + 2 * j] = jnp.where(lo, x, y).astype(BF16)
            coeff_ref[32 * d + 2 * j + 1] = jnp.where(lo, y, x).astype(BF16)
    for leaf in range(32):
        for c in range(4):
            ends = []
            for m in range(2):
                link = links_ref[leaf, 2 * c + m] & 127
                slot = ((sub - (link >> 5)) & 3) * 32 + (link & 31)
                ends.append(coeff_ref[slot].astype(F32))
            picked_ref[16 * leaf : 16 * leaf + 16, 128 * c : 128 * c + 128] = jnp.where(
                lo, ends[0], ends[1]
            ).astype(BF16)
    spread_ref[...] = dot(picked_ref[...], map_ref[...]).astype(BF16)
    for j in range(TILES):
        outs = []
        for leaf in (2 * j, 2 * j + 1):
            rows = spread_ref[16 * leaf : 16 * leaf + 16, :]
            outs.append(
                dot(jnp.concatenate([rows[:, :256], rows[:, 256:]], axis=0), coupling_ref[leaf])
            )
        a, b = outs
        linked_ref[:, 128 * j : 128 * j + 128] = jnp.where(
            lo, a[:16] + swap(a[16:]), swap(b[:16]) + b[16:]
        )

    left = jnp.where(sub == 0, cross_ref[...].astype(F32), tile(one_ref, 18).astype(F32)).astype(BF16)
    right = jnp.where(sub == 3, cross_ref[...].astype(F32), tile(three_ref, 17).astype(F32)).astype(BF16)
    for j in range(TILES):
        far = (linked_ref[:, 128 * j : 128 * j + 128] + inherited[:, 128 * j : 128 * j + 128]).astype(BF16)
        out = dot_t(far, basis_ref[128 * j : 128 * j + 128, :]) + tile(field_ref, j)
        if j == 0:
            out = out + dot_t(left, edge_ref[0])
        if j == 15:
            out = out + dot_t(right, edge_ref[1])
        out_ref[:, 128 * j : 128 * j + 128] = jnp.where(present(size_ref, j), out, 0.0).astype(BF16)


VMEM = pl.BlockSpec(memory_space=pltpu.VMEM)
SMEM = pl.BlockSpec(memory_space=pltpu.SMEM)
ANY = pl.BlockSpec(memory_space=pl.ANY)


def params(mib):
    return pltpu.CompilerParams(vmem_limit_bytes=mib << 20)


def cost(flops, size):
    return pl.CostEstimate(flops=flops, bytes_accessed=size, transcendentals=0)


def shape(dims, dtype=BF16):
    return jax.ShapeDtypeStruct(dims, dtype)


def grouped(table):
    rows = table.shape[0]
    return table.reshape(rows // 8, 8, 32, 128).transpose(0, 2, 1, 3).reshape(rows // 8, 256, 128)


def body(
    vectors, leaf_size, leaf_basis, near_blocks, leaf_links, leaf_coupling, leaf_transfer,
    node_transfer, node_links, node_coupling,
):
    basis, transfer, nodes = grouped(leaf_basis), grouped(leaf_transfer), grouped(node_transfer)
    coupling = leaf_coupling.reshape(32, 8, 32, 128).transpose(0, 2, 1, 3).reshape(32, 256, 128)
    near = near_blocks.reshape(32, 3, 32, 128).transpose(0, 2, 1, 3)
    node_coupled = node_coupling.reshape(128, 3, 32, 128).transpose(0, 2, 1, 3)

    payload, masked, cross = pl.pallas_call(
        upward_kernel,
        out_shape=[shape((16, PAYLOAD)), shape((16, 2048)), shape((16, 128))],
        in_specs=[SMEM, VMEM, VMEM, VMEM],
        out_specs=[VMEM, VMEM, VMEM],
        scratch_shapes=[pltpu.VMEM((512, 512), BF16)],
        compiler_params=params(16),
        cost_estimate=cost(10**8, 10**6),
        name="upward",
    )(leaf_size, vectors, basis, transfer)

    others = [
        lax.ppermute(payload, "sub", [(s, (s + d) % 4) for s in range(4)]) for d in (1, 2, 3)
    ]
    branches = lax.axis_size("leaf")
    routes = [(4 * b + 3, 4 * b + 4) for b in range(branches - 1)]
    routes += [(4 * b, 4 * b - 1) for b in range(1, branches)]
    cross = lax.ppermute(cross, ("leaf", "sub"), routes)

    field, edge, basis_p, transfer_p, nodes_p, coupled, split = pl.pallas_call(
        prepare_kernel,
        out_shape=[
            shape((16, 2048), F32), shape((2, 128, 128)), shape((2048, 128)), shape((2048, 128)),
            shape((56 * 128, 128)), shape((1024, 128)), shape((512, 512)),
        ],
        in_specs=[VMEM, VMEM, VMEM, VMEM, VMEM, ANY],
        out_specs=[VMEM] * 7,
        scratch_shapes=[
            pltpu.VMEM((34, 32, 128), BF16),
            pltpu.VMEM((2, 128, 128), F32),
            pltpu.VMEM((2, 512, 256), BF16),
            pltpu.VMEM((4, 32, 3, 128), BF16),
            pltpu.SemaphoreType.DMA((4,)),
        ],
        compiler_params=params(24),
        cost_estimate=cost(3 * 10**9, 6 * 10**6),
        name="prepare",
    )(masked, near, basis, transfer, nodes, node_coupled)

    share = pl.BlockSpec((16, 128), lambda n: (0, 16))
    messages = pl.pallas_call(
        message_kernel,
        grid=(1,),
        out_shape=shape((64, 8, 128)),
        in_specs=[share] * 4,
        out_specs=pl.BlockSpec((64, 8, 128), lambda n: (0, 0, 0)),
        compiler_params=params(4),
        name="message",
    )(payload, *others)
    messages = lax.all_to_all(messages, "leaf", 0, 0)

    return pl.pallas_call(
        downward_kernel,
        out_shape=shape((16, 2048)),
        in_specs=[SMEM] * 3 + [VMEM] * 14,
        out_specs=VMEM,
        scratch_shapes=[
            pltpu.VMEM((128, 16, 128), BF16),
            pltpu.VMEM((512, 512), BF16),
            pltpu.VMEM((512, 512), BF16),
            pltpu.VMEM((16, 2048), F32),
            pltpu.VMEM((128, 32, 128), BF16),
        ],
        compiler_params=params(24),
        name="downward",
    )(
        leaf_size, leaf_links, node_links, payload, *others, cross, messages,
        coupling, field, edge, basis_p, transfer_p, nodes_p, coupled, split,
    )


def solution(mesh):
    split = ("leaf", "sub")
    placed = (
        P(None, split), P(split), P(split, None), P(split, None, None), P(split, None),
        P(split, None, None), P(split, None), P(), P(), P(),
    )
    return jax.shard_map(
        body, mesh=mesh, in_specs=placed, out_specs=P(None, split), check_vma=False
    )
```

time: 298 us -> 73.9 us (0.25)
  blocking collectives: 230 us -> 0 us
  Pallas kernels: 0 us -> 17.1 us
  matrix products: 12.4 us -> 0 us
  starting transfers between devices: 10.2 us -> 20.7 us
  other arithmetic: 9.37 us -> 0 us
    all_gather x5 -> x0, blocking collectives: 220 us -> none  [the longest x4 209 us: body(): level_all = lax.all_gather(current[None], 'leaf', axis=0, tiled=True)]
    unnamed x46 -> x64, local copies, waits for them, and re-layouts: 0.1 us -> 28.9 us
    pallas_call x0 -> x4, Pallas kernels: none -> 17.1 us  [the longest x1 9.81 us: body(): pl.pallas_call(prepare_kernel, out_shape=[shape((16, 2048), F32), shape((...]
    reshape x18 -> x2, local copies, waits for them, and re-layouts: 20.9 us -> 6.12 us  [the longest x1 5.45 us: body(): node_coupled = node_coupling.reshape(128, 3, 32, 128).transpose(0, 2, 1, 3)]
    dot_general x20 -> x0, matrix products: 12.4 us -> none  [the longest x1 3.63 us: body(): jnp.einsum('lckr,lcrs->lks', picked, coupling, preferred_element_type=jnp...]
    all_to_all x0 -> x1, starting transfers between devices: none -> 11.9 us  [body(): messages = lax.all_to_all(messages, 'leaf', 0, 0)]
    psum x1 -> x0, blocking collectives: 9.95 us -> none  [body(): current = lax.psum(partial_sum, 'sub')]
    gather x5 -> x0, local copies, waits for them, and re-layouts: 5.48 us -> none  [the longest x4 3.72 us: ancestor_sum(): gathered = jnp.take(level_rows, partners, axis=0)]
  transfers between devices with their start and end apart: 5 -> 5, of which waited for: 2 -> 0; matrix products, arithmetic and copies ran while one was open for 16% -> 15% of each run, Pallas kernels for 0% -> 14%
where the time goes in v1:
time: 73.9 us; the launch traced here: 73 us
  local copies, waits for them, and re-layouts  35 us (47%)
  starting transfers between devices  20.7 us (28%)
  Pallas kernels  17.1 us (23%)
    unnamed x64, local copies, waits for them, and re-layouts  28.9 us
    all_to_all x1, starting transfers between devices, body(): messages = lax.all_to_all(messages, 'leaf', 0, 0)  11.9 us
    pallas_call x1, Pallas kernels, body(): pl.pallas_call(prepare_kernel, out_shape=[shape((16, 2048), F32), shape((...  9.81 us
    ppermute x3, starting transfers between devices, body(): lax.ppermute(payload, 'sub', [(s, (s + d) % 4) for s in range(4)])  5.81 us
    reshape x1, local copies, waits for them, and re-layouts, body(): node_coupled = node_coupling.reshape(128, 3, 32, 128).transpose(0, 2, 1, 3)  5.45 us
    pallas_call x1, Pallas kernels, body(): pl.pallas_call(downward_kernel, out_shape=shape((16, 2048)), in_specs=[SM...  5.08 us
    ppermute x1, starting transfers between devices, body(): cross = lax.ppermute(cross, ('leaf', 'sub'), routes)  3.03 us
    pallas_call x1, Pallas kernels, body(): pl.pallas_call(upward_kernel, out_shape=[shape((16, PAYLOAD)), shape((16,...  1.51 us
  transfers between devices with their start and end apart: 5, of which 0 were waited for; matrix products, arithmetic and copies ran while one was open for 15% of the time, Pallas kernels for 14%

profile of v1, /device:TPU:1, one launch (start us, length us, event | category | flops | bytes accessed | tf_op | source)
XLA Modules:
  0.0 73.0 jit_solution(2425957272178637132)
XLA Ops:
  0.0 0.9 %copy-done.14 = bf16[32,4096]{1,0:T(8,128)(2,1)S(1)} copy-done((bf16[32,4096]{1,0:T(8,128)(2,1)S(1)}, bf16[32,4096]{1,0:T(8,128)(2,1)}, u32[]{:S(2)}) %copy-start.14) | copy-done | bytes 262168
  1.0 0.9 %copy-done.16 = bf16[32,4096]{1,0:T(8,128)(2,1)S(1)} copy-done((bf16[32,4096]{1,0:T(8,128)(2,1)S(1)}, bf16[32,4096]{1,0:T(8,128)(2,1)}, u32[]{:S(2)}) %copy-start.16) | copy-done | bytes 262168
  1.9 0.8 %copy-done.22 = bf16[16,2048]{1,0:T(8,128)(2,1)S(1)} copy-done((bf16[16,2048]{1,0:T(8,128)(2,1)S(1)}, bf16[16,2048]{1,0:T(8,128)(2,1)}, u32[]{:S(2)}) %copy-start.22) | copy-done | bytes 65560
  3.4 1.5 %upward.1 = (bf16[16,2432]{1,0:T(8,128)(2,1)S(1)}, bf16[16,2048]{1,0:T(8,128)(2,1)S(1)}, bf16[16,128]{1,0:T(8,128)(2,1)S(1)}) custom-call(s32[32]{0:T(128)S(1)} %copy-done.23, bf16[16,2048]{1,0:T(8,128)(2,1)S(1)} %copy-done.22, bf16[4,256,128]{2,1,0:T(8,128)(2,1)S(1)} %bitcast.34, bf16[4,256,128]{2,1,0:T(8,128)(2,1)S(1)} %bitcast.36), custom_call_target="tpu_custom_call" | custom-call | flops 100000000 | bytes 1000000 | tf_op jit(solution)/shard_map/upward/pallas_call | solution.py:363
  5.5 2.1 %collective-permute-start = (bf16[16,2432]{1,0:T(8,128)(2,1)S(1)}, bf16[16,2432]{1,0:T(8,128)(2,1)S(1)}, u32[]{:S(2)}, u32[]{:S(2)}) collective-permute-start(bf16[16,2432]{1,0:T(8,128)(2,1)S(1)} %get-tuple-element.15.own_ref), channel_id=1, source_target_pairs={{0,1},{1,2},{2,3},{3,0},{4,5},{5,6},{6,7},{7,4},{8,9},{9,10},{10,1... | collective-permute-start | bytes 233480 | tf_op jit(solution)/shard_map/ppermute | solution.py:375
  7.7 2.6 %collective-permute-start.1 = (bf16[16,2432]{1,0:T(8,128)(2,1)S(1)}, bf16[16,2432]{1,0:T(8,128)(2,1)S(1)}, u32[]{:S(2)}, u32[]{:S(2)}) collective-permute-start(bf16[16,2432]{1,0:T(8,128)(2,1)S(1)} %get-tuple-element.15.own_ref), channel_id=1, source_target_pairs={{0,2},{1,3},{2,0},{3,1},{4,6},{5,7},{6,4},{7,5},{8,10},{9,11},{10,... | collective-permute-start | bytes 233480 | tf_op jit(solution)/shard_map/ppermute | solution.py:375
  10.3 1.1 %collective-permute-start.2 = (bf16[16,2432]{1,0:T(8,128)(2,1)S(1)}, bf16[16,2432]{1,0:T(8,128)(2,1)S(1)}, u32[]{:S(2)}, u32[]{:S(2)}) collective-permute-start(bf16[16,2432]{1,0:T(8,128)(2,1)S(1)} %get-tuple-element.15.own_ref), channel_id=1, source_target_pairs={{0,3},{1,0},{2,1},{3,2},{4,7},{5,4},{6,5},{7,6},{8,11},{9,8},{10,9... | collective-permute-start | bytes 233480 | tf_op jit(solution)/shard_map/ppermute | solution.py:375
  11.4 3.0 %collective-permute-start.3 = (bf16[16,128]{1,0:T(8,128)(2,1)S(1)}, bf16[16,128]{1,0:T(8,128)(2,1)S(1)}, u32[]{:S(2)}, u32[]{:S(2)}) collective-permute-start(bf16[16,128]{1,0:T(8,128)(2,1)S(1)} %get-tuple-element.16), channel_id=1, source_target_pairs={{3,4},{7,8},{11,12},{15,16},{19,20},{23,24},{27,28},{31,32},{35,36... | collective-permute-start | bytes 12296 | tf_op jit(solution)/shard_map/ppermute | solution.py:380
  14.4 3.5 %copy.14 = bf16[128,3,4096]{0,2,1:T(8,128)(2,1)S(1)} copy(bf16[128,3,4096]{2,0,1:T(8,128)(2,1)} %param.19) | data formatting | bytes 6291456 | tf_op args[9]
  17.9 5.4 %copy.15 = bf16[128,3,32,128]{3,1,2,0:T(4,128)(2,1)} copy(bf16[128,3,32,128]{0,3,2,1:T(8,128)(2,1)S(1)} %bitcast.39) | data formatting | bytes 6291456 | tf_op jit(solution)/shard_map/reshape | solution.py:361
  23.3 1.3 %copy.18 = bf16[12,8,32,128]{3,2,1,0:T(8,128)(2,1)S(1)} copy(bf16[12,8,32,128]{3,1,2,0:T(8,128)(2,1)} %bitcast.41) | data formatting | bytes 1572864
  25.4 0.7 %message.1 = bf16[64,8,128]{2,1,0:T(8,128)(2,1)} custom-call(bf16[16,2432]{1,0:T(8,128)(2,1)S(1)} %get-tuple-element.15.own_ref, bf16[16,2432]{1,0:T(8,128)(2,1)S(1)} %collective-permute-done.one_ref, bf16[16,2432]{1,0:T(8,128)(2,1)S(1)} %collective-permute-done.1.two_ref, bf16[16,2432]{1,0:T(8,128)(2,1)S(1)} %collective-permute-done.2.three_ref), custom_call_target="tpu_custom_call" | custom-call | tf_op jit(solution)/shard_map/message/pallas_call | solution.py:403
  26.1 11.9 %all-to-all-start = ((bf16[64,8,128]{2,1,0:T(8,128)(2,1)}), bf16[64,8,128]{2,1,0:T(8,128)(2,1)S(1)}, u32[]{:S(2)}, u32[]{:S(2)}) async-start(bf16[64,8,128]{2,1,0:T(8,128)(2,1)} %message.1), calls=%async_computation | async-start | bytes 262144 | tf_op jit(solution)/shard_map/all_to_all | solution.py:412
  38.0 2.2 %copy-done = bf16[128,3,32,128]{3,1,2,0:T(4,128)(2,1)S(1)} copy-done((bf16[128,3,32,128]{3,1,2,0:T(4,128)(2,1)S(1)}, bf16[128,3,32,128]{3,1,2,0:T(4,128)(2,1)}, u32[]{:S(2)}) %copy-start) | copy-done | bytes 3145752
  40.2 0.9 %copy-done.15 = bf16[32,4096]{1,0:T(8,128)(2,1)S(1)} copy-done((bf16[32,4096]{1,0:T(8,128)(2,1)S(1)}, bf16[32,4096]{1,0:T(8,128)(2,1)}, u32[]{:S(2)}) %copy-start.15) | copy-done | bytes 262168
  41.1 0.9 %copy-done.17 = bf16[32,4096]{1,0:T(8,128)(2,1)S(1)} copy-done((bf16[32,4096]{1,0:T(8,128)(2,1)S(1)}, bf16[32,4096]{1,0:T(8,128)(2,1)}, u32[]{:S(2)}) %copy-start.17) | copy-done | bytes 262168
  42.1 1.2 %copy-done.25 = bf16[128,4096]{1,0:T(8,128)(2,1)S(1)} copy-done((bf16[128,4096]{1,0:T(8,128)(2,1)S(1)}, bf16[128,4096]{1,0:T(8,128)(2,1)}, u32[]{:S(2)}) %copy-start.25) | copy-done | bytes 1048600
  43.3 0.8 %copy-done.27 = bf16[16,2048]{1,0:T(8,128)(2,1)S(1)} copy-done((bf16[16,2048]{1,0:T(8,128)(2,1)S(1)}, bf16[16,2048]{1,0:T(8,128)(2,1)}, u32[]{:S(2)}) %copy-start.27) | copy-done | bytes 65560
  44.1 9.8 %prepare.1 = (f32[16,2048]{1,0:T(8,128)S(1)}, bf16[2,128,128]{2,1,0:T(8,128)(2,1)S(1)}, bf16[2048,128]{1,0:T(8,128)(2,1)S(1)}, bf16[2048,128]{1,0:T(8,128)(2,1)S...) custom-call(bf16[16,2048]{1,0:T(8,128)(2,1)S(1)} %copy-done.27, ...), custom_call_target="tpu_custom_call" | custom-call | flops 3000000000 | bytes 6000000 | tf_op jit(solution)/shard_map/prepare/pallas_call | solution.py:382
  54.0 1.2 %copy-done.2 = bf16[7168,128]{1,0:T(8,128)(2,1)} copy-done((bf16[7168,128]{1,0:T(8,128)(2,1)}, bf16[7168,128]{1,0:T(8,128)(2,1)S(1)}, u32[]{:S(2)}) %copy-start.2) | copy-done | bytes 1835032
  55.2 0.8 %copy-done.4 = bf16[2048,128]{1,0:T(8,128)(2,1)} copy-done((bf16[2048,128]{1,0:T(8,128)(2,1)}, bf16[2048,128]{1,0:T(8,128)(2,1)S(1)}, u32[]{:S(2)}) %copy-start.4) | copy-done | bytes 524312
  56.0 0.8 %copy-done.6 = bf16[2048,128]{1,0:T(8,128)(2,1)} copy-done((bf16[2048,128]{1,0:T(8,128)(2,1)}, bf16[2048,128]{1,0:T(8,128)(2,1)S(1)}, u32[]{:S(2)}) %copy-start.6) | copy-done | bytes 524312
  56.8 0.8 %copy-done.8 = bf16[512,512]{1,0:T(8,128)(2,1)} copy-done((bf16[512,512]{1,0:T(8,128)(2,1)}, bf16[512,512]{1,0:T(8,128)(2,1)S(1)}, u32[]{:S(2)}) %copy-start.8) | copy-done | bytes 524312
  59.8 1.5 %copy-done.3 = bf16[7168,128]{1,0:T(8,128)(2,1)S(1)} copy-done((bf16[7168,128]{1,0:T(8,128)(2,1)S(1)}, bf16[7168,128]{1,0:T(8,128)(2,1)}, u32[]{:S(2)}) %copy-start.3) | copy-done | bytes 1835032
  61.3 1.0 %copy-done.5 = bf16[2048,128]{1,0:T(8,128)(2,1)S(1)} copy-done((bf16[2048,128]{1,0:T(8,128)(2,1)S(1)}, bf16[2048,128]{1,0:T(8,128)(2,1)}, u32[]{:S(2)}) %copy-start.5) | copy-done | bytes 524312
  62.3 1.0 %copy-done.7 = bf16[2048,128]{1,0:T(8,128)(2,1)S(1)} copy-done((bf16[2048,128]{1,0:T(8,128)(2,1)S(1)}, bf16[2048,128]{1,0:T(8,128)(2,1)}, u32[]{:S(2)}) %copy-start.7) | copy-done | bytes 524312
  63.3 1.0 %copy-done.9 = bf16[512,512]{1,0:T(8,128)(2,1)S(1)} copy-done((bf16[512,512]{1,0:T(8,128)(2,1)S(1)}, bf16[512,512]{1,0:T(8,128)(2,1)}, u32[]{:S(2)}) %copy-start.9) | copy-done | bytes 524312
  64.4 0.9 %copy-done.11 = bf16[16,2432]{1,0:T(8,128)(2,1)S(1)} copy-done((bf16[16,2432]{1,0:T(8,128)(2,1)S(1)}, bf16[16,2432]{1,0:T(8,128)(2,1)}, u32[]{:S(2)}) %copy-start.11) | copy-done | bytes 77848
  65.3 0.9 %copy-done.13 = bf16[1024,128]{1,0:T(8,128)(2,1)S(1)} copy-done((bf16[1024,128]{1,0:T(8,128)(2,1)S(1)}, bf16[1024,128]{1,0:T(8,128)(2,1)}, u32[]{:S(2)}) %copy-start.13) | copy-done | bytes 262168
  66.2 0.9 %copy-done.19 = f32[16,2048]{1,0:T(8,128)S(1)} copy-done((f32[16,2048]{1,0:T(8,128)S(1)}, f32[16,2048]{1,0:T(8,128)}, u32[]{:S(2)}) %copy-start.19) | copy-done | bytes 131096
  67.1 0.8 %copy-done.21 = bf16[2,128,128]{2,1,0:T(8,128)(2,1)S(1)} copy-done((bf16[2,128,128]{2,1,0:T(8,128)(2,1)S(1)}, bf16[2,128,128]{2,1,0:T(8,128)(2,1)}, u32[]{:S(2)}) %copy-start.21) | copy-done | bytes 65560
  68.0 5.1 %downward.1 = bf16[16,2048]{1,0:T(8,128)(2,1)} custom-call(s32[32]{0:T(128)S(1)} %copy-done.24, s32[32,8]{1,0:T(8,128)S(1)} %copy.16.links_ref, s32[128,3]{1,0:T(8,128)S(1)} %copy.17.node_links_ref, bf16[16,2432]{1,0:T(8,128)(2,1)S(1)} %get-tuple-element.15.own_ref, bf16[16,2432]{1,0:T(8,128)(2,1)S(1)} %collective-permute-done.one_ref, ...), custom_call_target="tpu_custom_call" | custom-call | tf_op jit(solution)/shard_map/downward/pallas_call | solution.py:414
  (48 shorter events, 4.2 us)
Async XLA Ops:
  0.0 0.9 %copy-start.14 = (bf16[32,4096]{1,0:T(8,128)(2,1)S(1)}, bf16[32,4096]{1,0:T(8,128)(2,1)}, u32[]{:S(2)}) copy-start(bf16[32,4096]{1,0:T(8,128)(2,1)} %param.12) | copy-start | bytes 786436
  1.0 0.9 %copy-start.16 = (bf16[32,4096]{1,0:T(8,128)(2,1)S(1)}, bf16[32,4096]{1,0:T(8,128)(2,1)}, u32[]{:S(2)}) copy-start(bf16[32,4096]{1,0:T(8,128)(2,1)} %param.16) | copy-start | bytes 786436
  1.9 0.8 %copy-start.22 = (bf16[16,2048]{1,0:T(8,128)(2,1)S(1)}, bf16[16,2048]{1,0:T(8,128)(2,1)}, u32[]{:S(2)}) copy-start(bf16[16,2048]{1,0:T(8,128)(2,1)} %x_ref.1) | copy-start | bytes 196612
  2.7 0.7 copy-start.23
  5.5 19.8 %collective-permute-start = (bf16[16,2432]{1,0:T(8,128)(2,1)S(1)}, bf16[16,2432]{1,0:T(8,128)(2,1)S(1)}, u32[]{:S(2)}, u32[]{:S(2)}) collective-permute-start(bf16[16,2432]{1,0:T(8,128)(2,1)S(1)} %get-tuple-element.15.own_ref), channel_id=1, source_target_pairs={{0,1},{1,2},{2,3},{3,0},{4,5},{5,6},{6,7},{7,4},{8,9},{9,10},{10,1... | collective-permute-start | bytes 233480 | tf_op jit(solution)/shard_map/ppermute | solution.py:375
  7.7 17.6 %collective-permute-start.1 = (bf16[16,2432]{1,0:T(8,128)(2,1)S(1)}, bf16[16,2432]{1,0:T(8,128)(2,1)S(1)}, u32[]{:S(2)}, u32[]{:S(2)}) collective-permute-start(bf16[16,2432]{1,0:T(8,128)(2,1)S(1)} %get-tuple-element.15.own_ref), channel_id=1, source_target_pairs={{0,2},{1,3},{2,0},{3,1},{4,6},{5,7},{6,4},{7,5},{8,10},{9,11},{10,... | collective-permute-start | bytes 233480 | tf_op jit(solution)/shard_map/ppermute | solution.py:375
  10.3 15.0 %collective-permute-start.2 = (bf16[16,2432]{1,0:T(8,128)(2,1)S(1)}, bf16[16,2432]{1,0:T(8,128)(2,1)S(1)}, u32[]{:S(2)}, u32[]{:S(2)}) collective-permute-start(bf16[16,2432]{1,0:T(8,128)(2,1)S(1)} %get-tuple-element.15.own_ref), channel_id=1, source_target_pairs={{0,3},{1,0},{2,1},{3,2},{4,7},{5,4},{6,5},{7,6},{8,11},{9,8},{10,9... | collective-permute-start | bytes 233480 | tf_op jit(solution)/shard_map/ppermute | solution.py:375
  11.4 48.4 %collective-permute-start.3 = (bf16[16,128]{1,0:T(8,128)(2,1)S(1)}, bf16[16,128]{1,0:T(8,128)(2,1)S(1)}, u32[]{:S(2)}, u32[]{:S(2)}) collective-permute-start(bf16[16,128]{1,0:T(8,128)(2,1)S(1)} %get-tuple-element.16), channel_id=1, source_target_pairs={{3,4},{7,8},{11,12},{15,16},{19,20},{23,24},{27,28},{31,32},{35,36... | collective-permute-start | bytes 12296 | tf_op jit(solution)/shard_map/ppermute | solution.py:380
  25.3 0.7 %copy-start.10 = (bf16[16,2432]{1,0:T(8,128)(2,1)}, bf16[16,2432]{1,0:T(8,128)(2,1)S(1)}, u32[]{:S(2)}) copy-start(bf16[16,2432]{1,0:T(8,128)(2,1)S(1)} %collective-permute-done.2.three_ref) | copy-start | bytes 233476
  26.1 33.6 %all-to-all-start = ((bf16[64,8,128]{2,1,0:T(8,128)(2,1)}), bf16[64,8,128]{2,1,0:T(8,128)(2,1)S(1)}, u32[]{:S(2)}, u32[]{:S(2)}) async-start(bf16[64,8,128]{2,1,0:T(8,128)(2,1)} %message.1), calls=%async_computation | async-start | bytes 262144 | tf_op jit(solution)/shard_map/all_to_all | solution.py:412
  38.0 2.2 %copy-start = (bf16[128,3,32,128]{3,1,2,0:T(4,128)(2,1)S(1)}, bf16[128,3,32,128]{3,1,2,0:T(4,128)(2,1)}, u32[]{:S(2)}) copy-start(bf16[128,3,32,128]{3,1,2,0:T(4,128)(2,1)} %copy.15) | copy-start | bytes 9437188
  40.2 0.9 %copy-start.15 = (bf16[32,4096]{1,0:T(8,128)(2,1)S(1)}, bf16[32,4096]{1,0:T(8,128)(2,1)}, u32[]{:S(2)}) copy-start(bf16[32,4096]{1,0:T(8,128)(2,1)} %param.12) | copy-start | bytes 786436
  41.1 0.9 %copy-start.17 = (bf16[32,4096]{1,0:T(8,128)(2,1)S(1)}, bf16[32,4096]{1,0:T(8,128)(2,1)}, u32[]{:S(2)}) copy-start(bf16[32,4096]{1,0:T(8,128)(2,1)} %param.16) | copy-start | bytes 786436
  42.1 1.2 %copy-start.25 = (bf16[128,4096]{1,0:T(8,128)(2,1)S(1)}, bf16[128,4096]{1,0:T(8,128)(2,1)}, u32[]{:S(2)}) copy-start(bf16[128,4096]{1,0:T(8,128)(2,1)} %param.17) | copy-start | bytes 3145732
  43.3 0.8 %copy-start.27 = (bf16[16,2048]{1,0:T(8,128)(2,1)S(1)}, bf16[16,2048]{1,0:T(8,128)(2,1)}, u32[]{:S(2)}) copy-start(bf16[16,2048]{1,0:T(8,128)(2,1)} %copy-done.26) | copy-start | bytes 196612
  44.1 15.4 %copy-start.29 = (s32[128,3]{0,1:T(4,128)S(1)}, s32[128,3]{0,1:T(4,128)}, u32[]{:S(2)}) copy-start(s32[128,3]{0,1:T(4,128)} %param.18) | copy-start | bytes 4612
  44.1 15.5 %copy-start.28 = (s32[32,8]{0,1:T(8,128)S(1)}, s32[32,8]{0,1:T(8,128)}, u32[]{:S(2)}) copy-start(s32[32,8]{0,1:T(8,128)} %param.14) | copy-start | bytes 3076
  44.1 15.6 %copy-start.1 = (bf16[32,8,4096]{2,1,0:T(8,128)(2,1)S(1)}, bf16[32,8,4096]{2,1,0:T(8,128)(2,1)}, u32[]{:S(2)}) copy-start(bf16[32,8,4096]{2,1,0:T(8,128)(2,1)} %param.15) | copy-start | bytes 6291460
  44.1 15.6 %copy-start.24 = (s32[32]{0:T(128)S(1)}, s32[32]{0:T(128)}, u32[]{:S(2)}) copy-start(s32[32]{0:T(128)} %size_ref.3) | copy-start | bytes 388
  54.0 1.2 %copy-start.2 = (bf16[7168,128]{1,0:T(8,128)(2,1)}, bf16[7168,128]{1,0:T(8,128)(2,1)S(1)}, u32[]{:S(2)}) copy-start(bf16[7168,128]{1,0:T(8,128)(2,1)S(1)} %get-tuple-element.22.nodes_ref) | copy-start | bytes 5505028
  55.2 0.8 %copy-start.4 = (bf16[2048,128]{1,0:T(8,128)(2,1)}, bf16[2048,128]{1,0:T(8,128)(2,1)S(1)}, u32[]{:S(2)}) copy-start(bf16[2048,128]{1,0:T(8,128)(2,1)S(1)} %get-tuple-element.20.basis_ref) | copy-start | bytes 1572868
  56.0 0.8 %copy-start.6 = (bf16[2048,128]{1,0:T(8,128)(2,1)}, bf16[2048,128]{1,0:T(8,128)(2,1)S(1)}, u32[]{:S(2)}) copy-start(bf16[2048,128]{1,0:T(8,128)(2,1)S(1)} %get-tuple-element.21.transfer_ref) | copy-start | bytes 1572868
  56.8 0.8 %copy-start.8 = (bf16[512,512]{1,0:T(8,128)(2,1)}, bf16[512,512]{1,0:T(8,128)(2,1)S(1)}, u32[]{:S(2)}) copy-start(bf16[512,512]{1,0:T(8,128)(2,1)S(1)} %get-tuple-element.24.map_ref) | copy-start | bytes 1572868
  57.6 0.7 copy-start.12
  59.8 1.5 %copy-start.3 = (bf16[7168,128]{1,0:T(8,128)(2,1)S(1)}, bf16[7168,128]{1,0:T(8,128)(2,1)}, u32[]{:S(2)}) copy-start(bf16[7168,128]{1,0:T(8,128)(2,1)} %copy-done.2) | copy-start | bytes 5505028
  61.3 1.0 %copy-start.5 = (bf16[2048,128]{1,0:T(8,128)(2,1)S(1)}, bf16[2048,128]{1,0:T(8,128)(2,1)}, u32[]{:S(2)}) copy-start(bf16[2048,128]{1,0:T(8,128)(2,1)} %copy-done.4) | copy-start | bytes 1572868
  62.3 1.0 %copy-start.7 = (bf16[2048,128]{1,0:T(8,128)(2,1)S(1)}, bf16[2048,128]{1,0:T(8,128)(2,1)}, u32[]{:S(2)}) copy-start(bf16[2048,128]{1,0:T(8,128)(2,1)} %copy-done.6) | copy-start | bytes 1572868
  63.3 1.0 %copy-start.9 = (bf16[512,512]{1,0:T(8,128)(2,1)S(1)}, bf16[512,512]{1,0:T(8,128)(2,1)}, u32[]{:S(2)}) copy-start(bf16[512,512]{1,0:T(8,128)(2,1)} %copy-done.8) | copy-start | bytes 1572868
  64.4 0.9 %copy-start.11 = (bf16[16,2432]{1,0:T(8,128)(2,1)S(1)}, bf16[16,2432]{1,0:T(8,128)(2,1)}, u32[]{:S(2)}) copy-start(bf16[16,2432]{1,0:T(8,128)(2,1)} %copy-done.10) | copy-start | bytes 233476
  65.3 0.9 %copy-start.13 = (bf16[1024,128]{1,0:T(8,128)(2,1)S(1)}, bf16[1024,128]{1,0:T(8,128)(2,1)}, u32[]{:S(2)}) copy-start(bf16[1024,128]{1,0:T(8,128)(2,1)} %copy-done.12) | copy-start | bytes 786436
  66.2 0.9 %copy-start.19 = (f32[16,2048]{1,0:T(8,128)S(1)}, f32[16,2048]{1,0:T(8,128)}, u32[]{:S(2)}) copy-start(f32[16,2048]{1,0:T(8,128)} %copy-done.18) | copy-start | bytes 393220
  67.1 0.8 %copy-start.21 = (bf16[2,128,128]{2,1,0:T(8,128)(2,1)S(1)}, bf16[2,128,128]{2,1,0:T(8,128)(2,1)}, u32[]{:S(2)}) copy-start(bf16[2,128,128]{2,1,0:T(8,128)(2,1)} %copy-done.20) | copy-start | bytes 196612
  (3 other events, 1.9 us)

commit v2 on v1

v2 whole, which is shorter than its diff:
```python
import jax
import jax.numpy as jnp
from jax import lax
from jax.experimental import pallas as pl
from jax.experimental.pallas import tpu as pltpu
from jax.sharding import PartitionSpec as P

F32, BF16, I32 = jnp.float32, jnp.bfloat16, jnp.int32
TILES = 16
COEFF = 16 * 128
PAYLOAD = 19 * 128


def iota(shape, dim):
    return lax.broadcasted_iota(I32, shape, dim)


def dot(a, b):
    return jnp.dot(a, b, preferred_element_type=F32)


def dot_t(a, b):
    return lax.dot_general(a, b, (((1,), (1,)), ((), ())), preferred_element_type=F32)


def swap(x):
    return pltpu.roll(x, 64, 1)


def low_half(rows):
    return iota((rows, 128), 1) < 64


def tile(ref, j):
    return ref[:, 128 * j : 128 * j + 128]


def pieces(x):
    high = x.astype(BF16)
    return high, (x - high.astype(F32)).astype(BF16)


def split_map():
    row = iota((512, 128), 0)
    rank = row & 63
    target = (rank & 1) * 256 + (rank >> 1) * 8 + (row >> 6) - iota((512, 128), 1)
    return jnp.concatenate(
        [jnp.where(target == 128 * q, 1.0, 0.0).astype(BF16) for q in range(4)], axis=1
    )


def present(size_ref, j):
    lane = iota((16, 128), 1)
    limit = jnp.where(lane < 64, size_ref[2 * j], size_ref[2 * j + 1])
    return (lane & 63) < limit


def kept(size_ref, x_ref, j):
    return jnp.where(present(size_ref, j), tile(x_ref, j).astype(F32), 0.0)


def start_all(sems, pairs):
    copies = [pltpu.make_async_copy(a, b, sems.at[n]) for n, (a, b) in enumerate(pairs)]
    for copy in copies:
        copy.start()
    return copies


def upward_kernel(
    size_hbm, x_hbm, basis_hbm, transfer_hbm, pay_ref,
    size_ref, x_ref, basis_ref, transfer_ref, masked_ref, map_ref, sems,
):
    copies = start_all(
        sems,
        [(x_hbm, x_ref), (size_hbm, size_ref), (basis_hbm, basis_ref), (transfer_hbm, transfer_ref)],
    )
    lo = low_half(16)
    map_ref[...] = split_map()
    copies[0].wait()
    copies[1].wait()
    for j in range(TILES):
        masked_ref[:, 128 * j : 128 * j + 128] = kept(size_ref, x_ref, j).astype(BF16)
    points = jnp.concatenate([masked_ref[:, 512 * g : 512 * g + 512] for g in range(4)], axis=0)
    spread = dot(points, map_ref[...]).astype(BF16)
    member = iota((16, 256), 1) & 7
    picks = [jnp.where(member == m, 1.0, 0.0).astype(BF16) for m in range(8)]
    copies[2].wait()
    for g in range(4):
        halves = [spread[16 * g : 16 * g + 16, 256 * h : 256 * h + 256] for h in range(2)]
        rows = jnp.concatenate([halves[h] * picks[m] for m in range(8) for h in range(2)], axis=0)
        out = dot(rows, basis_ref[g])
        for q in range(4):
            a0, a1, b0, b1 = [out[64 * q + 16 * n : 64 * q + 16 * n + 16] for n in range(4)]
            coeff = jnp.where(lo, a0 + swap(a1), swap(b0) + b1)
            j = 4 * g + q
            pay_ref[:, 128 * j : 128 * j + 128] = coeff.astype(BF16)
    coeffs = jnp.concatenate([pay_ref[:, 512 * g : 512 * g + 512] for g in range(4)], axis=0)
    spread = dot(coeffs, map_ref[...]).astype(BF16)
    copies[3].wait()
    total = jnp.zeros((32, 128), F32)
    for g in range(4):
        rows = jnp.concatenate(
            [spread[16 * g : 16 * g + 16, 256 * h : 256 * h + 256] for h in range(2)], axis=0
        )
        total = total + dot(rows, transfer_ref[g])
    share = jnp.where(lo, total[:16] + swap(total[16:]), swap(total[:16]) + total[16:])
    high = share.astype(BF16).astype(F32)
    pay_ref[:, COEFF : COEFF + 128] = jnp.where(lo, high, share - high).astype(BF16)
    pay_ref[:, COEFF + 128 : COEFF + 256] = tile(masked_ref, 0)
    pay_ref[:, COEFF + 256 : COEFF + 384] = tile(masked_ref, 15)


def parity_rows(raw, count):
    even = (iota((count, 128), 0) & 1) == 0
    return jnp.where(low_half(count) == even, raw, swap(raw))


def plain_order():
    row, col = iota((512, 256), 0), iota((512, 256), 1)
    return jnp.where(((row >> 6) == (col & 7)) & (((row & 63) >> 1) == (col >> 3)), 1.0, 0.0).astype(BF16)


def near_kernel(
    size_hbm, x_hbm, near_hbm, basis_hbm, transfer_hbm, _, field_hbm, edge_hbm, basis_out, transfer_out,
    size_ref, x_ref, near_ref, basis_ref, transfer_ref,
    masked_ref, blocks_ref, field_ref, edge_ref, basis_rows, transfer_rows, sems, out_sems,
):
    copies = start_all(
        sems,
        [
            (basis_hbm, basis_ref), (transfer_hbm, transfer_ref), (x_hbm, x_ref), (size_hbm, size_ref),
            (near_hbm, near_ref),
        ],
    )
    plain = plain_order()
    own_half = (((iota((512, 128), 0) >> 6) & 1) == 0) == (iota((512, 128), 1) < 64)
    outs = []
    for n, (source, rows, target) in enumerate(
        ((basis_ref, basis_rows, basis_out), (transfer_ref, transfer_rows, transfer_out))
    ):
        copies[n].wait()
        for g in range(4):
            full = parity_rows(dot(plain, source[g]), 512)
            rows[512 * g : 512 * g + 512] = jnp.where(own_half, full, 0.0).astype(BF16)
        outs.append(pltpu.make_async_copy(rows, target, out_sems.at[n]))
        outs[-1].start()
    for n in (2, 3, 4):
        copies[n].wait()
    masked_ref[:, 0:128] = jnp.zeros((16, 128), BF16)
    masked_ref[:, 17 * 128 : 18 * 128] = jnp.zeros((16, 128), BF16)
    for j in range(TILES):
        masked_ref[:, 128 * j + 128 : 128 * j + 256] = kept(size_ref, x_ref, j).astype(BF16)
    lo = low_half(16)
    half = low_half(64)
    for g in range(4):
        for s in range(3):
            blocks_ref[s] = parity_rows(dot(plain, near_ref[s, g]), 512)
        for q in range(4):
            j = 4 * g + q
            a = [blocks_ref[s, 128 * q : 128 * q + 64, :] for s in range(3)]
            b = [blocks_ref[s, 128 * q + 64 : 128 * q + 128, :] for s in range(3)]
            inner = jnp.concatenate([jnp.where(half, a[1], a[2]), jnp.where(half, b[0], b[1])], axis=0)
            outer = jnp.concatenate([jnp.where(half, 0.0, a[0]), jnp.where(half, b[2], 0.0)], axis=0)
            outer = outer.astype(BF16)
            if j in (0, 15):
                edge_ref[j // 15] = outer
            around = jnp.where(lo, tile(masked_ref, j + 2).astype(F32), tile(masked_ref, j).astype(F32))
            field_ref[:, 128 * j : 128 * j + 128] = dot_t(
                tile(masked_ref, j + 1), inner.astype(BF16)
            ) + dot_t(around.astype(BF16), outer)
    for n, (source, target) in enumerate(((field_ref, field_hbm), (edge_ref, edge_hbm))):
        outs.append(pltpu.make_async_copy(source, target, out_sems.at[2 + n]))
        outs[-1].start()
    for copy in outs:
        copy.wait()


def message_kernel(own_ref, one_ref, two_ref, three_ref, _, out_ref, cross_ref):
    share = slice(COEFF, COEFF + 128)
    total = (
        own_ref[:, share].astype(F32) + one_ref[:, share].astype(F32)
        + two_ref[:, share].astype(F32) + three_ref[:, share].astype(F32)
    )
    total = total + swap(total)
    packed = jnp.where(low_half(8), total[:8], total[8:]).astype(BF16)
    for n in range(64):
        out_ref[n] = packed
    at_start = lax.axis_index("sub") == 0
    cross_ref[...] = jnp.where(
        at_start, tile(own_ref, 17).astype(F32), tile(own_ref, 18).astype(F32)
    ).astype(BF16)


def nodes_kernel(
    nodes_hbm, coupling_hbm, _, nodes_out, coupled_out,
    nodes_ref, coupling_ref, rows_ref, coupled_ref, sems, out_sems,
):
    branch = lax.axis_index("leaf")
    own = [64 + branch, 32 + (branch >> 1), 16 + (branch >> 2), 8 + (branch >> 3)]
    copies = start_all(
        sems,
        [(nodes_hbm, nodes_ref)] + [(coupling_hbm.at[:, own[n] >> 3], coupling_ref.at[n]) for n in range(4)],
    )
    plain = plain_order()
    copies[0].wait()
    for g in range(2, 16):
        start = 512 * (g - 2)
        rows_ref[start : start + 512, :] = parity_rows(dot(plain, nodes_ref[g]), 512).astype(BF16)
    outs = [pltpu.make_async_copy(rows_ref, nodes_out, out_sems.at[0])]
    outs[0].start()

    half = low_half(64)
    row, col = iota((64, 256), 0), iota((64, 256), 1)

    def node(n):
        return rows_ref[pl.ds(pl.multiple_of((own[n] - 16) * 64, 64), 64), :]

    def low_only(x):
        return jnp.where(half, x.astype(F32), 0.0).astype(BF16)

    carried = [None, (node(0), None)]
    for n in (1, 2):
        high, low = carried[n]
        longer = dot(high[:, :64], node(n))
        if low is not None:
            longer = longer + dot(low[:, :64], node(n))
        carried.append(pieces(longer))
    for copy in copies[1:]:
        copy.wait()
    lo192 = low_half(192)
    for n in range(4):
        pick = jnp.where(((row >> 1) == (col >> 3)) & ((col & 7) == (own[n] & 7)), 1.0, 0.0).astype(BF16)
        blocks = jnp.concatenate(
            [parity_rows(dot(pick, coupling_ref[n, c]), 64) for c in range(3)], axis=0
        )
        if n == 0:
            rows = jnp.where(lo192, blocks, 0.0)
        else:
            blocks = jnp.where(lo192, blocks, 0.0).astype(BF16)
            high, low = carried[n]
            full = dot_t(blocks, jnp.concatenate([high, high], axis=0))
            if low is not None:
                full = full + dot_t(blocks, jnp.concatenate([low, low], axis=0))
            upper = full.astype(BF16).astype(F32)
            rows = jnp.where(lo192, upper, full - upper)
        coupled_ref[256 * n : 256 * n + 192, :] = rows.astype(BF16)
        coupled_ref[256 * n + 192 : 256 * n + 256, :] = jnp.zeros((64, 128), BF16)
    outs.append(pltpu.make_async_copy(coupled_ref, coupled_out, out_sems.at[1]))
    outs[1].start()
    for copy in outs:
        copy.wait()


def couple_kernel(
    links_hbm, coupling_hbm, own_ref, one_ref, two_ref, three_ref, _, linked_hbm,
    links_ref, coupling_ref, coeff_ref, picked_ref, spread_ref, linked_ref, sems, out_sem,
):
    copies = start_all(
        sems,
        [(links_hbm, links_ref)]
        + [(coupling_hbm.at[pl.ds(8 * n, 8)], coupling_ref.at[pl.ds(8 * n, 8)]) for n in range(4)],
    )
    sub = lax.axis_index("sub")
    lo = low_half(16)
    split = split_map()
    for d, ref in enumerate((own_ref, one_ref, two_ref, three_ref)):
        for j in range(TILES):
            x = tile(ref, j).astype(F32)
            y = swap(x)
            coeff_ref[32 * d + 2 * j] = jnp.where(lo, x, y).astype(BF16)
            coeff_ref[32 * d + 2 * j + 1] = jnp.where(lo, y, x).astype(BF16)
    copies[0].wait()
    for leaf in range(32):
        for c in range(4):
            ends = []
            for m in range(2):
                link = links_ref[2 * c + m, leaf] & 127
                slot = ((sub - (link >> 5)) & 3) * 32 + (link & 31)
                ends.append(coeff_ref[slot].astype(F32))
            picked_ref[16 * leaf : 16 * leaf + 16, 128 * c : 128 * c + 128] = jnp.where(
                lo, ends[0], ends[1]
            ).astype(BF16)
    spread_ref[...] = dot(picked_ref[...], split).astype(BF16)
    for j in range(TILES):
        if j % 4 == 0:
            copies[1 + j // 4].wait()
        outs = []
        for leaf in (2 * j, 2 * j + 1):
            rows = spread_ref[16 * leaf : 16 * leaf + 16, :]
            outs.append(
                dot(jnp.concatenate([rows[:, :256], rows[:, 256:]], axis=0), coupling_ref[leaf])
            )
        a, b = outs
        linked_ref[:, 128 * j : 128 * j + 128] = jnp.where(
            lo, a[:16] + swap(a[16:]), swap(b[:16]) + b[16:]
        )
    copy = pltpu.make_async_copy(linked_ref, linked_hbm, out_sem)
    copy.start()
    copy.wait()


def downward_kernel(
    size_hbm, node_links_hbm, one_ref, three_ref, cross_ref, message_ref,
    linked_hbm, field_hbm, edge_hbm, basis_hbm, transfer_hbm, nodes_hbm, coupled_hbm,
    out_ref,
    size_ref, node_links_ref, linked_ref, field_ref, edge_ref, basis_ref, transfer_ref, nodes_ref,
    coupled_ref, table_ref, sems,
):
    copies = start_all(
        sems,
        [
            (nodes_hbm.at[pl.ds(24 * 128, 32 * 128)], nodes_ref.at[pl.ds(24 * 128, 32 * 128)]),
            (nodes_hbm.at[pl.ds(0, 24 * 128)], nodes_ref.at[pl.ds(0, 24 * 128)]),
            (node_links_hbm, node_links_ref), (coupled_hbm, coupled_ref), (transfer_hbm, transfer_ref),
            (basis_hbm, basis_ref), (linked_hbm, linked_ref), (field_hbm, field_ref), (edge_hbm, edge_ref),
            (size_hbm, size_ref),
        ],
    )
    branch, sub = lax.axis_index("leaf"), lax.axis_index("sub")
    lo = low_half(16)
    lo8 = low_half(8)
    lo32 = low_half(32)

    pairs = []
    for q in range(32):
        one, two = message_ref[2 * q].astype(F32), message_ref[2 * q + 1].astype(F32)
        one_s, two_s = swap(one), swap(two)
        pairs.append(
            jnp.concatenate([jnp.where(lo8, one, two_s), jnp.where(lo8, one_s, two)], axis=0).astype(BF16)
        )
        first = jnp.concatenate([jnp.where(lo8, one, one_s), jnp.where(lo8, one_s, one)], axis=0)
        second = jnp.concatenate([jnp.where(lo8, two, two_s), jnp.where(lo8, two_s, two)], axis=0)
        zeros = jnp.zeros((16, 128), BF16)
        table_ref[64 + 2 * q] = jnp.concatenate([first.astype(BF16), zeros], axis=0)
        table_ref[65 + 2 * q] = jnp.concatenate([second.astype(BF16), zeros], axis=0)

    def weights(q):
        return nodes_ref[128 * (q - 8) : 128 * (q - 8) + 128, :]

    size = 32
    copies[0].wait()
    while size >= 8:
        parents = []
        for q in range(size, 2 * size):
            a = dot(pairs[q - size], weights(q))
            if size < 32:
                a = a[:16] + a[16:]
            high, low = pieces(a)
            parents.append(jnp.concatenate([high, low], axis=0))
            table_ref[q] = parents[-1]
        if size == 32:
            copies[1].wait()
        pairs = [
            jnp.where(lo32, parents[2 * q].astype(F32), parents[2 * q + 1].astype(F32)).astype(BF16)
            for q in range(size // 2)
        ]
        size = size // 2
    copies[2].wait()
    sources = []
    for n in range(4):
        own = (64 >> n) + (branch >> n)
        a, b, c = [table_ref[node_links_ref[m, own]].astype(F32) for m in range(3)]
        sources += [jnp.where(lo32, a, b).astype(BF16), jnp.where(lo32, c, 0.0).astype(BF16)]
    copies[3].wait()
    down = dot(jnp.concatenate(sources, axis=1), coupled_ref[...])
    down = down[:16] + down[16:]
    down = (down + swap(down)).astype(BF16)
    for copy in copies[4:]:
        copy.wait()
    inherited = dot_t(down, transfer_ref[...])

    left = jnp.where(sub == 0, cross_ref[...].astype(F32), tile(one_ref, 18).astype(F32))
    left = jnp.where(lo, 0.0, left).astype(BF16)
    right = jnp.where(sub == 3, cross_ref[...].astype(F32), tile(three_ref, 17).astype(F32))
    right = jnp.where(lo, right, 0.0).astype(BF16)
    for j in range(TILES):
        far = (tile(linked_ref, j) + inherited[:, 128 * j : 128 * j + 128]).astype(BF16)
        out = dot_t(far, basis_ref[128 * j : 128 * j + 128, :]) + tile(field_ref, j)
        if j == 0:
            out = out + dot_t(left, edge_ref[0])
        if j == 15:
            out = out + dot_t(right, edge_ref[1])
        out_ref[:, 128 * j : 128 * j + 128] = jnp.where(present(size_ref, j), out, 0.0).astype(BF16)


VMEM = pl.BlockSpec(memory_space=pltpu.VMEM)
HBM = pl.BlockSpec(memory_space=pltpu.HBM)
ANY = pl.BlockSpec(memory_space=pl.ANY)


def params(mib):
    return pltpu.CompilerParams(vmem_limit_bytes=mib << 20)


def cost(flops, size):
    return pl.CostEstimate(flops=flops, bytes_accessed=size, transcendentals=0)


def shape(dims, dtype=BF16):
    return jax.ShapeDtypeStruct(dims, dtype)


def grouped(table):
    lead, rows = table.shape[:-2], table.shape[-2]
    table = jnp.swapaxes(table.reshape(*lead, rows // 8, 8, 32, 128), -3, -2)
    return table.reshape(*lead, rows // 8, 256, 128)


def dma(count):
    return pltpu.SemaphoreType.DMA((count,))


def body(
    vectors, leaf_size, leaf_basis, near_blocks, leaf_links, leaf_coupling, leaf_transfer,
    node_transfer, node_links, node_coupling,
):
    basis, transfer, nodes = grouped(leaf_basis), grouped(leaf_transfer), grouped(node_transfer)
    coupling = grouped(leaf_coupling)[:, 0]
    near = grouped(near_blocks.transpose(1, 0, 2))
    node_coupled = grouped(node_coupling.transpose(1, 0, 2))

    payload = pl.pallas_call(
        upward_kernel,
        out_shape=shape((16, PAYLOAD)),
        in_specs=[HBM] * 4,
        out_specs=VMEM,
        scratch_shapes=[
            pltpu.SMEM((32,), I32),
            pltpu.VMEM((16, 2048), BF16),
            pltpu.VMEM((4, 256, 128), BF16),
            pltpu.VMEM((4, 256, 128), BF16),
            pltpu.VMEM((16, 2048), BF16),
            pltpu.VMEM((512, 512), BF16),
            dma(4),
        ],
        compiler_params=params(60),
        cost_estimate=cost(10**8, 10**6),
        name="upward",
    )(leaf_size, vectors, basis, transfer)

    others = [
        lax.ppermute(payload, "sub", [(s, (s + d) % 4) for s in range(4)]) for d in (1, 2, 3)
    ]

    field, edge, basis_p, transfer_p = pl.pallas_call(
        near_kernel,
        out_shape=[
            shape((16, 2048), F32), shape((2, 128, 128)), shape((2048, 128)), shape((2048, 128)),
        ],
        in_specs=[HBM] * 5 + [ANY],
        out_specs=[HBM] * 4,
        scratch_shapes=[
            pltpu.SMEM((32,), I32),
            pltpu.VMEM((16, 2048), BF16),
            pltpu.VMEM((3, 4, 256, 128), BF16),
            pltpu.VMEM((4, 256, 128), BF16),
            pltpu.VMEM((4, 256, 128), BF16),
            pltpu.VMEM((16, 18 * 128), BF16),
            pltpu.VMEM((3, 512, 128), F32),
            pltpu.VMEM((16, 2048), F32),
            pltpu.VMEM((2, 128, 128), BF16),
            pltpu.VMEM((2048, 128), BF16),
            pltpu.VMEM((2048, 128), BF16),
            dma(5),
            dma(4),
        ],
        compiler_params=params(60),
        cost_estimate=cost(10**9, 3 * 10**6),
        name="near",
    )(leaf_size, vectors, near, basis, transfer, payload)

    messages, cross = pl.pallas_call(
        message_kernel,
        out_shape=[shape((64, 8, 128)), shape((16, 128))],
        in_specs=[VMEM] * 4 + [ANY],
        out_specs=[VMEM] * 2,
        compiler_params=params(60),
        name="message",
    )(payload, *others, edge)
    summed = lax.all_to_all(messages, "leaf", 0, 0)

    branches = lax.axis_size("leaf")
    routes = [(4 * b + 3, 4 * b + 4) for b in range(branches - 1)]
    routes += [(4 * b, 4 * b - 1) for b in range(1, branches)]
    cross = lax.ppermute(cross, ("leaf", "sub"), routes)

    nodes_p, coupled = pl.pallas_call(
        nodes_kernel,
        out_shape=[shape((56 * 128, 128)), shape((1024, 128))],
        in_specs=[HBM] * 2 + [ANY],
        out_specs=[HBM] * 2,
        scratch_shapes=[
            pltpu.VMEM((16, 256, 128), BF16),
            pltpu.VMEM((4, 3, 256, 128), BF16),
            pltpu.VMEM((56 * 128, 128), BF16),
            pltpu.VMEM((1024, 128), BF16),
            dma(5),
            dma(2),
        ],
        compiler_params=params(60),
        cost_estimate=cost(10**9, 3 * 10**6),
        name="nodes",
    )(nodes, node_coupled, messages)

    linked = pl.pallas_call(
        couple_kernel,
        out_shape=shape((16, 2048), F32),
        in_specs=[HBM] * 2 + [VMEM] * 4 + [ANY],
        out_specs=HBM,
        scratch_shapes=[
            pltpu.SMEM((8, 32), I32),
            pltpu.VMEM((32, 256, 128), BF16),
            pltpu.VMEM((128, 16, 128), BF16),
            pltpu.VMEM((512, 512), BF16),
            pltpu.VMEM((512, 512), BF16),
            pltpu.VMEM((16, 2048), F32),
            dma(5),
            pltpu.SemaphoreType.DMA,
        ],
        compiler_params=params(60),
        cost_estimate=cost(10**9, 3 * 10**6),
        name="couple",
    )(leaf_links.T, coupling, payload, *others, messages)

    return pl.pallas_call(
        downward_kernel,
        out_shape=shape((16, 2048)),
        in_specs=[HBM] * 2 + [VMEM] * 4 + [HBM] * 7,
        out_specs=VMEM,
        scratch_shapes=[
            pltpu.SMEM((32,), I32),
            pltpu.SMEM((3, 128), I32),
            pltpu.VMEM((16, 2048), F32),
            pltpu.VMEM((16, 2048), F32),
            pltpu.VMEM((2, 128, 128), BF16),
            pltpu.VMEM((2048, 128), BF16),
            pltpu.VMEM((2048, 128), BF16),
            pltpu.VMEM((56 * 128, 128), BF16),
            pltpu.VMEM((1024, 128), BF16),
            pltpu.VMEM((128, 32, 128), BF16),
            dma(10),
        ],
        compiler_params=params(60),
        name="downward",
    )(
        leaf_size, node_links.T, others[0], others[2], cross, summed,
        linked, field, edge, basis_p, transfer_p, nodes_p, coupled,
    )


def solution(mesh):
    split = ("leaf", "sub")
    placed = (
        P(None, split), P(split), P(split, None), P(split, None, None), P(split, None),
        P(split, None, None), P(split, None), P(), P(), P(),
    )
    return jax.shard_map(
        body, mesh=mesh, in_specs=placed, out_specs=P(None, split), check_vma=False
    )
```

time: 73.9 us -> 48 us (0.65)
  the two profiles are of different devices: /device:TPU:1 before, /device:TPU:6 now
where the time goes in v2:
time: 48 us; the launch traced here: 47.7 us
  starting transfers between devices  23.8 us (50%)
  Pallas kernels  22.4 us (47%)
  local copies, waits for them, and re-layouts  1.3 us (3%)
    all_to_all x1, starting transfers between devices, body(): summed = lax.all_to_all(messages, 'leaf', 0, 0)  12.2 us
    ppermute x1, starting transfers between devices, body(): cross = lax.ppermute(cross, ('leaf', 'sub'), routes)  6.32 us
    ppermute x3, starting transfers between devices, body(): lax.ppermute(payload, 'sub', [(s, (s + d) % 4) for s in range(4)])  5.3 us
    pallas_call x1, Pallas kernels, body(): pl.pallas_call(near_kernel, out_shape=[shape((16, 2048), F32), shape((2,...  4.93 us
    pallas_call x1, Pallas kernels, body(): pl.pallas_call(downward_kernel, out_shape=shape((16, 2048)), in_specs=[HB...  4.57 us
    pallas_call x1, Pallas kernels, body(): pl.pallas_call(couple_kernel, out_shape=shape((16, 2048), F32), in_specs=...  4.52 us
    pallas_call x1, Pallas kernels, body(): pl.pallas_call(nodes_kernel, out_shape=[shape((56 * 128, 128)), shape((10...  4.2 us
    pallas_call x1, Pallas kernels, body(): pl.pallas_call(upward_kernel, out_shape=shape((16, PAYLOAD)), in_specs=[H...  2.49 us
  transfers between devices with their start and end apart: 5, of which 0 were waited for; matrix products, arithmetic and copies ran while one was open for 0% of the time, Pallas kernels for 29%

profile of v2, /device:TPU:6, one launch (start us, length us, event | category | flops | bytes accessed | tf_op | source)
XLA Modules:
  0.0 47.7 jit_solution(3786464949243879937)
XLA Ops:
  0.0 2.5 %upward.1._.own_ref = bf16[16,2432]{1,0:T(8,128)(2,1)} custom-call(s32[32]{0:T(128)} %size_hbm.5, bf16[16,2048]{1,0:T(8,128)(2,1)} %x_hbm.3, bf16[4,256,128]{2,1,0:T(8,128)(2,1)} %bitcast.38, bf16[4,256,128]{2,1,0:T(8,128)(2,1)} %bitcast.40), custom_call_target="tpu_custom_call" | custom-call | flops 100000000 | bytes 1000000 | tf_op jit(solution)/shard_map/upward/pallas_call | solution.py:422
  2.5 3.3 %collective-permute-start.2 = (bf16[16,2432]{1,0:T(8,128)(2,1)}, bf16[16,2432]{1,0:T(8,128)(2,1)S(1)}, u32[]{:S(2)}, u32[]{:S(2)}) collective-permute-start(bf16[16,2432]{1,0:T(8,128)(2,1)} %upward.1._.own_ref), channel_id=1, source_target_pairs={{0,2},{1,3},{2,0},{3,1},{4,6},{5,7},{6,4},{7,5},{8,10},{9,11},{10,... | collective-permute-start | bytes 233480 | tf_op jit(solution)/shard_map/ppermute | solution.py:442
  5.8 1.1 %collective-permute-start.1 = (bf16[16,2432]{1,0:T(8,128)(2,1)}, bf16[16,2432]{1,0:T(8,128)(2,1)S(1)}, u32[]{:S(2)}, u32[]{:S(2)}) collective-permute-start(bf16[16,2432]{1,0:T(8,128)(2,1)} %upward.1._.own_ref), channel_id=1, source_target_pairs={{0,3},{1,0},{2,1},{3,2},{4,7},{5,4},{6,5},{7,6},{8,11},{9,8},{10,9... | collective-permute-start | bytes 233480 | tf_op jit(solution)/shard_map/ppermute | solution.py:442
  6.8 1.0 %collective-permute-start = (bf16[16,2432]{1,0:T(8,128)(2,1)}, bf16[16,2432]{1,0:T(8,128)(2,1)S(1)}, u32[]{:S(2)}, u32[]{:S(2)}) collective-permute-start(bf16[16,2432]{1,0:T(8,128)(2,1)} %upward.1._.own_ref), channel_id=1, source_target_pairs={{0,1},{1,2},{2,3},{3,0},{4,5},{5,6},{6,7},{7,4},{8,9},{9,10},{10,1... | collective-permute-start | bytes 233480 | tf_op jit(solution)/shard_map/ppermute | solution.py:442
  7.8 4.9 %near.1 = (f32[16,2048]{1,0:T(8,128)}, bf16[2,128,128]{2,1,0:T(8,128)(2,1)}, bf16[2048,128]{1,0:T(8,128)(2,1)}, bf16[2048,128]{1,0:T(8,128)(2,1)}) custom-call(s32[32]{0:T(128)} %size_hbm.5, bf16[16,2048]{1,0:T(8,128)(2,1)} %x_hbm.3, bf16[3,4,256,128]{3,2,1,0:T(8,128)(2,1)} %bitcast.44, bf16[4,256,128]{2,1,0:T(8,128)(2,1)} %bitcast.39, ...), custom_call_target="tpu_custom_call" | custom-call | flops 1000000000 | bytes 3000000 | tf_op jit(solution)/shard_map/near/pallas_call | solution.py:445
  12.7 0.0 collective-permute-done.2.two_ref
  12.8 0.0 copy-start.3
  12.8 0.0 collective-permute-done.1.three_ref
  12.8 0.0 copy-start.1
  12.8 0.0 collective-permute-done.one_ref
  12.8 0.0 copy-start.2
  12.8 0.6 %copy-done.3 = bf16[16,2432]{1,0:T(8,128)(2,1)} copy-done((bf16[16,2432]{1,0:T(8,128)(2,1)}, bf16[16,2432]{1,0:T(8,128)(2,1)S(1)}, u32[]{:S(2)}) %copy-start.3) | copy-done | bytes 77848
  13.4 0.0 copy-done.1
  13.4 0.0 copy-done.2
  13.5 1.7 %message.1 = (bf16[64,8,128]{2,1,0:T(8,128)(2,1)}, bf16[16,128]{1,0:T(8,128)(2,1)}) custom-call(bf16[16,2432]{1,0:T(8,128)(2,1)} %upward.1._.own_ref, bf16[16,2432]{1,0:T(8,128)(2,1)} %copy-done.2, bf16[16,2432]{1,0:T(8,128)(2,1)} %copy-done.3, bf16[16,2432]{1,0:T(8,128)(2,1)} %copy-done.1, bf16[2,128,128]{2,1,0:T(8,128)(2,1)} %get-tuple-element.13._.edge_hbm), custom_call_target="tpu_custom_call" | custom-call | tf_op jit(solution)/shard_map/message/pallas_call | solution.py:472
  15.2 12.2 %all-to-all-start = ((bf16[64,8,128]{2,1,0:T(8,128)(2,1)}), bf16[64,8,128]{2,1,0:T(8,128)(2,1)S(1)}, u32[]{:S(2)}, u32[]{:S(2)}) async-start(bf16[64,8,128]{2,1,0:T(8,128)(2,1)} %get-tuple-element.15._), calls=%async_computation | async-start | bytes 262144 | tf_op jit(solution)/shard_map/all_to_all | solution.py:480
  27.4 6.3 %collective-permute-start.3 = (bf16[16,128]{1,0:T(8,128)(2,1)}, bf16[16,128]{1,0:T(8,128)(2,1)S(1)}, u32[]{:S(2)}, u32[]{:S(2)}) collective-permute-start(bf16[16,128]{1,0:T(8,128)(2,1)} %get-tuple-element.14), channel_id=1, source_target_pairs={{3,4},{7,8},{11,12},{15,16},{19,20},{23,24},{27,28},{31,32},{35,36... | collective-permute-start | bytes 12296 | tf_op jit(solution)/shard_map/ppermute | solution.py:485
  33.7 4.2 %nodes.1 = (bf16[7168,128]{1,0:T(8,128)(2,1)}, bf16[1024,128]{1,0:T(8,128)(2,1)}) custom-call(bf16[16,256,128]{2,1,0:T(8,128)(2,1)} %bitcast.37, bf16[3,16,256,128]{3,2,1,0:T(8,128)(2,1)} %bitcast.36, bf16[64,8,128]{2,1,0:T(8,128)(2,1)} %get-tuple-element.15._), custom_call_target="tpu_custom_call" | custom-call | flops 1000000000 | bytes 3000000 | tf_op jit(solution)/shard_map/nodes/pallas_call | solution.py:487
  37.9 4.5 %couple.1.linked_hbm = f32[16,2048]{1,0:T(8,128)} custom-call(s32[8,32]{1,0:T(8,128)} %bitcast.45, bf16[32,256,128]{2,1,0:T(8,128)(2,1)} %bitcast.43, bf16[16,2432]{1,0:T(8,128)(2,1)} %upward.1._.own_ref, bf16[16,2432]{1,0:T(8,128)(2,1)} %copy-done.2, bf16[16,2432]{1,0:T(8,128)(2,1)} %copy-done.3, bf16[16,2432]{1,0:T(8,128)(2,1)} %copy-done.1, ...), custom_call_target="tpu_custom_call" | custom-call | flops 1000000000 | bytes 3000000 | tf_op jit(solution)/shard_map/couple/pallas_call | solution.py:505
  42.4 0.0 collective-permute-done.3.cross_ref
  42.4 0.0 copy-start.4
  42.5 0.0 all-to-all-done.message_ref
  42.5 0.0 copy-start
  42.5 0.5 %copy-done.4 = bf16[16,128]{1,0:T(8,128)(2,1)} copy-done((bf16[16,128]{1,0:T(8,128)(2,1)}, bf16[16,128]{1,0:T(8,128)(2,1)S(1)}, u32[]{:S(2)}) %copy-start.4) | copy-done | bytes 4120
  43.0 0.1 copy-done
  43.1 4.6 %downward.1 = bf16[16,2048]{1,0:T(8,128)(2,1)} custom-call(s32[32]{0:T(128)} %size_hbm.5, s32[3,128]{1,0:T(4,128)} %bitcast.42, bf16[16,2432]{1,0:T(8,128)(2,1)} %copy-done.2, bf16[16,2432]{1,0:T(8,128)(2,1)} %copy-done.1, bf16[16,128]{1,0:T(8,128)(2,1)} %copy-done.4, bf16[64,8,128]{2,1,0:T(8,128)(2,1)} %copy-done, f32[16,2048]{1,0:T(8,128)} %couple.1.linked_hbm, ...), custom_call_target="tpu_custom_call" | custom-call | tf_op jit(solution)/shard_map/downward/pallas_call | solution.py:525
Async XLA Ops:
  2.5 10.2 %collective-permute-start.2 = (bf16[16,2432]{1,0:T(8,128)(2,1)}, bf16[16,2432]{1,0:T(8,128)(2,1)S(1)}, u32[]{:S(2)}, u32[]{:S(2)}) collective-permute-start(bf16[16,2432]{1,0:T(8,128)(2,1)} %upward.1._.own_ref), channel_id=1, source_target_pairs={{0,2},{1,3},{2,0},{3,1},{4,6},{5,7},{6,4},{7,5},{8,10},{9,11},{10,... | collective-permute-start | bytes 233480 | tf_op jit(solution)/shard_map/ppermute | solution.py:442
  5.8 7.0 %collective-permute-start.1 = (bf16[16,2432]{1,0:T(8,128)(2,1)}, bf16[16,2432]{1,0:T(8,128)(2,1)S(1)}, u32[]{:S(2)}, u32[]{:S(2)}) collective-permute-start(bf16[16,2432]{1,0:T(8,128)(2,1)} %upward.1._.own_ref), channel_id=1, source_target_pairs={{0,3},{1,0},{2,1},{3,2},{4,7},{5,4},{6,5},{7,6},{8,11},{9,8},{10,9... | collective-permute-start | bytes 233480 | tf_op jit(solution)/shard_map/ppermute | solution.py:442
  6.8 6.0 %collective-permute-start = (bf16[16,2432]{1,0:T(8,128)(2,1)}, bf16[16,2432]{1,0:T(8,128)(2,1)S(1)}, u32[]{:S(2)}, u32[]{:S(2)}) collective-permute-start(bf16[16,2432]{1,0:T(8,128)(2,1)} %upward.1._.own_ref), channel_id=1, source_target_pairs={{0,1},{1,2},{2,3},{3,0},{4,5},{5,6},{6,7},{7,4},{8,9},{9,10},{10,1... | collective-permute-start | bytes 233480 | tf_op jit(solution)/shard_map/ppermute | solution.py:442
  12.8 0.6 %copy-start.3 = (bf16[16,2432]{1,0:T(8,128)(2,1)}, bf16[16,2432]{1,0:T(8,128)(2,1)S(1)}, u32[]{:S(2)}) copy-start(bf16[16,2432]{1,0:T(8,128)(2,1)S(1)} %collective-permute-done.2.two_ref) | copy-start | bytes 233476
  12.8 0.7 %copy-start.1 = (bf16[16,2432]{1,0:T(8,128)(2,1)}, bf16[16,2432]{1,0:T(8,128)(2,1)S(1)}, u32[]{:S(2)}) copy-start(bf16[16,2432]{1,0:T(8,128)(2,1)S(1)} %collective-permute-done.1.three_ref) | copy-start | bytes 233476
  12.8 0.7 %copy-start.2 = (bf16[16,2432]{1,0:T(8,128)(2,1)}, bf16[16,2432]{1,0:T(8,128)(2,1)S(1)}, u32[]{:S(2)}) copy-start(bf16[16,2432]{1,0:T(8,128)(2,1)S(1)} %collective-permute-done.one_ref) | copy-start | bytes 233476
  15.2 27.3 %all-to-all-start = ((bf16[64,8,128]{2,1,0:T(8,128)(2,1)}), bf16[64,8,128]{2,1,0:T(8,128)(2,1)S(1)}, u32[]{:S(2)}, u32[]{:S(2)}) async-start(bf16[64,8,128]{2,1,0:T(8,128)(2,1)} %get-tuple-element.15._), calls=%async_computation | async-start | bytes 262144 | tf_op jit(solution)/shard_map/all_to_all | solution.py:480
  27.4 15.1 %collective-permute-start.3 = (bf16[16,128]{1,0:T(8,128)(2,1)}, bf16[16,128]{1,0:T(8,128)(2,1)S(1)}, u32[]{:S(2)}, u32[]{:S(2)}) collective-permute-start(bf16[16,128]{1,0:T(8,128)(2,1)} %get-tuple-element.14), channel_id=1, source_target_pairs={{3,4},{7,8},{11,12},{15,16},{19,20},{23,24},{27,28},{31,32},{35,36... | collective-permute-start | bytes 12296 | tf_op jit(solution)/shard_map/ppermute | solution.py:485
  42.4 0.6 %copy-start.4 = (bf16[16,128]{1,0:T(8,128)(2,1)}, bf16[16,128]{1,0:T(8,128)(2,1)S(1)}, u32[]{:S(2)}) copy-start(bf16[16,128]{1,0:T(8,128)(2,1)S(1)} %collective-permute-done.3.cross_ref) | copy-start | bytes 12292
  42.5 0.6 %copy-start = (bf16[64,8,128]{2,1,0:T(8,128)(2,1)}, bf16[64,8,128]{2,1,0:T(8,128)(2,1)S(1)}, u32[]{:S(2)}) copy-start(bf16[64,8,128]{2,1,0:T(8,128)(2,1)S(1)} %all-to-all-done.message_ref) | copy-start | bytes 393220

commit v3 on v2

v3 whole, which is shorter than its diff:
```python
import jax
import jax.numpy as jnp
from jax import lax
from jax.experimental import pallas as pl
from jax.experimental.pallas import tpu as pltpu
from jax.sharding import PartitionSpec as P

F32, BF16, I32 = jnp.float32, jnp.bfloat16, jnp.int32
TILES = 16
COEFF = 16 * 128
PAYLOAD = 19 * 128


def iota(shape, dim):
    return lax.broadcasted_iota(I32, shape, dim)


def dot(a, b):
    return jnp.dot(a, b, preferred_element_type=F32)


def dot_t(a, b):
    return lax.dot_general(a, b, (((1,), (1,)), ((), ())), preferred_element_type=F32)


def swap(x):
    return pltpu.roll(x, 64, 1)


def low_half(rows):
    return iota((rows, 128), 1) < 64


def tile(ref, j):
    return ref[:, 128 * j : 128 * j + 128]


def pieces(x):
    high = x.astype(BF16)
    return high, (x - high.astype(F32)).astype(BF16)


def split_map():
    row = iota((512, 128), 0)
    rank = row & 63
    target = (rank & 1) * 256 + (rank >> 1) * 8 + (row >> 6) - iota((512, 128), 1)
    return jnp.concatenate(
        [jnp.where(target == 128 * q, 1.0, 0.0).astype(BF16) for q in range(4)], axis=1
    )


def group_map():
    row, col = iota((256, 256), 0), iota((256, 256), 1)
    return jnp.where(col == (row & 31) * 8 + (row >> 5), 1.0, 0.0).astype(BF16)


def plain_rows(raw, rows_ref):
    count = raw.shape[0]
    lo = low_half(count)
    other = swap(raw)
    rows_ref[pl.ds(0, count, stride=2), :] = jnp.where(lo, raw, other)
    rows_ref[pl.ds(1, count, stride=2), :] = jnp.where(lo, other, raw)


def present(size_ref, j):
    lane = iota((16, 128), 1)
    limit = jnp.where(lane < 64, size_ref[2 * j], size_ref[2 * j + 1])
    return (lane & 63) < limit


def kept(size_ref, x_ref, j):
    return jnp.where(present(size_ref, j), tile(x_ref, j).astype(F32), 0.0)


def start_all(sems, pairs):
    copies = [pltpu.make_async_copy(a, b, sems.at[n]) for n, (a, b) in enumerate(pairs)]
    for copy in copies:
        copy.start()
    return copies


def upward_kernel(
    size_hbm, x_hbm, basis_hbm, transfer_hbm, pay_ref, cross_ref,
    size_ref, x_ref, basis_ref, transfer_ref, masked_ref, map_ref, sems,
):
    copies = start_all(
        sems,
        [(x_hbm, x_ref), (size_hbm, size_ref), (basis_hbm, basis_ref), (transfer_hbm, transfer_ref)],
    )
    lo = low_half(16)
    map_ref[...] = split_map()
    copies[0].wait()
    copies[1].wait()
    for j in range(TILES):
        masked_ref[:, 128 * j : 128 * j + 128] = kept(size_ref, x_ref, j).astype(BF16)
    points = jnp.concatenate([masked_ref[:, 512 * g : 512 * g + 512] for g in range(4)], axis=0)
    spread = dot(points, map_ref[...]).astype(BF16)
    member = iota((16, 256), 1) & 7
    picks = [jnp.where(member == m, 1.0, 0.0).astype(BF16) for m in range(8)]
    copies[2].wait()
    for g in range(4):
        halves = [spread[16 * g : 16 * g + 16, 256 * h : 256 * h + 256] for h in range(2)]
        rows = jnp.concatenate([halves[h] * picks[m] for m in range(8) for h in range(2)], axis=0)
        out = dot(rows, basis_ref[g])
        for q in range(4):
            a0, a1, b0, b1 = [out[64 * q + 16 * n : 64 * q + 16 * n + 16] for n in range(4)]
            coeff = jnp.where(lo, a0 + swap(a1), swap(b0) + b1)
            j = 4 * g + q
            pay_ref[:, 128 * j : 128 * j + 128] = coeff.astype(BF16)
    coeffs = jnp.concatenate([pay_ref[:, 512 * g : 512 * g + 512] for g in range(4)], axis=0)
    spread = dot(coeffs, map_ref[...]).astype(BF16)
    copies[3].wait()
    total = jnp.zeros((32, 128), F32)
    for g in range(4):
        rows = jnp.concatenate(
            [spread[16 * g : 16 * g + 16, 256 * h : 256 * h + 256] for h in range(2)], axis=0
        )
        total = total + dot(rows, transfer_ref[g])
    share = jnp.where(lo, total[:16] + swap(total[16:]), swap(total[:16]) + total[16:])
    packed = jnp.where(low_half(8), share[:8], share[8:])
    high = packed.astype(BF16).astype(F32)
    pay_ref[:, COEFF : COEFF + 128] = jnp.concatenate([high, packed - high], axis=0).astype(BF16)
    first, last = tile(masked_ref, 0), tile(masked_ref, 15)
    pay_ref[:, COEFF + 128 : COEFF + 256] = first
    pay_ref[:, COEFF + 256 : COEFF + 384] = last
    cross_ref[...] = jnp.where(lax.axis_index("sub") == 0, first, last)


def near_kernel(
    size_hbm, x_hbm, near_hbm, basis_hbm, transfer_hbm, pay_ref,
    field_ref, basis_rows, transfer_rows, share_ref,
    size_ref, x_ref, near_ref, basis_ref, transfer_ref, masked_ref, raw_ref, sems,
):
    copies = start_all(
        sems,
        [
            (basis_hbm, basis_ref), (transfer_hbm, transfer_ref), (x_hbm, x_ref), (size_hbm, size_ref),
            (near_hbm, near_ref),
        ],
    )
    share_ref[...] = tile(pay_ref, 16)
    collect = group_map()
    half = low_half(64)
    copies[0].wait()
    copies[1].wait()
    for g in range(4):
        raw = dot(collect, jnp.concatenate([basis_ref[g], transfer_ref[g]], axis=1))
        for n, rows in enumerate((basis_rows, transfer_rows)):
            plain_rows(raw[:, 128 * n : 128 * n + 128], raw_ref.at[n])
            for q in range(4):
                pair = [raw_ref[n, 128 * q + 64 * m : 128 * q + 64 * m + 64, :] for m in range(2)]
                start = 256 * g + 64 * q
                rows[start : start + 64, :] = jnp.where(half, pair[0], pair[1]).astype(BF16)
    for copy in copies[2:]:
        copy.wait()
    masked_ref[:, 0:128] = jnp.zeros((16, 128), BF16)
    masked_ref[:, 17 * 128 : 18 * 128] = jnp.zeros((16, 128), BF16)
    for j in range(TILES):
        masked_ref[:, 128 * j + 128 : 128 * j + 256] = kept(size_ref, x_ref, j).astype(BF16)
    lo = low_half(16)
    for pair in range(2):
        for s in range(3):
            raw = dot(
                collect, jnp.concatenate([near_ref[s, 2 * pair], near_ref[s, 2 * pair + 1]], axis=1)
            )
            for n in range(2):
                plain_rows(raw[:, 128 * n : 128 * n + 128], raw_ref.at[3 * n + s])
        for q in range(8):
            j = 8 * pair + q
            at = 128 * (q % 4)
            a = [raw_ref[3 * (q // 4) + s, at : at + 64, :] for s in range(3)]
            b = [raw_ref[3 * (q // 4) + s, at + 64 : at + 128, :] for s in range(3)]
            inner = jnp.concatenate([jnp.where(half, a[1], a[2]), jnp.where(half, b[0], b[1])], axis=0)
            outer = jnp.concatenate([jnp.where(half, 0.0, a[0]), jnp.where(half, b[2], 0.0)], axis=0)
            outer = outer.astype(BF16)
            if j in (0, 15):
                start = 1024 + 128 * (j // 15)
                transfer_rows[start : start + 128, :] = outer
            around = jnp.where(lo, tile(masked_ref, j + 2), tile(masked_ref, j))
            field_ref[:, 128 * j : 128 * j + 128] = dot_t(
                jnp.concatenate([tile(masked_ref, j + 1), around], axis=1),
                jnp.concatenate([inner.astype(BF16), outer], axis=1),
            )


def message_kernel(share_ref, one_ref, two_ref, three_ref, out_ref):
    total = share_ref[...].astype(F32)
    for ref in (one_ref, two_ref, three_ref):
        total = total + tile(ref, 16).astype(F32)
    packed = (total[:8] + total[8:]).astype(BF16)
    for n in range(64):
        out_ref[n] = packed


def middle_kernel(
    nodes_hbm, node_coupling_hbm, links_hbm, coupling_hbm, own_ref, one_ref, two_ref, three_ref,
    rows_ref, coupled_ref, linked_ref,
    links_ref, nodes_ref, node_coupling_ref, coupling_ref,
    raw_ref, coeff_ref, picked_ref, spread_ref, sems,
):
    branch = lax.axis_index("leaf")
    own = [64 + branch, 32 + (branch >> 1), 16 + (branch >> 2), 8 + (branch >> 3)]
    sources = (own_ref, one_ref, two_ref, three_ref)
    copies = start_all(
        sems,
        [(nodes_hbm.at[pl.ds(2, 14)], nodes_ref)]
        + [(node_coupling_hbm.at[:, own[n] >> 3], node_coupling_ref.at[n]) for n in range(4)]
        + [(links_hbm, links_ref)]
        + [(coupling_hbm.at[pl.ds(8 * n, 8)], coupling_ref.at[pl.ds(8 * n, 8)]) for n in range(4)],
    )
    collect = group_map()
    split = split_map()
    copies[0].wait()
    for g in range(0, 14, 2):
        raw = dot(collect, jnp.concatenate([nodes_ref[g], nodes_ref[g + 1]], axis=1))
        for n in range(2):
            plain_rows(raw[:, 128 * n : 128 * n + 128], raw_ref.at[n])
            rows_ref[512 * (g + n) : 512 * (g + n) + 512, :] = raw_ref[n].astype(BF16)

    half = low_half(64)
    row, col = iota((64, 256), 0), iota((64, 256), 1)
    even = (iota((64, 128), 0) & 1) == 0

    def node(n):
        return rows_ref[pl.ds(pl.multiple_of((own[n] - 16) * 64, 64), 64), :]

    carried = [None, (node(0), None)]
    for n in (1, 2):
        high, low = carried[n]
        longer = dot(high[:, :64], node(n))
        if low is not None:
            longer = longer + dot(low[:, :64], node(n))
        carried.append(pieces(longer))
    for copy in copies[1:5]:
        copy.wait()
    lo192 = low_half(192)
    for n in range(4):
        pick = jnp.where(((row >> 1) == (col >> 3)) & ((col & 7) == (own[n] & 7)), 1.0, 0.0).astype(BF16)
        blocks = []
        for c in range(3):
            raw = dot(pick, node_coupling_ref[n, c])
            blocks.append(jnp.where(half == even, raw, swap(raw)))
        blocks = jnp.where(lo192, jnp.concatenate(blocks, axis=0), 0.0)
        if n == 0:
            rows = blocks
        else:
            blocks = blocks.astype(BF16)
            high, low = carried[n]
            full = dot_t(blocks, jnp.concatenate([high, high], axis=0))
            if low is not None:
                full = full + dot_t(blocks, jnp.concatenate([low, low], axis=0))
            upper = full.astype(BF16).astype(F32)
            rows = jnp.where(lo192, upper, full - upper)
        coupled_ref[256 * n : 256 * n + 192, :] = rows.astype(BF16)
        coupled_ref[256 * n + 192 : 256 * n + 256, :] = jnp.zeros((64, 128), BF16)

    lo = low_half(16)
    nothing = jnp.zeros((16, 128), BF16)
    sub = lax.axis_index("sub")
    for d, ref in enumerate(sources):
        first = (sub ^ d) * 32
        for j in range(TILES):
            x = tile(ref, j)
            y = swap(x)
            for m, (a, b) in enumerate(((x, y), (y, x))):
                coeff_ref[0, first + 2 * j + m] = jnp.where(lo, a, nothing)
                coeff_ref[1, first + 2 * j + m] = jnp.where(lo, nothing, b)
    copies[5].wait()
    for leaf in range(32):
        for c in range(4):
            picked_ref[16 * leaf : 16 * leaf + 16, 128 * c : 128 * c + 128] = (
                coeff_ref[0, links_ref[2 * c, leaf] & 127]
                + coeff_ref[1, links_ref[2 * c + 1, leaf] & 127]
            )
    spread_ref[...] = dot(picked_ref[...], split).astype(BF16)
    for j in range(TILES):
        if j % 4 == 0:
            copies[6 + j // 4].wait()
        pair = []
        for leaf in (2 * j, 2 * j + 1):
            rows = spread_ref[16 * leaf : 16 * leaf + 16, :]
            pair.append(
                dot(jnp.concatenate([rows[:, :256], rows[:, 256:]], axis=0), coupling_ref[leaf])
            )
        a, b = pair
        linked_ref[:, 128 * j : 128 * j + 128] = jnp.where(
            lo, a[:16] + swap(a[16:]), swap(b[:16]) + b[16:]
        )


def downward_kernel(
    size_hbm, node_links_hbm, one_ref, three_ref, cross_ref, message_ref,
    linked_ref, field_ref, basis_ref, transfer_ref, nodes_ref, coupled_ref,
    out_ref,
    size_ref, node_links_ref, table_ref, sems,
):
    copies = start_all(sems, [(size_hbm, size_ref), (node_links_hbm, node_links_ref)])
    branch, sub = lax.axis_index("leaf"), lax.axis_index("sub")
    lo = low_half(16)
    lo8 = low_half(8)
    lo32 = low_half(32)

    pairs = []
    zeros = jnp.zeros((16, 128), BF16)
    for q in range(32):
        one, two = message_ref[2 * q].astype(F32), message_ref[2 * q + 1].astype(F32)
        one_s, two_s = swap(one), swap(two)
        pairs.append(
            jnp.concatenate([jnp.where(lo8, one, two_s), jnp.where(lo8, one_s, two)], axis=0).astype(BF16)
        )
        first = jnp.concatenate([jnp.where(lo8, one, one_s), jnp.where(lo8, one_s, one)], axis=0)
        second = jnp.concatenate([jnp.where(lo8, two, two_s), jnp.where(lo8, two_s, two)], axis=0)
        table_ref[64 + 2 * q] = jnp.concatenate([first.astype(BF16), zeros], axis=0)
        table_ref[65 + 2 * q] = jnp.concatenate([second.astype(BF16), zeros], axis=0)

    def weights(q):
        return nodes_ref[128 * (q - 8) : 128 * (q - 8) + 128, :]

    size = 32
    while size >= 8:
        parents = []
        for q in range(size, 2 * size):
            a = dot(pairs[q - size], weights(q))
            if size < 32:
                a = a[:16] + a[16:]
            high, low = pieces(a)
            parents.append(jnp.concatenate([high, low], axis=0))
            table_ref[q] = parents[-1]
        pairs = [jnp.where(lo32, parents[2 * q], parents[2 * q + 1]) for q in range(size // 2)]
        size = size // 2
    for copy in copies:
        copy.wait()
    sources = []
    for n in range(4):
        own = (64 >> n) + (branch >> n)
        a, b, c = [table_ref[node_links_ref[m, own]] for m in range(3)]
        sources += [jnp.where(lo32, a, b), c]
    down = dot(jnp.concatenate(sources, axis=1), coupled_ref[...])
    down = down[:16] + down[16:]
    down = (down + swap(down)).astype(BF16)
    half = low_half(64)
    blank = jnp.zeros((64, 128), BF16)

    def leaves(ref, j):
        both = ref[64 * j : 64 * j + 64, :]
        return jnp.concatenate([jnp.where(half, both, blank), jnp.where(half, blank, both)], axis=0)


    left = jnp.where(sub == 2, tile(three_ref, 18), tile(one_ref, 18))
    left = jnp.where(lo, zeros, jnp.where(sub == 0, cross_ref[...], left))
    right = jnp.where(sub == 1, tile(three_ref, 17), tile(one_ref, 17))
    right = jnp.where(lo, jnp.where(sub == 3, cross_ref[...], right), zeros)
    for j in range(TILES):
        far = (tile(linked_ref, j) + dot_t(down, leaves(transfer_ref, j))).astype(BF16)
        out = dot_t(far, leaves(basis_ref, j)) + tile(field_ref, j)
        if j == 0:
            out = out + dot_t(left, transfer_ref[1024:1152, :])
        if j == 15:
            out = out + dot_t(right, transfer_ref[1152:1280, :])
        out_ref[:, 128 * j : 128 * j + 128] = jnp.where(present(size_ref, j), out, 0.0).astype(BF16)


VMEM = pl.BlockSpec(memory_space=pltpu.VMEM)
HBM = pl.BlockSpec(memory_space=pltpu.HBM)


def shape(dims, dtype=BF16):
    return jax.ShapeDtypeStruct(dims, dtype)


def pinned(dims, dtype=BF16):
    return pltpu.VMEM(dims, dtype)


def stays(x):
    return pltpu.with_memory_space_constraint(x, pltpu.HBM)


def near_by(x):
    return pltpu.with_memory_space_constraint(x, pltpu.VMEM)


def call(kernel, name, outs, in_specs, out_specs, scratch, size, mib):
    return pl.pallas_call(
        kernel,
        out_shape=outs,
        in_specs=in_specs,
        out_specs=out_specs,
        scratch_shapes=scratch,
        compiler_params=pltpu.CompilerParams(vmem_limit_bytes=mib << 20),
        cost_estimate=pl.CostEstimate(flops=10**9, bytes_accessed=size, transcendentals=0),
        name=name,
    )


def dma(count):
    return pltpu.SemaphoreType.DMA((count,))


def upward(*args):
    return call(
        upward_kernel, "upward", [shape((16, PAYLOAD)), shape((16, 128))], [HBM] * 4, [VMEM] * 2,
        [
            pltpu.SMEM((32,), I32),
            pltpu.VMEM((16, 2048), BF16),
            pltpu.VMEM((4, 256, 128), BF16),
            pltpu.VMEM((4, 256, 128), BF16),
            pltpu.VMEM((16, 2048), BF16),
            pltpu.VMEM((512, 512), BF16),
            dma(4),
        ],
        10**6, 8,
    )(*args)


def near_field(*args):
    return call(
        near_kernel, "near",
        [
            pinned((16, 2048), F32), pinned((1024, 128)), pinned((1280, 128)), pinned((16, 128)),
        ],
        [HBM] * 5 + [VMEM], [VMEM] * 4,
        [
            pltpu.SMEM((32,), I32),
            pltpu.VMEM((16, 2048), BF16),
            pltpu.VMEM((3, 4, 256, 128), BF16),
            pltpu.VMEM((4, 256, 128), BF16),
            pltpu.VMEM((4, 256, 128), BF16),
            pltpu.VMEM((16, 18 * 128), BF16),
            pltpu.VMEM((6, 512, 128), F32),
            dma(5),
        ],
        3 * 10**6, 12,
    )(*args)


def message(*args):
    return call(
        message_kernel, "message", pinned((64, 8, 128)), [VMEM] * 4, VMEM, [], 10**5, 4
    )(*args)


def middle(*args):
    return call(
        middle_kernel, "middle",
        [pinned((56 * 128, 128)), pinned((1024, 128)), pinned((16, 2048), F32)],
        [HBM] * 4 + [VMEM] * 4, [VMEM] * 3,
        [
            pltpu.SMEM((8, 32), I32),
            pltpu.VMEM((14, 256, 128), BF16),
            pltpu.VMEM((4, 3, 256, 128), BF16),
            pltpu.VMEM((32, 256, 128), BF16),
            pltpu.VMEM((2, 512, 128), F32),
            pltpu.VMEM((2, 128, 16, 128), BF16),
            pltpu.VMEM((512, 512), BF16),
            pltpu.VMEM((512, 512), BF16),
            dma(10),
        ],
        6 * 10**6, 16,
    )(*args)


def downward(*args):
    return call(
        downward_kernel, "downward", shape((16, 2048)), [HBM] * 2 + [VMEM] * 10, VMEM,
        [
            pltpu.SMEM((32,), I32),
            pltpu.SMEM((3, 128), I32),
            pltpu.VMEM((128, 32, 128), BF16),
            dma(2),
        ],
        4 * 10**6, 8,
    )(*args)


def grouped(table):
    lead, rows = table.shape[:-2], table.shape[-2]
    table = jnp.swapaxes(table.reshape(*lead, rows // 8, 8, 32, 128), -3, -2)
    return table.reshape(*lead, rows // 8, 256, 128)


def body(
    vectors, leaf_size, leaf_basis, near_blocks, leaf_links, leaf_coupling, leaf_transfer,
    node_transfer, node_links, node_coupling,
):
    basis, transfer, nodes = grouped(leaf_basis), grouped(leaf_transfer), grouped(node_transfer)
    coupling = grouped(leaf_coupling)[:, 0]
    near = grouped(near_blocks.transpose(1, 0, 2))
    node_coupled = grouped(node_coupling.transpose(1, 0, 2))

    basis, transfer, nodes, coupling, near, node_coupled, vectors, leaf_size, links, node_links = map(
        stays,
        (
            basis, transfer, nodes, coupling, near, node_coupled, vectors, leaf_size, leaf_links.T,
            node_links.T,
        ),
    )
    payload, cross = upward(leaf_size, vectors, basis, transfer)
    others = [
        lax.ppermute(payload, "sub", [(s, s ^ d) for s in range(4)]) for d in (1, 2, 3)
    ]
    field, basis_p, transfer_p, share = near_field(
        leaf_size, vectors, near, basis, transfer, payload
    )

    messages = message(share, *others)
    summed = lax.all_to_all(messages, "leaf", 0, 0)

    branches = lax.axis_size("leaf")
    routes = [(4 * b + 3, 4 * b + 4) for b in range(branches - 1)]
    routes += [(4 * b, 4 * b - 1) for b in range(1, branches)]
    cross = lax.ppermute(cross, ("leaf", "sub"), routes)

    nodes_p, coupled, linked = middle(
        nodes, node_coupled, links, coupling, payload, *others
    )
    return downward(
        leaf_size, node_links, others[0], others[2], cross, summed,
        *map(near_by, (linked, field, basis_p, transfer_p, nodes_p, coupled)),
    )


def solution(mesh):
    split = ("leaf", "sub")
    placed = (
        P(None, split), P(split), P(split, None), P(split, None, None), P(split, None),
        P(split, None, None), P(split, None), P(), P(), P(),
    )
    return jax.shard_map(
        body, mesh=mesh, in_specs=placed, out_specs=P(None, split), check_vma=False
    )
```

time: 48 us -> 38 us (0.79)
  the two profiles are of different devices: /device:TPU:6 before, /device:TPU:1 now
where the time goes in v3:
time: 38 us; the launch traced here: 37.8 us
  starting transfers between devices  20.9 us (55%)
  Pallas kernels  13.6 us (36%)
  waiting for transfers between devices  3.29 us (9%)
    all_to_all x1, starting transfers between devices, body(): summed = lax.all_to_all(messages, 'leaf', 0, 0)  12.3 us
    pallas_call x1, Pallas kernels, middle(): call(middle_kernel, 'middle', [pinned((56 * 128, 128)), pinned((1024, 128...  4.93 us
    ppermute x3, starting transfers between devices, body(): lax.ppermute(payload, 'sub', [(s, s ^ d) for s in range(4)])  4.61 us
    ppermute x1, starting transfers between devices, body(): cross = lax.ppermute(cross, ('leaf', 'sub'), routes)  3.99 us
    pallas_call x1, Pallas kernels, near_field(): call(near_kernel, 'near', [pinned((16, 2048), F32), pinned((1024, 128)),...  3.11 us
    pallas_call x1, Pallas kernels, downward(): call(downward_kernel, 'downward', shape((16, 2048)), [HBM] * 2 + [VMEM] *...  3.04 us
    ppermute x3, waiting for transfers between devices, body(): lax.ppermute(payload, 'sub', [(s, s ^ d) for s in range(4)])  1.87 us
    pallas_call x1, Pallas kernels, upward(): call(upward_kernel, 'upward', [shape((16, PAYLOAD)), shape((16, 128))], [...  1.86 us
  transfers between devices with their start and end apart: 5, of which 2 were waited for; matrix products, arithmetic and copies ran while one was open for 0% of the time, Pallas kernels for 21%

profile of v3, /device:TPU:1, one launch (start us, length us, event | category | flops | bytes accessed | tf_op | source)
XLA Modules:
  0.0 37.8 jit_solution(15946908637493598981)
XLA Ops:
  0.0 1.9 %upward.1 = (bf16[16,2432]{1,0:T(8,128)(2,1)S(1)}, bf16[16,128]{1,0:T(8,128)(2,1)S(1)}) custom-call(s32[32]{0:T(128)} %size_hbm.5, bf16[16,2048]{1,0:T(8,128)(2,1)} %x_hbm.3, bf16[4,256,128]{2,1,0:T(8,128)(2,1)} %bitcast.41, bf16[4,256,128]{2,1,0:T(8,128)(2,1)} %bitcast.43), custom_call_target="tpu_custom_call" | custom-call | flops 1000000000 | bytes 1000000 | tf_op jit(solution)/shard_map/upward/pallas_call | solution.py:401
  1.9 3.8 %collective-permute-start.3 = (bf16[16,2432]{1,0:T(8,128)(2,1)S(1)}, bf16[16,2432]{1,0:T(8,128)(2,1)S(1)}, u32[]{:S(2)}, u32[]{:S(2)}) collective-permute-start(bf16[16,2432]{1,0:T(8,128)(2,1)S(1)} %get-tuple-element.14.pay_ref.own_ref), channel_id=1, source_target_pairs={{0,2},{1,3},{2,0},{3,1},{4,6},{5,7},{6,4},{7,5},{8,10},{9,11},{10,... | collective-permute-start | bytes 233480 | tf_op jit(solution)/shard_map/ppermute | solution.py:500
  5.7 0.8 %collective-permute-start.1 = (bf16[16,2432]{1,0:T(8,128)(2,1)S(1)}, bf16[16,2432]{1,0:T(8,128)(2,1)S(1)}, u32[]{:S(2)}, u32[]{:S(2)}) collective-permute-start(bf16[16,2432]{1,0:T(8,128)(2,1)S(1)} %get-tuple-element.14.pay_ref.own_ref), channel_id=1, source_target_pairs={{0,3},{1,2},{2,1},{3,0},{4,7},{5,6},{6,5},{7,4},{8,11},{9,10},{10,... | collective-permute-start | bytes 233480 | tf_op jit(solution)/shard_map/ppermute | solution.py:500
  6.5 0.0 collective-permute-start
  6.5 3.1 %near.1 = (f32[16,2048]{1,0:T(8,128)S(1)}, bf16[1024,128]{1,0:T(8,128)(2,1)S(1)}, bf16[1280,128]{1,0:T(8,128)(2,1)S(1)}, bf16[16,128]{1,0:T(8,128)(2,1)S(1)}) custom-call(s32[32]{0:T(128)} %size_hbm.5, bf16[16,2048]{1,0:T(8,128)(2,1)} %x_hbm.3, bf16[3,4,256,128]{3,2,1,0:T(8,128)(2,1)} %bitcast.40, bf16[4,256,128]{2,1,0:T(8,128)(2,1)} %bitcast.42, ...), custom_call_target="tpu_custom_call" | custom-call | flops 1000000000 | bytes 3000000 | tf_op jit(solution)/shard_map/near/pallas_call | solution.py:417
  9.6 0.0 collective-permute-done.3.two_ref
  9.6 1.9 %collective-permute-done.1.three_ref = bf16[16,2432]{1,0:T(8,128)(2,1)S(1)} collective-permute-done((bf16[16,2432]{1,0:T(8,128)(2,1)S(1)}, bf16[16,2432]{1,0:T(8,128)(2,1)S(1)}, u32[]{:S(2)}, u32[]{:S(2)}) %collective-permute-start.1) | collective-permute-done | bytes 77856 | tf_op jit(solution)/shard_map/ppermute | solution.py:500
  11.5 0.0 collective-permute-done.one_ref
  11.5 0.7 %message.1 = bf16[64,8,128]{2,1,0:T(8,128)(2,1)} custom-call(bf16[16,128]{1,0:T(8,128)(2,1)S(1)} %get-tuple-element.16.share_ref, bf16[16,2432]{1,0:T(8,128)(2,1)S(1)} %collective-permute-done.one_ref, bf16[16,2432]{1,0:T(8,128)(2,1)S(1)} %collective-permute-done.3.two_ref, bf16[16,2432]{1,0:T(8,128)(2,1)S(1)} %collective-permute-done.1.three_ref), custom_call_target="tpu_custom_call" | custom-call | flops 1000000000 | bytes 100000 | tf_op jit(solution)/shard_map/message/pallas_call | solution.py:438
  12.1 12.3 %all-to-all-start = ((bf16[64,8,128]{2,1,0:T(8,128)(2,1)}), bf16[64,8,128]{2,1,0:T(8,128)(2,1)S(1)}, u32[]{:S(2)}, u32[]{:S(2)}) async-start(bf16[64,8,128]{2,1,0:T(8,128)(2,1)} %message.1), calls=%async_computation | async-start | bytes 262144 | tf_op jit(solution)/shard_map/all_to_all | solution.py:507
  24.4 4.0 %collective-permute-start.2 = (bf16[16,128]{1,0:T(8,128)(2,1)S(1)}, bf16[16,128]{1,0:T(8,128)(2,1)S(1)}, u32[]{:S(2)}, u32[]{:S(2)}) collective-permute-start(bf16[16,128]{1,0:T(8,128)(2,1)S(1)} %get-tuple-element.15), channel_id=1, source_target_pairs={{3,4},{7,8},{11,12},{15,16},{19,20},{23,24},{27,28},{31,32},{35,36... | collective-permute-start | bytes 12296 | tf_op jit(solution)/shard_map/ppermute | solution.py:512
  28.4 4.9 %middle.1 = (bf16[7168,128]{1,0:T(8,128)(2,1)S(1)}, bf16[1024,128]{1,0:T(8,128)(2,1)S(1)}, f32[16,2048]{1,0:T(8,128)S(1)}) custom-call(bf16[16,256,128]{2,1,0:T(8,128)(2,1)} %bitcast.38, bf16[3,16,256,128]{3,2,1,0:T(8,128)(2,1)} %bitcast.36, s32[8,32]{1,0:T(8,128)} %bitcast.39, bf16[32,256,128]{2,1,0:T(8,128)(2,1)} %bitcast.37, ...), custom_call_target="tpu_custom_call" | custom-call | flops 1000000000 | bytes 6000000 | tf_op jit(solution)/shard_map/middle/pallas_call | solution.py:444
  33.4 0.0 collective-permute-done.2.cross_ref
  33.4 1.4 %all-to-all-done.message_ref = bf16[64,8,128]{2,1,0:T(8,128)(2,1)S(1)} async-done(((bf16[64,8,128]{2,1,0:T(8,128)(2,1)}), bf16[64,8,128]{2,1,0:T(8,128)(2,1)S(1)}, u32[]{:S(2)}, u32[]{:S(2)}) %all-to-all-start) | async-done | bytes 131104 | tf_op jit(solution)/shard_map/all_to_all | solution.py:507
  34.8 3.0 %downward.1 = bf16[16,2048]{1,0:T(8,128)(2,1)} custom-call(s32[32]{0:T(128)} %size_hbm.5, s32[3,128]{1,0:T(4,128)} %bitcast.45, bf16[16,2432]{1,0:T(8,128)(2,1)S(1)} %collective-permute-done.one_ref, bf16[16,2432]{1,0:T(8,128)(2,1)S(1)} %collective-permute-done.1.three_ref, bf16[16,128]{1,0:T(8,128)(2,1)S(1)} %collective-permute-done.2.cross_ref, ...), custom_call_target="tpu_custom_call" | custom-call | flops 1000000000 | bytes 4000000 | tf_op jit(solution)/shard_map/downward/pallas_call | solution.py:464
Async XLA Ops:
  1.9 7.7 %collective-permute-start.3 = (bf16[16,2432]{1,0:T(8,128)(2,1)S(1)}, bf16[16,2432]{1,0:T(8,128)(2,1)S(1)}, u32[]{:S(2)}, u32[]{:S(2)}) collective-permute-start(bf16[16,2432]{1,0:T(8,128)(2,1)S(1)} %get-tuple-element.14.pay_ref.own_ref), channel_id=1, source_target_pairs={{0,2},{1,3},{2,0},{3,1},{4,6},{5,7},{6,4},{7,5},{8,10},{9,11},{10,... | collective-permute-start | bytes 233480 | tf_op jit(solution)/shard_map/ppermute | solution.py:500
  5.7 5.8 %collective-permute-start.1 = (bf16[16,2432]{1,0:T(8,128)(2,1)S(1)}, bf16[16,2432]{1,0:T(8,128)(2,1)S(1)}, u32[]{:S(2)}, u32[]{:S(2)}) collective-permute-start(bf16[16,2432]{1,0:T(8,128)(2,1)S(1)} %get-tuple-element.14.pay_ref.own_ref), channel_id=1, source_target_pairs={{0,3},{1,2},{2,1},{3,0},{4,7},{5,6},{6,5},{7,4},{8,11},{9,10},{10,... | collective-permute-start | bytes 233480 | tf_op jit(solution)/shard_map/ppermute | solution.py:500
  6.5 5.0 %collective-permute-start = (bf16[16,2432]{1,0:T(8,128)(2,1)S(1)}, bf16[16,2432]{1,0:T(8,128)(2,1)S(1)}, u32[]{:S(2)}, u32[]{:S(2)}) collective-permute-start(bf16[16,2432]{1,0:T(8,128)(2,1)S(1)} %get-tuple-element.14.pay_ref.own_ref), channel_id=1, source_target_pairs={{0,1},{1,0},{2,3},{3,2},{4,5},{5,4},{6,7},{7,6},{8,9},{9,8},{10,11... | collective-permute-start | bytes 233480 | tf_op jit(solution)/shard_map/ppermute | solution.py:500
  12.1 22.6 %all-to-all-start = ((bf16[64,8,128]{2,1,0:T(8,128)(2,1)}), bf16[64,8,128]{2,1,0:T(8,128)(2,1)S(1)}, u32[]{:S(2)}, u32[]{:S(2)}) async-start(bf16[64,8,128]{2,1,0:T(8,128)(2,1)} %message.1), calls=%async_computation | async-start | bytes 262144 | tf_op jit(solution)/shard_map/all_to_all | solution.py:507
  24.4 8.9 %collective-permute-start.2 = (bf16[16,128]{1,0:T(8,128)(2,1)S(1)}, bf16[16,128]{1,0:T(8,128)(2,1)S(1)}, u32[]{:S(2)}, u32[]{:S(2)}) collective-permute-start(bf16[16,128]{1,0:T(8,128)(2,1)S(1)} %get-tuple-element.15), channel_id=1, source_target_pairs={{3,4},{7,8},{11,12},{15,16},{19,20},{23,24},{27,28},{31,32},{35,36... | collective-permute-start | bytes 12296 | tf_op jit(solution)/shard_map/ppermute | solution.py:512

commit v4 on v3

--- a/solution.py
+++ b/solution.py
@@ -80,7 +80,7 @@
 
 
 def upward_kernel(
-    size_hbm, x_hbm, basis_hbm, transfer_hbm, pay_ref, cross_ref,
+    size_hbm, x_hbm, basis_hbm, transfer_hbm, pay_ref,
     size_ref, x_ref, basis_ref, transfer_ref, masked_ref, map_ref, sems,
 ):
     copies = start_all(
@@ -120,15 +120,13 @@
     packed = jnp.where(low_half(8), share[:8], share[8:])
     high = packed.astype(BF16).astype(F32)
     pay_ref[:, COEFF : COEFF + 128] = jnp.concatenate([high, packed - high], axis=0).astype(BF16)
-    first, last = tile(masked_ref, 0), tile(masked_ref, 15)
-    pay_ref[:, COEFF + 128 : COEFF + 256] = first
-    pay_ref[:, COEFF + 256 : COEFF + 384] = last
-    cross_ref[...] = jnp.where(lax.axis_index("sub") == 0, first, last)
+    pay_ref[:, COEFF + 128 : COEFF + 256] = tile(masked_ref, 0)
+    pay_ref[:, COEFF + 256 : COEFF + 384] = tile(masked_ref, 15)
 
 
 def near_kernel(
     size_hbm, x_hbm, near_hbm, basis_hbm, transfer_hbm, pay_ref,
-    field_ref, basis_rows, transfer_rows, share_ref,
+    field_ref, basis_rows, carry_rows, share_ref,
     size_ref, x_ref, near_ref, basis_ref, transfer_ref, masked_ref, raw_ref, sems,
 ):
     copies = start_all(
@@ -141,18 +139,22 @@
     share_ref[...] = tile(pay_ref, 16)
     collect = group_map()
     half = low_half(64)
-    copies[0].wait()
-    copies[1].wait()
+    row = iota((64, 128), 0)
+    for copy in copies:
+        copy.wait()
     for g in range(4):
         raw = dot(collect, jnp.concatenate([basis_ref[g], transfer_ref[g]], axis=1))
-        for n, rows in enumerate((basis_rows, transfer_rows)):
-            plain_rows(raw[:, 128 * n : 128 * n + 128], raw_ref.at[n])
-            for q in range(4):
-                pair = [raw_ref[n, 128 * q + 64 * m : 128 * q + 64 * m + 64, :] for m in range(2)]
-                start = 256 * g + 64 * q
-                rows[start : start + 64, :] = jnp.where(half, pair[0], pair[1]).astype(BF16)
-    for copy in copies[2:]:
-        copy.wait()
+        for n in range(2):
+            plain_rows(raw[:, 128 * n : 128 * n + 128], raw_ref.at[2 * g + n])
+        for q in range(4):
+            j = 4 * g + q
+            pair = [raw_ref[2 * g, 128 * q + 64 * m : 128 * q + 64 * m + 64, :] for m in range(2)]
+            pair = [jnp.where(row < size_ref[2 * j + m], pair[m], 0.0) for m in range(2)]
+            start = 64 * j
+            basis_rows[start : start + 64, :] = jnp.where(half, *pair).astype(BF16)
+            blocks = jnp.concatenate([jnp.where(half, pair[0], 0.0), jnp.where(half, 0.0, pair[1])], axis=0)
+            carry = dot(blocks.astype(BF16), raw_ref[2 * g + 1, 128 * q : 128 * q + 128, :].astype(BF16))
+            carry_rows[start : start + 64, :] = jnp.where(half, carry[:64], carry[64:]).astype(BF16)
     masked_ref[:, 0:128] = jnp.zeros((16, 128), BF16)
     masked_ref[:, 17 * 128 : 18 * 128] = jnp.zeros((16, 128), BF16)
     for j in range(TILES):
@@ -172,29 +174,37 @@
             b = [raw_ref[3 * (q // 4) + s, at + 64 : at + 128, :] for s in range(3)]
             inner = jnp.concatenate([jnp.where(half, a[1], a[2]), jnp.where(half, b[0], b[1])], axis=0)
             outer = jnp.concatenate([jnp.where(half, 0.0, a[0]), jnp.where(half, b[2], 0.0)], axis=0)
-            outer = outer.astype(BF16)
             if j in (0, 15):
                 start = 1024 + 128 * (j // 15)
-                transfer_rows[start : start + 128, :] = outer
+                limit = jnp.where(iota((128, 128), 0) < 64, size_ref[2 * j], size_ref[2 * j + 1])
+                edge = jnp.where((iota((128, 128), 0) & 63) < limit, outer, 0.0)
+                carry_rows[start : start + 128, :] = edge.astype(BF16)
+            outer = outer.astype(BF16)
             around = jnp.where(lo, tile(masked_ref, j + 2), tile(masked_ref, j))
-            field_ref[:, 128 * j : 128 * j + 128] = dot_t(
+            near = dot_t(
                 jnp.concatenate([tile(masked_ref, j + 1), around], axis=1),
                 jnp.concatenate([inner.astype(BF16), outer], axis=1),
             )
-
-
-def message_kernel(share_ref, one_ref, two_ref, three_ref, out_ref):
+            field_ref[:, 128 * j : 128 * j + 128] = jnp.where(present(size_ref, j), near, 0.0)
+
+
+def message_kernel(share_ref, one_ref, two_ref, three_ref, out_ref, cross_ref, sides_ref):
     total = share_ref[...].astype(F32)
     for ref in (one_ref, two_ref, three_ref):
         total = total + tile(ref, 16).astype(F32)
     packed = (total[:8] + total[8:]).astype(BF16)
     for n in range(64):
         out_ref[n] = packed
+    sub = lax.axis_index("sub")
+    cross_ref[...] = jnp.where(sub == 0, tile(three_ref, 18), tile(three_ref, 17))
+    sides_ref[0] = jnp.where(sub == 2, tile(three_ref, 18), tile(one_ref, 18))
+    sides_ref[1] = jnp.where(sub == 1, tile(three_ref, 17), tile(one_ref, 17))
 
 
 def middle_kernel(
-    nodes_hbm, node_coupling_hbm, links_hbm, coupling_hbm, own_ref, one_ref, two_ref, three_ref,
-    rows_ref, coupled_ref, linked_ref,
+    nodes_hbm, node_coupling_hbm, links_hbm, node_links_hbm, coupling_hbm,
+    own_ref, two_ref, three_ref, one_ref, near_ref, basis_ref,
+    rows_ref, coupled_ref, field_ref, node_links_ref,
     links_ref, nodes_ref, node_coupling_ref, coupling_ref,
     raw_ref, coeff_ref, picked_ref, spread_ref, sems,
 ):
@@ -206,11 +216,34 @@
         [(nodes_hbm.at[pl.ds(2, 14)], nodes_ref)]
         + [(node_coupling_hbm.at[:, own[n] >> 3], node_coupling_ref.at[n]) for n in range(4)]
         + [(links_hbm, links_ref)]
-        + [(coupling_hbm.at[pl.ds(8 * n, 8)], coupling_ref.at[pl.ds(8 * n, 8)]) for n in range(4)],
+        + [(coupling_hbm.at[pl.ds(8 * n, 8)], coupling_ref.at[pl.ds(8 * n, 8)]) for n in range(4)]
+        + [(node_links_hbm, node_links_ref)],
     )
     collect = group_map()
     split = split_map()
-    copies[0].wait()
+    lo = low_half(16)
+    nothing = jnp.zeros((16, 128), BF16)
+    half = low_half(64)
+    blank = jnp.zeros((64, 128), BF16)
+    sub = lax.axis_index("sub")
+    for d, ref in enumerate(sources):
+        first = (sub ^ d) * 32
+        for j in range(TILES):
+            x = tile(ref, j)
+            y = swap(x)
+            for m, (a, b) in enumerate(((x, y), (y, x))):
+                coeff_ref[0, first + 2 * j + m] = jnp.where(lo, a, nothing)
+                coeff_ref[1, first + 2 * j + m] = jnp.where(lo, nothing, b)
+    copies[5].wait()
+    for leaf in range(32):
+        for c in range(4):
+            picked_ref[16 * leaf : 16 * leaf + 16, 128 * c : 128 * c + 128] = (
+                coeff_ref[0, links_ref[2 * c, leaf] & 127]
+                + coeff_ref[1, links_ref[2 * c + 1, leaf] & 127]
+            )
+    spread_ref[...] = dot(picked_ref[...], split).astype(BF16)
+    for copy in copies[:5] + copies[6:]:
+        copy.wait()
     for g in range(0, 14, 2):
         raw = dot(collect, jnp.concatenate([nodes_ref[g], nodes_ref[g + 1]], axis=1))
         for n in range(2):
@@ -231,8 +264,6 @@
         if low is not None:
             longer = longer + dot(low[:, :64], node(n))
         carried.append(pieces(longer))
-    for copy in copies[1:5]:
-        copy.wait()
     lo192 = low_half(192)
     for n in range(4):
         pick = jnp.where(((row >> 1) == (col >> 3)) & ((col & 7) == (own[n] & 7)), 1.0, 0.0).astype(BF16)
@@ -254,110 +285,85 @@
         coupled_ref[256 * n : 256 * n + 192, :] = rows.astype(BF16)
         coupled_ref[256 * n + 192 : 256 * n + 256, :] = jnp.zeros((64, 128), BF16)
 
-    lo = low_half(16)
-    nothing = jnp.zeros((16, 128), BF16)
-    sub = lax.axis_index("sub")
-    for d, ref in enumerate(sources):
-        first = (sub ^ d) * 32
-        for j in range(TILES):
-            x = tile(ref, j)
-            y = swap(x)
-            for m, (a, b) in enumerate(((x, y), (y, x))):
-                coeff_ref[0, first + 2 * j + m] = jnp.where(lo, a, nothing)
-                coeff_ref[1, first + 2 * j + m] = jnp.where(lo, nothing, b)
-    copies[5].wait()
-    for leaf in range(32):
-        for c in range(4):
-            picked_ref[16 * leaf : 16 * leaf + 16, 128 * c : 128 * c + 128] = (
-                coeff_ref[0, links_ref[2 * c, leaf] & 127]
-                + coeff_ref[1, links_ref[2 * c + 1, leaf] & 127]
-            )
-    spread_ref[...] = dot(picked_ref[...], split).astype(BF16)
     for j in range(TILES):
-        if j % 4 == 0:
-            copies[6 + j // 4].wait()
-        pair = []
-        for leaf in (2 * j, 2 * j + 1):
-            rows = spread_ref[16 * leaf : 16 * leaf + 16, :]
-            pair.append(
-                dot(jnp.concatenate([rows[:, :256], rows[:, 256:]], axis=0), coupling_ref[leaf])
-            )
-        a, b = pair
-        linked_ref[:, 128 * j : 128 * j + 128] = jnp.where(
-            lo, a[:16] + swap(a[16:]), swap(b[:16]) + b[16:]
+        rows = spread_ref[32 * j : 32 * j + 32, :]
+        both = dot(
+            jnp.concatenate([rows[:, :256], rows[:, 256:]], axis=0),
+            jnp.concatenate([coupling_ref[2 * j], coupling_ref[2 * j + 1]], axis=1),
         )
+        a = jnp.concatenate([both[:16, :128], both[32:48, :128]], axis=0)
+        b = jnp.concatenate([both[16:32, 128:], both[48:, 128:]], axis=0)
+        far = jnp.where(lo, a[:16] + swap(a[16:]), swap(b[:16]) + b[16:]).astype(BF16)
+        rows = basis_ref[64 * j : 64 * j + 64, :]
+        blocks = jnp.concatenate([jnp.where(half, rows, blank), jnp.where(half, blank, rows)], axis=0)
+        field_ref[:, 128 * j : 128 * j + 128] = tile(near_ref, j) + dot_t(far, blocks)
 
 
 def downward_kernel(
-    size_hbm, node_links_hbm, one_ref, three_ref, cross_ref, message_ref,
-    linked_ref, field_ref, basis_ref, transfer_ref, nodes_ref, coupled_ref,
+    links_ref, sides_ref, cross_ref, message_ref,
+    field_ref, carry_ref, nodes_ref, coupled_ref,
     out_ref,
-    size_ref, node_links_ref, table_ref, sems,
+    node_links_ref, table_ref, sem,
 ):
-    copies = start_all(sems, [(size_hbm, size_ref), (node_links_hbm, node_links_ref)])
+    copy = pltpu.make_async_copy(links_ref, node_links_ref, sem)
+    copy.start()
     branch, sub = lax.axis_index("leaf"), lax.axis_index("sub")
     lo = low_half(16)
     lo8 = low_half(8)
     lo32 = low_half(32)
 
-    pairs = []
     zeros = jnp.zeros((16, 128), BF16)
+
+    def weights(k):
+        return nodes_ref[pl.ds(pl.multiple_of(128 * (k - 8), 128), 128), :]
+
     for q in range(32):
         one, two = message_ref[2 * q].astype(F32), message_ref[2 * q + 1].astype(F32)
-        one_s, two_s = swap(one), swap(two)
-        pairs.append(
-            jnp.concatenate([jnp.where(lo8, one, two_s), jnp.where(lo8, one_s, two)], axis=0).astype(BF16)
+        pair = jnp.concatenate(
+            [jnp.where(lo8, one, swap(two)), jnp.where(lo8, swap(one), two)], axis=0
         )
-        first = jnp.concatenate([jnp.where(lo8, one, one_s), jnp.where(lo8, one_s, one)], axis=0)
-        second = jnp.concatenate([jnp.where(lo8, two, two_s), jnp.where(lo8, two_s, two)], axis=0)
-        table_ref[64 + 2 * q] = jnp.concatenate([first.astype(BF16), zeros], axis=0)
-        table_ref[65 + 2 * q] = jnp.concatenate([second.astype(BF16), zeros], axis=0)
-
-    def weights(q):
-        return nodes_ref[128 * (q - 8) : 128 * (q - 8) + 128, :]
-
-    size = 32
-    while size >= 8:
-        parents = []
-        for q in range(size, 2 * size):
-            a = dot(pairs[q - size], weights(q))
-            if size < 32:
-                a = a[:16] + a[16:]
-            high, low = pieces(a)
-            parents.append(jnp.concatenate([high, low], axis=0))
-            table_ref[q] = parents[-1]
-        pairs = [jnp.where(lo32, parents[2 * q], parents[2 * q + 1]) for q in range(size // 2)]
-        size = size // 2
-    for copy in copies:
-        copy.wait()
+        value = dot(pair.astype(BF16), nodes_ref[128 * (q + 24) : 128 * (q + 24) + 128, :])
+        table_ref[q] = jnp.concatenate(pieces(value), axis=0)
+
+    def leaf_node(k):
+        one = message_ref[k - 64].astype(F32)
+        other = swap(one)
+        rows = jnp.concatenate([jnp.where(lo8, one, other), jnp.where(lo8, other, one)], axis=0)
+        return jnp.concatenate([rows.astype(BF16), zeros], axis=0)
+
+    def parent(k, children):
+        value = dot(jnp.where(lo32, *children), weights(k))
+        return jnp.concatenate(pieces(value[:16] + value[16:]), axis=0)
+
+    copy.wait()
+    ends = [[node_links_ref[m, (64 >> n) + (branch >> n)] for m in range(3)] for n in range(4)]
+    sixteen = ends[2] + [2 * k + m for k in ends[3] for m in range(2)]
+    values = [parent(k, [table_ref[2 * k - 32], table_ref[2 * k - 31]]) for k in sixteen]
+    found = [
+        [leaf_node(k) for k in ends[0]],
+        [table_ref[k - 32] for k in ends[1]],
+        values[:3],
+        [parent(k, values[3 + 2 * n : 5 + 2 * n]) for n, k in enumerate(ends[3])],
+    ]
     sources = []
-    for n in range(4):
-        own = (64 >> n) + (branch >> n)
-        a, b, c = [table_ref[node_links_ref[m, own]] for m in range(3)]
+    for a, b, c in found:
         sources += [jnp.where(lo32, a, b), c]
     down = dot(jnp.concatenate(sources, axis=1), coupled_ref[...])
     down = down[:16] + down[16:]
     down = (down + swap(down)).astype(BF16)
-    half = low_half(64)
-    blank = jnp.zeros((64, 128), BF16)
-
-    def leaves(ref, j):
-        both = ref[64 * j : 64 * j + 64, :]
-        return jnp.concatenate([jnp.where(half, both, blank), jnp.where(half, blank, both)], axis=0)
-
-
-    left = jnp.where(sub == 2, tile(three_ref, 18), tile(one_ref, 18))
-    left = jnp.where(lo, zeros, jnp.where(sub == 0, cross_ref[...], left))
-    right = jnp.where(sub == 1, tile(three_ref, 17), tile(one_ref, 17))
-    right = jnp.where(lo, jnp.where(sub == 3, cross_ref[...], right), zeros)
-    for j in range(TILES):
-        far = (tile(linked_ref, j) + dot_t(down, leaves(transfer_ref, j))).astype(BF16)
-        out = dot_t(far, leaves(basis_ref, j)) + tile(field_ref, j)
-        if j == 0:
-            out = out + dot_t(left, transfer_ref[1024:1152, :])
-        if j == 15:
-            out = out + dot_t(right, transfer_ref[1152:1280, :])
-        out_ref[:, 128 * j : 128 * j + 128] = jnp.where(present(size_ref, j), out, 0.0).astype(BF16)
+    ends = jnp.concatenate([jnp.where(lo, down, zeros), jnp.where(lo, zeros, down)], axis=0)
+    shared = dot_t(ends, carry_ref[0:1024, :])
+    left = jnp.where(lo, zeros, jnp.where(sub == 0, cross_ref[...], sides_ref[0]))
+    right = jnp.where(lo, jnp.where(sub == 3, cross_ref[...], sides_ref[1]), zeros)
+    for t in range(8):
+        a, b = shared[:16, 128 * t : 128 * t + 128], shared[16:, 128 * t : 128 * t + 128]
+        for j, far in ((2 * t, jnp.where(lo, a, swap(b))), (2 * t + 1, jnp.where(lo, swap(a), b))):
+            out = far + tile(field_ref, j)
+            if j == 0:
+                out = out + dot_t(left, carry_ref[1024:1152, :])
+            if j == 15:
+                out = out + dot_t(right, carry_ref[1152:1280, :])
+            out_ref[:, 128 * j : 128 * j + 128] = out.astype(BF16)
 
 
 VMEM = pl.BlockSpec(memory_space=pltpu.VMEM)
@@ -399,7 +405,7 @@
 
 def upward(*args):
     return call(
-        upward_kernel, "upward", [shape((16, PAYLOAD)), shape((16, 128))], [HBM] * 4, [VMEM] * 2,
+        upward_kernel, "upward", shape((16, PAYLOAD)), [HBM] * 4, VMEM,
         [
             pltpu.SMEM((32,), I32),
             pltpu.VMEM((16, 2048), BF16),
@@ -427,7 +433,7 @@
             pltpu.VMEM((4, 256, 128), BF16),
             pltpu.VMEM((4, 256, 128), BF16),
             pltpu.VMEM((16, 18 * 128), BF16),
-            pltpu.VMEM((6, 512, 128), F32),
+            pltpu.VMEM((8, 512, 128), F32),
             dma(5),
         ],
         3 * 10**6, 12,
@@ -436,15 +442,16 @@
 
 def message(*args):
     return call(
-        message_kernel, "message", pinned((64, 8, 128)), [VMEM] * 4, VMEM, [], 10**5, 4
+        message_kernel, "message", [shape((64, 8, 128)), shape((16, 128)), shape((2, 16, 128))], [VMEM] * 4, [VMEM] * 3, [],
+        10**5, 4,
     )(*args)
 
 
 def middle(*args):
     return call(
         middle_kernel, "middle",
-        [pinned((56 * 128, 128)), pinned((1024, 128)), pinned((16, 2048), F32)],
-        [HBM] * 4 + [VMEM] * 4, [VMEM] * 3,
+        [pinned((56 * 128, 128)), pinned((1024, 128)), pinned((16, 2048), F32), pinned((3, 128), I32)],
+        [HBM] * 5 + [VMEM] * 6, [VMEM] * 4,
         [
             pltpu.SMEM((8, 32), I32),
             pltpu.VMEM((14, 256, 128), BF16),
@@ -454,7 +461,7 @@
             pltpu.VMEM((2, 128, 16, 128), BF16),
             pltpu.VMEM((512, 512), BF16),
             pltpu.VMEM((512, 512), BF16),
-            dma(10),
+            dma(11),
         ],
         6 * 10**6, 16,
     )(*args)
@@ -462,13 +469,8 @@
 
 def downward(*args):
     return call(
-        downward_kernel, "downward", shape((16, 2048)), [HBM] * 2 + [VMEM] * 10, VMEM,
-        [
-            pltpu.SMEM((32,), I32),
-            pltpu.SMEM((3, 128), I32),
-            pltpu.VMEM((128, 32, 128), BF16),
-            dma(2),
-        ],
+        downward_kernel, "downward", shape((16, 2048)), [VMEM] * 8, VMEM,
+        [pltpu.SMEM((3, 128), I32), pltpu.VMEM((32, 32, 128), BF16), pltpu.SemaphoreType.DMA],
         4 * 10**6, 8,
     )(*args)
 
@@ -495,28 +497,29 @@
             node_links.T,
         ),
     )
-    payload, cross = upward(leaf_size, vectors, basis, transfer)
+    payload = upward(leaf_size, vectors, basis, transfer)
     others = [
         lax.ppermute(payload, "sub", [(s, s ^ d) for s in range(4)]) for d in (1, 2, 3)
     ]
-    field, basis_p, transfer_p, share = near_field(
+    near_part, basis_p, carry, share = near_field(
         leaf_size, vectors, near, basis, transfer, payload
     )
 
-    messages = message(share, *others)
+    messages, cross, sides = message(share, *others)
     summed = lax.all_to_all(messages, "leaf", 0, 0)
 
     branches = lax.axis_size("leaf")
-    routes = [(4 * b + 3, 4 * b + 4) for b in range(branches - 1)]
-    routes += [(4 * b, 4 * b - 1) for b in range(1, branches)]
+    routes = [(4 * b, 4 * b + 4) for b in range(branches - 1)]
+    routes += [(4 * b + 3, 4 * b - 1) for b in range(1, branches)]
     cross = lax.ppermute(cross, ("leaf", "sub"), routes)
 
-    nodes_p, coupled, linked = middle(
-        nodes, node_coupled, links, coupling, payload, *others
+    nodes_p, coupled, field, partners = middle(
+        nodes, node_coupled, links, node_links, coupling, payload, others[1], others[2], others[0],
+        near_by(near_part), near_by(basis_p),
     )
     return downward(
-        leaf_size, node_links, others[0], others[2], cross, summed,
-        *map(near_by, (linked, field, basis_p, transfer_p, nodes_p, coupled)),
+        near_by(partners), sides, cross, summed,
+        *map(near_by, (field, carry, nodes_p, coupled)),
     )
 
 

time: 38 us -> 37.1 us (0.976)
  Pallas kernels: 13.6 us -> 12.6 us
  starting transfers between devices: 20.9 us -> 20.4 us
  waiting for transfers between devices: 3.29 us -> 3.79 us
    pallas_call x3, Pallas kernels: 5.56 us -> 4.59 us  [the longest x1 2.07 us: downward(): call(downward_kernel, 'downward', shape((16, 2048)), [VMEM] * 8, VMEM, [p...]
    all_to_all x1, waiting for transfers between devices: 1.42 us -> 2.09 us  [body(): summed = lax.all_to_all(messages, 'leaf', 0, 0)]
    ppermute x1, starting transfers between devices: 3.99 us -> 3.54 us  [body(): cross = lax.ppermute(cross, ('leaf', 'sub'), routes)]
  transfers between devices with their start and end apart: 5 -> 5, of which waited for: 2 -> 2; matrix products, arithmetic and copies ran while one was open for 0% -> 0% of each run, Pallas kernels for 21% -> 22%
where the time goes in v4:
time: 37.1 us; the launch traced here: 36.9 us
  starting transfers between devices  20.4 us (55%)
  Pallas kernels  12.6 us (34%)
  waiting for transfers between devices  3.79 us (10%)
    all_to_all x1, starting transfers between devices, body(): summed = lax.all_to_all(messages, 'leaf', 0, 0)  12.3 us
    pallas_call x1, Pallas kernels, middle(): call(middle_kernel, 'middle', [pinned((56 * 128, 128)), pinned((1024, 128...  4.71 us
    ppermute x3, starting transfers between devices, body(): lax.ppermute(payload, 'sub', [(s, s ^ d) for s in range(4)])  4.61 us
    ppermute x1, starting transfers between devices, body(): cross = lax.ppermute(cross, ('leaf', 'sub'), routes)  3.54 us
    pallas_call x1, Pallas kernels, near_field(): call(near_kernel, 'near', [pinned((16, 2048), F32), pinned((1024, 128)),...  3.28 us
    all_to_all x1, waiting for transfers between devices, body(): summed = lax.all_to_all(messages, 'leaf', 0, 0)  2.09 us
    pallas_call x1, Pallas kernels, downward(): call(downward_kernel, 'downward', shape((16, 2048)), [VMEM] * 8, VMEM, [p...  2.07 us
    pallas_call x1, Pallas kernels, upward(): call(upward_kernel, 'upward', shape((16, PAYLOAD)), [HBM] * 4, VMEM, [plt...  1.86 us
  transfers between devices with their start and end apart: 5, of which 2 were waited for; matrix products, arithmetic and copies ran while one was open for 0% of the time, Pallas kernels for 22%

profile of v4, /device:TPU:1, one launch (start us, length us, event | category | flops | bytes accessed | tf_op | source)
XLA Modules:
  0.0 36.9 jit_solution(8072397557585457247)
XLA Ops:
  0.0 1.9 %upward.1.pay_ref.own_ref = bf16[16,2432]{1,0:T(8,128)(2,1)S(1)} custom-call(s32[32]{0:T(128)} %size_hbm.3, bf16[16,2048]{1,0:T(8,128)(2,1)} %x_hbm.3, bf16[4,256,128]{2,1,0:T(8,128)(2,1)} %bitcast.42, bf16[4,256,128]{2,1,0:T(8,128)(2,1)} %bitcast.44), custom_call_target="tpu_custom_call" | custom-call | flops 1000000000 | bytes 1000000 | tf_op jit(solution)/shard_map/upward/pallas_call | solution.py:407
  1.9 3.8 %collective-permute-start = (bf16[16,2432]{1,0:T(8,128)(2,1)S(1)}, bf16[16,2432]{1,0:T(8,128)(2,1)S(1)}, u32[]{:S(2)}, u32[]{:S(2)}) collective-permute-start(bf16[16,2432]{1,0:T(8,128)(2,1)S(1)} %upward.1.pay_ref.own_ref), channel_id=1, source_target_pairs={{0,2},{1,3},{2,0},{3,1},{4,6},{5,7},{6,4},{7,5},{8,10},{9,11},{10,... | collective-permute-start | bytes 233480 | tf_op jit(solution)/shard_map/ppermute | solution.py:502
  5.7 0.8 %collective-permute-start.1 = (bf16[16,2432]{1,0:T(8,128)(2,1)S(1)}, bf16[16,2432]{1,0:T(8,128)(2,1)S(1)}, u32[]{:S(2)}, u32[]{:S(2)}) collective-permute-start(bf16[16,2432]{1,0:T(8,128)(2,1)S(1)} %upward.1.pay_ref.own_ref), channel_id=1, source_target_pairs={{0,3},{1,2},{2,1},{3,0},{4,7},{5,6},{6,5},{7,4},{8,11},{9,10},{10,... | collective-permute-start | bytes 233480 | tf_op jit(solution)/shard_map/ppermute | solution.py:502
  6.5 0.0 collective-permute-start.2
  6.5 3.3 %near.1 = (f32[16,2048]{1,0:T(8,128)S(1)}, bf16[1024,128]{1,0:T(8,128)(2,1)S(1)}, bf16[1280,128]{1,0:T(8,128)(2,1)S(1)}, bf16[16,128]{1,0:T(8,128)(2,1)S(1)}) custom-call(s32[32]{0:T(128)} %size_hbm.3, bf16[16,2048]{1,0:T(8,128)(2,1)} %x_hbm.3, bf16[3,4,256,128]{3,2,1,0:T(8,128)(2,1)} %bitcast.41, bf16[4,256,128]{2,1,0:T(8,128)(2,1)} %bitcast.43, ...), custom_call_target="tpu_custom_call" | custom-call | flops 1000000000 | bytes 3000000 | tf_op jit(solution)/shard_map/near/pallas_call | solution.py:423
  9.8 0.0 collective-permute-done.two_ref
  9.8 1.7 %collective-permute-done.1.three_ref = bf16[16,2432]{1,0:T(8,128)(2,1)S(1)} collective-permute-done((bf16[16,2432]{1,0:T(8,128)(2,1)S(1)}, bf16[16,2432]{1,0:T(8,128)(2,1)S(1)}, u32[]{:S(2)}, u32[]{:S(2)}) %collective-permute-start.1) | collective-permute-done | bytes 77856 | tf_op jit(solution)/shard_map/ppermute | solution.py:502
  11.5 0.0 collective-permute-done.2.one_ref
  11.5 0.7 %message.1 = (bf16[64,8,128]{2,1,0:T(8,128)(2,1)}, bf16[16,128]{1,0:T(8,128)(2,1)S(1)}, bf16[2,16,128]{2,1,0:T(8,128)(2,1)S(1)}) custom-call(bf16[16,128]{1,0:T(8,128)(2,1)S(1)} %get-tuple-element.19.share_ref, bf16[16,2432]{1,0:T(8,128)(2,1)S(1)} %collective-permute-done.2.one_ref, bf16[16,2432]{1,0:T(8,128)(2,1)S(1)} %collective-permute-done.two_ref, ...), custom_call_target="tpu_custom_call" | custom-call | flops 1000000000 | bytes 100000 | tf_op jit(solution)/shard_map/message/pallas_call | solution.py:444
  12.1 12.3 %all-to-all-start = ((bf16[64,8,128]{2,1,0:T(8,128)(2,1)}), bf16[64,8,128]{2,1,0:T(8,128)(2,1)S(1)}, u32[]{:S(2)}, u32[]{:S(2)}) async-start(bf16[64,8,128]{2,1,0:T(8,128)(2,1)} %get-tuple-element.22), calls=%async_computation | async-start | bytes 262144 | tf_op jit(solution)/shard_map/all_to_all | solution.py:509
  24.4 3.5 %collective-permute-start.3 = (bf16[16,128]{1,0:T(8,128)(2,1)S(1)}, bf16[16,128]{1,0:T(8,128)(2,1)S(1)}, u32[]{:S(2)}, u32[]{:S(2)}) collective-permute-start(bf16[16,128]{1,0:T(8,128)(2,1)S(1)} %get-tuple-element.21), channel_id=1, source_target_pairs={{0,4},{4,8},{8,12},{12,16},{16,20},{20,24},{24,28},{28,32},{32,36}... | collective-permute-start | bytes 12296 | tf_op jit(solution)/shard_map/ppermute | solution.py:514
  28.0 4.7 %middle.1 = (bf16[7168,128]{1,0:T(8,128)(2,1)S(1)}, bf16[1024,128]{1,0:T(8,128)(2,1)S(1)}, f32[16,2048]{1,0:T(8,128)S(1)}, s32[3,128]{1,0:T(4,128)S(1)}) custom-call(bf16[16,256,128]{2,1,0:T(8,128)(2,1)} %bitcast.38, bf16[3,16,256,128]{3,2,1,0:T(8,128)(2,1)} %bitcast.36, s32[8,32]{1,0:T(8,128)} %bitcast.39, s32[3,128]{1,0:T(4,128)} %bitcast.40, ...), custom_call_target="tpu_custom_call" | custom-call | flops 1000000000 | bytes 6000000 | tf_op jit(solution)/shard_map/middle/pallas_call | solution.py:451
  32.7 0.0 collective-permute-done.3.cross_ref
  32.7 2.1 %all-to-all-done.message_ref = bf16[64,8,128]{2,1,0:T(8,128)(2,1)S(1)} async-done(((bf16[64,8,128]{2,1,0:T(8,128)(2,1)}), bf16[64,8,128]{2,1,0:T(8,128)(2,1)S(1)}, u32[]{:S(2)}, u32[]{:S(2)}) %all-to-all-start) | async-done | bytes 131104 | tf_op jit(solution)/shard_map/all_to_all | solution.py:509
  34.8 2.1 %downward.1 = bf16[16,2048]{1,0:T(8,128)(2,1)} custom-call(s32[3,128]{1,0:T(4,128)S(1)} %get-tuple-element.18.links_ref, bf16[2,16,128]{2,1,0:T(8,128)(2,1)S(1)} %get-tuple-element.20.sides_ref, bf16[16,128]{1,0:T(8,128)(2,1)S(1)} %collective-permute-done.3.cross_ref, bf16[64,8,128]{2,1,0:T(8,128)(2,1)S(1)} %all-to-all-done.message_ref, ...), custom_call_target="tpu_custom_call" | custom-call | flops 1000000000 | bytes 4000000 | tf_op jit(solution)/shard_map/downward/pallas_call | solution.py:471
Async XLA Ops:
  1.9 7.9 %collective-permute-start = (bf16[16,2432]{1,0:T(8,128)(2,1)S(1)}, bf16[16,2432]{1,0:T(8,128)(2,1)S(1)}, u32[]{:S(2)}, u32[]{:S(2)}) collective-permute-start(bf16[16,2432]{1,0:T(8,128)(2,1)S(1)} %upward.1.pay_ref.own_ref), channel_id=1, source_target_pairs={{0,2},{1,3},{2,0},{3,1},{4,6},{5,7},{6,4},{7,5},{8,10},{9,11},{10,... | collective-permute-start | bytes 233480 | tf_op jit(solution)/shard_map/ppermute | solution.py:502
  5.7 5.8 %collective-permute-start.1 = (bf16[16,2432]{1,0:T(8,128)(2,1)S(1)}, bf16[16,2432]{1,0:T(8,128)(2,1)S(1)}, u32[]{:S(2)}, u32[]{:S(2)}) collective-permute-start(bf16[16,2432]{1,0:T(8,128)(2,1)S(1)} %upward.1.pay_ref.own_ref), channel_id=1, source_target_pairs={{0,3},{1,2},{2,1},{3,0},{4,7},{5,6},{6,5},{7,4},{8,11},{9,10},{10,... | collective-permute-start | bytes 233480 | tf_op jit(solution)/shard_map/ppermute | solution.py:502
  6.5 5.0 %collective-permute-start.2 = (bf16[16,2432]{1,0:T(8,128)(2,1)S(1)}, bf16[16,2432]{1,0:T(8,128)(2,1)S(1)}, u32[]{:S(2)}, u32[]{:S(2)}) collective-permute-start(bf16[16,2432]{1,0:T(8,128)(2,1)S(1)} %upward.1.pay_ref.own_ref), channel_id=1, source_target_pairs={{0,1},{1,0},{2,3},{3,2},{4,5},{5,4},{6,7},{7,6},{8,9},{9,8},{10,11... | collective-permute-start | bytes 233480 | tf_op jit(solution)/shard_map/ppermute | solution.py:502
  12.1 22.6 %all-to-all-start = ((bf16[64,8,128]{2,1,0:T(8,128)(2,1)}), bf16[64,8,128]{2,1,0:T(8,128)(2,1)S(1)}, u32[]{:S(2)}, u32[]{:S(2)}) async-start(bf16[64,8,128]{2,1,0:T(8,128)(2,1)} %get-tuple-element.22), calls=%async_computation | async-start | bytes 262144 | tf_op jit(solution)/shard_map/all_to_all | solution.py:509
  24.4 8.3 %collective-permute-start.3 = (bf16[16,128]{1,0:T(8,128)(2,1)S(1)}, bf16[16,128]{1,0:T(8,128)(2,1)S(1)}, u32[]{:S(2)}, u32[]{:S(2)}) collective-permute-start(bf16[16,128]{1,0:T(8,128)(2,1)S(1)} %get-tuple-element.21), channel_id=1, source_target_pairs={{0,4},{4,8},{8,12},{12,16},{16,20},{20,24},{24,28},{28,32},{32,36}... | collective-permute-start | bytes 12296 | tf_op jit(solution)/shard_map/ppermute | solution.py:514

commit v5 on v4

--- a/solution.py
+++ b/solution.py
@@ -80,12 +80,16 @@
 
 
 def upward_kernel(
-    size_hbm, x_hbm, basis_hbm, transfer_hbm, pay_ref,
-    size_ref, x_ref, basis_ref, transfer_ref, masked_ref, map_ref, sems,
+    size_hbm, x_hbm, basis_hbm, transfer_hbm, near_hbm, nodes_hbm, links_hbm,
+    pay_ref, masked_ref, limits_ref, basis_ref, transfer_ref, near_ref, nodes_ref, links_ref,
+    size_ref, x_ref, map_ref, sems,
 ):
     copies = start_all(
         sems,
-        [(x_hbm, x_ref), (size_hbm, size_ref), (basis_hbm, basis_ref), (transfer_hbm, transfer_ref)],
+        [
+            (x_hbm, x_ref), (size_hbm, size_ref), (basis_hbm, basis_ref), (transfer_hbm, transfer_ref),
+            (near_hbm, near_ref), (nodes_hbm.at[pl.ds(2, 14)], nodes_ref), (links_hbm, links_ref),
+        ],
     )
     lo = low_half(16)
     map_ref[...] = split_map()
@@ -122,26 +126,22 @@
     pay_ref[:, COEFF : COEFF + 128] = jnp.concatenate([high, packed - high], axis=0).astype(BF16)
     pay_ref[:, COEFF + 128 : COEFF + 256] = tile(masked_ref, 0)
     pay_ref[:, COEFF + 256 : COEFF + 384] = tile(masked_ref, 15)
+    for n in range(32):
+        limits_ref[n : n + 1, :] = jnp.full((1, 128), size_ref[n], I32)
+    for copy in copies[4:]:
+        copy.wait()
 
 
 def near_kernel(
-    size_hbm, x_hbm, near_hbm, basis_hbm, transfer_hbm, pay_ref,
-    field_ref, basis_rows, carry_rows, share_ref,
-    size_ref, x_ref, near_ref, basis_ref, transfer_ref, masked_ref, raw_ref, sems,
+    kept_ref, limits_ref, near_ref, basis_ref, transfer_ref, nodes_ref, pay_ref,
+    field_ref, basis_rows, carry_rows, edge_ref, share_ref, node_rows,
+    masked_ref, raw_ref, node_raw,
 ):
-    copies = start_all(
-        sems,
-        [
-            (basis_hbm, basis_ref), (transfer_hbm, transfer_ref), (x_hbm, x_ref), (size_hbm, size_ref),
-            (near_hbm, near_ref),
-        ],
-    )
     share_ref[...] = tile(pay_ref, 16)
+    lane = iota((16, 128), 1)
     collect = group_map()
     half = low_half(64)
     row = iota((64, 128), 0)
-    for copy in copies:
-        copy.wait()
     for g in range(4):
         raw = dot(collect, jnp.concatenate([basis_ref[g], transfer_ref[g]], axis=1))
         for n in range(2):
@@ -149,7 +149,7 @@
         for q in range(4):
             j = 4 * g + q
             pair = [raw_ref[2 * g, 128 * q + 64 * m : 128 * q + 64 * m + 64, :] for m in range(2)]
-            pair = [jnp.where(row < size_ref[2 * j + m], pair[m], 0.0) for m in range(2)]
+            pair = [jnp.where(row < limits_ref[2 * j + m : 2 * j + m + 1, :], pair[m], 0.0) for m in range(2)]
             start = 64 * j
             basis_rows[start : start + 64, :] = jnp.where(half, *pair).astype(BF16)
             blocks = jnp.concatenate([jnp.where(half, pair[0], 0.0), jnp.where(half, 0.0, pair[1])], axis=0)
@@ -157,8 +157,7 @@
             carry_rows[start : start + 64, :] = jnp.where(half, carry[:64], carry[64:]).astype(BF16)
     masked_ref[:, 0:128] = jnp.zeros((16, 128), BF16)
     masked_ref[:, 17 * 128 : 18 * 128] = jnp.zeros((16, 128), BF16)
-    for j in range(TILES):
-        masked_ref[:, 128 * j + 128 : 128 * j + 256] = kept(size_ref, x_ref, j).astype(BF16)
+    masked_ref[:, 128 : 17 * 128] = kept_ref[...]
     lo = low_half(16)
     for pair in range(2):
         for s in range(3):
@@ -175,17 +174,30 @@
             inner = jnp.concatenate([jnp.where(half, a[1], a[2]), jnp.where(half, b[0], b[1])], axis=0)
             outer = jnp.concatenate([jnp.where(half, 0.0, a[0]), jnp.where(half, b[2], 0.0)], axis=0)
             if j in (0, 15):
-                start = 1024 + 128 * (j // 15)
-                limit = jnp.where(iota((128, 128), 0) < 64, size_ref[2 * j], size_ref[2 * j + 1])
-                edge = jnp.where((iota((128, 128), 0) & 63) < limit, outer, 0.0)
-                carry_rows[start : start + 128, :] = edge.astype(BF16)
+                edge = jnp.concatenate(
+                    [
+                        jnp.where(row < limits_ref[2 * j + m : 2 * j + m + 1, :], outer[64 * m : 64 * m + 64], 0.0)
+                        for m in range(2)
+                    ],
+                    axis=0,
+                )
+                edge_ref[j // 15] = edge.astype(BF16)
             outer = outer.astype(BF16)
             around = jnp.where(lo, tile(masked_ref, j + 2), tile(masked_ref, j))
             near = dot_t(
                 jnp.concatenate([tile(masked_ref, j + 1), around], axis=1),
                 jnp.concatenate([inner.astype(BF16), outer], axis=1),
             )
-            field_ref[:, 128 * j : 128 * j + 128] = jnp.where(present(size_ref, j), near, 0.0)
+            field_ref[:, 128 * j : 128 * j + 128] = jnp.where(
+                (lane & 63) < jnp.where(lane < 64, limits_ref[2 * j : 2 * j + 1, :], limits_ref[2 * j + 1 : 2 * j + 2, :]),
+                near,
+                0.0,
+            )
+    for g in range(0, 14, 2):
+        raw = dot(collect, jnp.concatenate([nodes_ref[g], nodes_ref[g + 1]], axis=1))
+        for n in range(2):
+            plain_rows(raw[:, 128 * n : 128 * n + 128], node_raw.at[(g + n) % 4])
+            node_rows[512 * (g + n) : 512 * (g + n) + 512, :] = node_raw[(g + n) % 4].astype(BF16)
 
 
 def message_kernel(share_ref, one_ref, two_ref, three_ref, out_ref, cross_ref, sides_ref):
@@ -202,25 +214,27 @@
 
 
 def middle_kernel(
-    nodes_hbm, node_coupling_hbm, links_hbm, node_links_hbm, coupling_hbm,
-    own_ref, two_ref, three_ref, one_ref, near_ref, basis_ref,
-    rows_ref, coupled_ref, field_ref, node_links_ref,
-    links_ref, nodes_ref, node_coupling_ref, coupling_ref,
-    raw_ref, coeff_ref, picked_ref, spread_ref, sems,
+    node_coupling_hbm, links_vmem, node_links_hbm, coupling_hbm, rows_ref,
+    own_ref, two_ref, three_ref, one_ref, near_ref, basis_ref, carry_rows,
+    coupled_ref, field_ref, carry_ref, node_links_ref,
+    links_ref, node_coupling_ref, coupling_ref, coeff_ref, picked_ref, spread_ref, sems,
 ):
     branch = lax.axis_index("leaf")
     own = [64 + branch, 32 + (branch >> 1), 16 + (branch >> 2), 8 + (branch >> 3)]
     sources = (own_ref, one_ref, two_ref, three_ref)
     copies = start_all(
         sems,
-        [(nodes_hbm.at[pl.ds(2, 14)], nodes_ref)]
+        [(links_vmem, links_ref)]
+        + [(coupling_hbm.at[pl.ds(8 * n, 8)], coupling_ref.at[pl.ds(8 * n, 8)]) for n in range(4)]
         + [(node_coupling_hbm.at[:, own[n] >> 3], node_coupling_ref.at[n]) for n in range(4)]
-        + [(links_hbm, links_ref)]
-        + [(coupling_hbm.at[pl.ds(8 * n, 8)], coupling_ref.at[pl.ds(8 * n, 8)]) for n in range(4)]
         + [(node_links_hbm, node_links_ref)],
     )
-    collect = group_map()
     split = split_map()
+    unit = jnp.where(iota((128, 128), 0) == iota((128, 128), 1), 1.0, 0.0).astype(BF16)
+    for j in range(TILES):
+        rows = carry_rows[64 * j : 64 * j + 64, :]
+        turned = dot_t(unit, jnp.concatenate([rows, rows], axis=0))
+        carry_ref[:, 128 * j : 128 * j + 128] = jnp.where(low_half(64), turned[:64], turned[64:]).astype(BF16)
     lo = low_half(16)
     nothing = jnp.zeros((16, 128), BF16)
     half = low_half(64)
@@ -234,7 +248,7 @@
             for m, (a, b) in enumerate(((x, y), (y, x))):
                 coeff_ref[0, first + 2 * j + m] = jnp.where(lo, a, nothing)
                 coeff_ref[1, first + 2 * j + m] = jnp.where(lo, nothing, b)
-    copies[5].wait()
+    copies[0].wait()
     for leaf in range(32):
         for c in range(4):
             picked_ref[16 * leaf : 16 * leaf + 16, 128 * c : 128 * c + 128] = (
@@ -242,14 +256,8 @@
                 + coeff_ref[1, links_ref[2 * c + 1, leaf] & 127]
             )
     spread_ref[...] = dot(picked_ref[...], split).astype(BF16)
-    for copy in copies[:5] + copies[6:]:
+    for copy in copies[1:]:
         copy.wait()
-    for g in range(0, 14, 2):
-        raw = dot(collect, jnp.concatenate([nodes_ref[g], nodes_ref[g + 1]], axis=1))
-        for n in range(2):
-            plain_rows(raw[:, 128 * n : 128 * n + 128], raw_ref.at[n])
-            rows_ref[512 * (g + n) : 512 * (g + n) + 512, :] = raw_ref[n].astype(BF16)
-
     half = low_half(64)
     row, col = iota((64, 256), 0), iota((64, 256), 1)
     even = (iota((64, 128), 0) & 1) == 0
@@ -300,13 +308,11 @@
 
 
 def downward_kernel(
-    links_ref, sides_ref, cross_ref, message_ref,
-    field_ref, carry_ref, nodes_ref, coupled_ref,
+    node_links_ref, sides_ref, cross_ref, message_ref,
+    field_ref, carry_ref, edge_ref, nodes_ref, coupled_ref,
     out_ref,
-    node_links_ref, table_ref, sem,
+    table_ref,
 ):
-    copy = pltpu.make_async_copy(links_ref, node_links_ref, sem)
-    copy.start()
     branch, sub = lax.axis_index("leaf"), lax.axis_index("sub")
     lo = low_half(16)
     lo8 = low_half(8)
@@ -335,7 +341,6 @@
         value = dot(jnp.where(lo32, *children), weights(k))
         return jnp.concatenate(pieces(value[:16] + value[16:]), axis=0)
 
-    copy.wait()
     ends = [[node_links_ref[m, (64 >> n) + (branch >> n)] for m in range(3)] for n in range(4)]
     sixteen = ends[2] + [2 * k + m for k in ends[3] for m in range(2)]
     values = [parent(k, [table_ref[2 * k - 32], table_ref[2 * k - 31]]) for k in sixteen]
@@ -351,23 +356,21 @@
     down = dot(jnp.concatenate(sources, axis=1), coupled_ref[...])
     down = down[:16] + down[16:]
     down = (down + swap(down)).astype(BF16)
-    ends = jnp.concatenate([jnp.where(lo, down, zeros), jnp.where(lo, zeros, down)], axis=0)
-    shared = dot_t(ends, carry_ref[0:1024, :])
+    shared = dot(down[:, :64], carry_ref[...])
     left = jnp.where(lo, zeros, jnp.where(sub == 0, cross_ref[...], sides_ref[0]))
     right = jnp.where(lo, jnp.where(sub == 3, cross_ref[...], sides_ref[1]), zeros)
-    for t in range(8):
-        a, b = shared[:16, 128 * t : 128 * t + 128], shared[16:, 128 * t : 128 * t + 128]
-        for j, far in ((2 * t, jnp.where(lo, a, swap(b))), (2 * t + 1, jnp.where(lo, swap(a), b))):
-            out = far + tile(field_ref, j)
-            if j == 0:
-                out = out + dot_t(left, carry_ref[1024:1152, :])
-            if j == 15:
-                out = out + dot_t(right, carry_ref[1152:1280, :])
-            out_ref[:, 128 * j : 128 * j + 128] = out.astype(BF16)
+    for j in range(TILES):
+        out = shared[:, 128 * j : 128 * j + 128] + tile(field_ref, j)
+        if j == 0:
+            out = out + dot_t(left, edge_ref[0])
+        if j == 15:
+            out = out + dot_t(right, edge_ref[1])
+        out_ref[:, 128 * j : 128 * j + 128] = out.astype(BF16)
 
 
 VMEM = pl.BlockSpec(memory_space=pltpu.VMEM)
 HBM = pl.BlockSpec(memory_space=pltpu.HBM)
+SMEM = pl.BlockSpec(memory_space=pltpu.SMEM)
 
 
 def shape(dims, dtype=BF16):
@@ -386,7 +389,7 @@
     return pltpu.with_memory_space_constraint(x, pltpu.VMEM)
 
 
-def call(kernel, name, outs, in_specs, out_specs, scratch, size, mib):
+def call(kernel, name, outs, in_specs, out_specs, scratch, size, mib, aliases={}):
     return pl.pallas_call(
         kernel,
         out_shape=outs,
@@ -395,6 +398,7 @@
         scratch_shapes=scratch,
         compiler_params=pltpu.CompilerParams(vmem_limit_bytes=mib << 20),
         cost_estimate=pl.CostEstimate(flops=10**9, bytes_accessed=size, transcendentals=0),
+        input_output_aliases=aliases,
         name=name,
     )
 
@@ -405,15 +409,17 @@
 
 def upward(*args):
     return call(
-        upward_kernel, "upward", shape((16, PAYLOAD)), [HBM] * 4, VMEM,
+        upward_kernel, "upward",
+        [
+            shape((16, PAYLOAD)), pinned((16, 2048)), pinned((32, 128), I32), pinned((4, 256, 128)),
+            pinned((4, 256, 128)), pinned((3, 4, 256, 128)), pinned((14, 256, 128)), pinned((8, 32), I32),
+        ],
+        [HBM] * 7, [VMEM] * 8,
         [
             pltpu.SMEM((32,), I32),
             pltpu.VMEM((16, 2048), BF16),
-            pltpu.VMEM((4, 256, 128), BF16),
-            pltpu.VMEM((4, 256, 128), BF16),
-            pltpu.VMEM((16, 2048), BF16),
             pltpu.VMEM((512, 512), BF16),
-            dma(4),
+            dma(7),
         ],
         10**6, 8,
     )(*args)
@@ -423,18 +429,15 @@
     return call(
         near_kernel, "near",
         [
-            pinned((16, 2048), F32), pinned((1024, 128)), pinned((1280, 128)), pinned((16, 128)),
+            pinned((16, 2048), F32), pinned((1024, 128)), pinned((1024, 128)), pinned((2, 128, 128)),
+            pinned((16, 128)),
+            pinned((56 * 128, 128)),
         ],
-        [HBM] * 5 + [VMEM], [VMEM] * 4,
+        [VMEM] * 7, [VMEM] * 6,
         [
-            pltpu.SMEM((32,), I32),
-            pltpu.VMEM((16, 2048), BF16),
-            pltpu.VMEM((3, 4, 256, 128), BF16),
-            pltpu.VMEM((4, 256, 128), BF16),
-            pltpu.VMEM((4, 256, 128), BF16),
             pltpu.VMEM((16, 18 * 128), BF16),
             pltpu.VMEM((8, 512, 128), F32),
-            dma(5),
+            pltpu.VMEM((4, 512, 128), F32),
         ],
         3 * 10**6, 12,
     )(*args)
@@ -450,27 +453,25 @@
 def middle(*args):
     return call(
         middle_kernel, "middle",
-        [pinned((56 * 128, 128)), pinned((1024, 128)), pinned((16, 2048), F32), pinned((3, 128), I32)],
-        [HBM] * 5 + [VMEM] * 6, [VMEM] * 4,
+        [pinned((1024, 128)), pinned((16, 2048), F32), pinned((64, 2048)), pltpu.SMEM((3, 128), I32)],
+        [HBM, VMEM, HBM, HBM] + [VMEM] * 8, [VMEM] * 3 + [SMEM],
         [
             pltpu.SMEM((8, 32), I32),
-            pltpu.VMEM((14, 256, 128), BF16),
             pltpu.VMEM((4, 3, 256, 128), BF16),
             pltpu.VMEM((32, 256, 128), BF16),
-            pltpu.VMEM((2, 512, 128), F32),
             pltpu.VMEM((2, 128, 16, 128), BF16),
             pltpu.VMEM((512, 512), BF16),
             pltpu.VMEM((512, 512), BF16),
-            dma(11),
+            dma(10),
         ],
-        6 * 10**6, 16,
+        6 * 10**6, 16, {9: 1},
     )(*args)
 
 
 def downward(*args):
     return call(
-        downward_kernel, "downward", shape((16, 2048)), [VMEM] * 8, VMEM,
-        [pltpu.SMEM((3, 128), I32), pltpu.VMEM((32, 32, 128), BF16), pltpu.SemaphoreType.DMA],
+        downward_kernel, "downward", shape((16, 2048)), [SMEM] + [VMEM] * 8, VMEM,
+        [pltpu.VMEM((32, 32, 128), BF16)],
         4 * 10**6, 8,
     )(*args)
 
@@ -497,14 +498,14 @@
             node_links.T,
         ),
     )
-    payload = upward(leaf_size, vectors, basis, transfer)
+    payload, *tables = upward(leaf_size, vectors, basis, transfer, near, nodes, links)
+    kept_points, limits, basis, transfer, near, nodes, links = map(near_by, tables)
     others = [
         lax.ppermute(payload, "sub", [(s, s ^ d) for s in range(4)]) for d in (1, 2, 3)
     ]
-    near_part, basis_p, carry, share = near_field(
-        leaf_size, vectors, near, basis, transfer, payload
-    )
-
+    near_part, basis_p, carry, edge, share, nodes_p = near_field(
+        kept_points, limits, near, basis, transfer, nodes, payload
+    )
     messages, cross, sides = message(share, *others)
     summed = lax.all_to_all(messages, "leaf", 0, 0)
 
@@ -513,13 +514,13 @@
     routes += [(4 * b + 3, 4 * b - 1) for b in range(1, branches)]
     cross = lax.ppermute(cross, ("leaf", "sub"), routes)
 
-    nodes_p, coupled, field, partners = middle(
-        nodes, node_coupled, links, node_links, coupling, payload, others[1], others[2], others[0],
-        near_by(near_part), near_by(basis_p),
+    coupled, field, turned, partners = middle(
+        node_coupled, links, node_links, coupling, near_by(nodes_p), payload, others[1], others[2], others[0],
+        near_by(near_part), near_by(basis_p), near_by(carry),
     )
     return downward(
-        near_by(partners), sides, cross, summed,
-        *map(near_by, (field, carry, nodes_p, coupled)),
+        pltpu.with_memory_space_constraint(partners, pltpu.SMEM), sides, cross, summed,
+        *map(near_by, (field, turned, edge, nodes_p, coupled)),
     )
 
 

time: 37.1 us -> 36.8 us (level)
  Pallas kernels: 12.6 us -> 10.9 us
  waiting for transfers between devices: 3.79 us -> 5.16 us
    pallas_call x3, Pallas kernels: 8.64 us -> 7.41 us  [the longest x1 3.74 us: middle(): call(middle_kernel, 'middle', [pinned((1024, 128)), pinned((16, 2048), F3...]
    all_to_all x1, waiting for transfers between devices: 2.09 us -> 3.05 us  [body(): summed = lax.all_to_all(messages, 'leaf', 0, 0)]
    ppermute x3, waiting for transfers between devices: 1.7 us -> 2.11 us  [body(): lax.ppermute(payload, 'sub', [(s, s ^ d) for s in range(4)])]
    pallas_call x1, Pallas kernels: 3.28 us -> 2.88 us  [near_field(): call(near_kernel, 'near', [pinned((16, 2048), F32), pinned((1024, 128)),...]
  transfers between devices with their start and end apart: 5 -> 5, of which waited for: 2 -> 2; matrix products, arithmetic and copies ran while one was open for 0% -> 0% of each run, Pallas kernels for 22% -> 18%
where the time goes in v5:
time: 36.8 us; the launch traced here: 36.6 us
  starting transfers between devices  20.4 us (55%)
  Pallas kernels  10.9 us (30%)
  waiting for transfers between devices  5.16 us (14%)
    all_to_all x1, starting transfers between devices, body(): summed = lax.all_to_all(messages, 'leaf', 0, 0)  12.3 us
    ppermute x3, starting transfers between devices, body(): lax.ppermute(payload, 'sub', [(s, s ^ d) for s in range(4)])  4.61 us
    pallas_call x1, Pallas kernels, middle(): call(middle_kernel, 'middle', [pinned((1024, 128)), pinned((16, 2048), F3...  3.74 us
    ppermute x1, starting transfers between devices, body(): cross = lax.ppermute(cross, ('leaf', 'sub'), routes)  3.54 us
    all_to_all x1, waiting for transfers between devices, body(): summed = lax.all_to_all(messages, 'leaf', 0, 0)  3.05 us
    pallas_call x1, Pallas kernels, near_field(): call(near_kernel, 'near', [pinned((16, 2048), F32), pinned((1024, 128)),...  2.88 us
    ppermute x3, waiting for transfers between devices, body(): lax.ppermute(payload, 'sub', [(s, s ^ d) for s in range(4)])  2.11 us
    pallas_call x1, Pallas kernels, upward(): call(upward_kernel, 'upward', [shape((16, PAYLOAD)), pinned((16, 2048)),...  1.89 us
  transfers between devices with their start and end apart: 5, of which 2 were waited for; matrix products, arithmetic and copies ran while one was open for 0% of the time, Pallas kernels for 18%

profile of v5, /device:TPU:1, one launch (start us, length us, event | category | flops | bytes accessed | tf_op | source)
XLA Modules:
  0.0 36.6 jit_solution(2064200903715939626)
XLA Ops:
  0.0 1.9 %upward.1 = (bf16[16,2432]{1,0:T(8,128)(2,1)S(1)}, bf16[16,2048]{1,0:T(8,128)(2,1)S(1)}, s32[32,128]{1,0:T(8,128)S(1)}, bf16[4,256,128]{2,1,0:T(8,128)(2,1)S(1)}...) custom-call(s32[32]{0:T(128)} %size_hbm.1, ...), custom_call_target="tpu_custom_call" | custom-call | flops 1000000000 | bytes 1000000 | tf_op jit(solution)/shard_map/upward/pallas_call | solution.py:411
  1.9 3.8 %collective-permute-start = (bf16[16,2432]{1,0:T(8,128)(2,1)S(1)}, bf16[16,2432]{1,0:T(8,128)(2,1)S(1)}, u32[]{:S(2)}, u32[]{:S(2)}) collective-permute-start(bf16[16,2432]{1,0:T(8,128)(2,1)S(1)} %get-tuple-element.33.pay_ref.own_ref), channel_id=1, source_target_pairs={{0,2},{1,3},{2,0},{3,1},{4,6},{5,7},{6,4},{7,5},{8,10},{9,11},{10,... | collective-permute-start | bytes 233480 | tf_op jit(solution)/shard_map/ppermute | solution.py:504
  5.7 0.8 %collective-permute-start.1 = (bf16[16,2432]{1,0:T(8,128)(2,1)S(1)}, bf16[16,2432]{1,0:T(8,128)(2,1)S(1)}, u32[]{:S(2)}, u32[]{:S(2)}) collective-permute-start(bf16[16,2432]{1,0:T(8,128)(2,1)S(1)} %get-tuple-element.33.pay_ref.own_ref), channel_id=1, source_target_pairs={{0,3},{1,2},{2,1},{3,0},{4,7},{5,6},{6,5},{7,4},{8,11},{9,10},{10,... | collective-permute-start | bytes 233480 | tf_op jit(solution)/shard_map/ppermute | solution.py:504
  6.5 0.0 collective-permute-start.2
  6.5 2.9 %near.1 = (f32[16,2048]{1,0:T(8,128)S(1)}, bf16[1024,128]{1,0:T(8,128)(2,1)S(1)}, bf16[1024,128]{1,0:T(8,128)(2,1)S(1)}, bf16[2,128,128]{2,1,0:T(8,128)(2,1)S(1)...) custom-call(bf16[16,2048]{1,0:T(8,128)(2,1)S(1)} %get-tuple-element.27.kept_ref, ...), custom_call_target="tpu_custom_call" | custom-call | flops 1000000000 | bytes 3000000 | tf_op jit(solution)/shard_map/near/pallas_call | solution.py:429
  9.4 0.0 collective-permute-done.two_ref
  9.4 2.1 %collective-permute-done.1.three_ref = bf16[16,2432]{1,0:T(8,128)(2,1)S(1)} collective-permute-done((bf16[16,2432]{1,0:T(8,128)(2,1)S(1)}, bf16[16,2432]{1,0:T(8,128)(2,1)S(1)}, u32[]{:S(2)}, u32[]{:S(2)}) %collective-permute-start.1) | collective-permute-done | bytes 77856 | tf_op jit(solution)/shard_map/ppermute | solution.py:504
  11.5 0.0 collective-permute-done.2.one_ref
  11.5 0.7 %message.1 = (bf16[64,8,128]{2,1,0:T(8,128)(2,1)}, bf16[16,128]{1,0:T(8,128)(2,1)S(1)}, bf16[2,16,128]{2,1,0:T(8,128)(2,1)S(1)}) custom-call(bf16[16,128]{1,0:T(8,128)(2,1)S(1)} %get-tuple-element.39.share_ref, bf16[16,2432]{1,0:T(8,128)(2,1)S(1)} %collective-permute-done.2.one_ref, bf16[16,2432]{1,0:T(8,128)(2,1)S(1)} %collective-permute-done.two_ref, ...), custom_call_target="tpu_custom_call" | custom-call | flops 1000000000 | bytes 100000 | tf_op jit(solution)/shard_map/message/pallas_call | solution.py:447
  12.2 12.3 %all-to-all-start = ((bf16[64,8,128]{2,1,0:T(8,128)(2,1)}), bf16[64,8,128]{2,1,0:T(8,128)(2,1)S(1)}, u32[]{:S(2)}, u32[]{:S(2)}) async-start(bf16[64,8,128]{2,1,0:T(8,128)(2,1)} %get-tuple-element.42), calls=%async_computation | async-start | bytes 262144 | tf_op jit(solution)/shard_map/all_to_all | solution.py:510
  24.5 3.5 %collective-permute-start.3 = (bf16[16,128]{1,0:T(8,128)(2,1)S(1)}, bf16[16,128]{1,0:T(8,128)(2,1)S(1)}, u32[]{:S(2)}, u32[]{:S(2)}) collective-permute-start(bf16[16,128]{1,0:T(8,128)(2,1)S(1)} %get-tuple-element.41), channel_id=1, source_target_pairs={{0,4},{4,8},{8,12},{12,16},{16,20},{20,24},{24,28},{28,32},{32,36}... | collective-permute-start | bytes 12296 | tf_op jit(solution)/shard_map/ppermute | solution.py:515
  28.0 3.7 %middle.1 = (bf16[1024,128]{1,0:T(8,128)(2,1)S(1)}, f32[16,2048]{1,0:T(8,128)S(1)}, bf16[64,2048]{1,0:T(8,128)(2,1)S(1)}, s32[3,128]{1,0:T(4,128)S(4)}) custom-call(bf16[3,16,256,128]{3,2,1,0:T(8,128)(2,1)} %bitcast.36, s32[8,32]{1,0:T(8,128)S(1)} %get-tuple-element.26.links_vmem, s32[3,128]{1,0:T(4,128)} %bitcast.38, ...), custom_call_target="tpu_custom_call", output_to_operand_aliasing={{1}: (9, {})} | custom-call | flops 1000000000 | bytes 6000000 | tf_op jit(solution)/shard_map/middle/pallas_call | solution.py:454
  31.8 0.0 collective-permute-done.3.cross_ref
  31.8 3.1 %all-to-all-done.message_ref = bf16[64,8,128]{2,1,0:T(8,128)(2,1)S(1)} async-done(((bf16[64,8,128]{2,1,0:T(8,128)(2,1)}), bf16[64,8,128]{2,1,0:T(8,128)(2,1)S(1)}, u32[]{:S(2)}, u32[]{:S(2)}) %all-to-all-start) | async-done | bytes 131104 | tf_op jit(solution)/shard_map/all_to_all | solution.py:510
  34.8 1.8 %downward.1 = bf16[16,2048]{1,0:T(8,128)(2,1)} custom-call(s32[3,128]{1,0:T(4,128)S(4)} %get-tuple-element.38.node_links_ref, bf16[2,16,128]{2,1,0:T(8,128)(2,1)S(1)} %get-tuple-element.40.sides_ref, bf16[16,128]{1,0:T(8,128)(2,1)S(1)} %collective-permute-done.3.cross_ref, bf16[64,8,128]{2,1,0:T(8,128)(2,1)S(1)} %all-to-all-done.message_ref, ...), custom_call_target="tpu_custom_call" | custom-call | flops 1000000000 | bytes 4000000 | tf_op jit(solution)/shard_map/downward/pallas_call | solution.py:472
Async XLA Ops:
  1.9 7.5 %collective-permute-start = (bf16[16,2432]{1,0:T(8,128)(2,1)S(1)}, bf16[16,2432]{1,0:T(8,128)(2,1)S(1)}, u32[]{:S(2)}, u32[]{:S(2)}) collective-permute-start(bf16[16,2432]{1,0:T(8,128)(2,1)S(1)} %get-tuple-element.33.pay_ref.own_ref), channel_id=1, source_target_pairs={{0,2},{1,3},{2,0},{3,1},{4,6},{5,7},{6,4},{7,5},{8,10},{9,11},{10,... | collective-permute-start | bytes 233480 | tf_op jit(solution)/shard_map/ppermute | solution.py:504
  5.7 5.8 %collective-permute-start.1 = (bf16[16,2432]{1,0:T(8,128)(2,1)S(1)}, bf16[16,2432]{1,0:T(8,128)(2,1)S(1)}, u32[]{:S(2)}, u32[]{:S(2)}) collective-permute-start(bf16[16,2432]{1,0:T(8,128)(2,1)S(1)} %get-tuple-element.33.pay_ref.own_ref), channel_id=1, source_target_pairs={{0,3},{1,2},{2,1},{3,0},{4,7},{5,6},{6,5},{7,4},{8,11},{9,10},{10,... | collective-permute-start | bytes 233480 | tf_op jit(solution)/shard_map/ppermute | solution.py:504
  6.5 5.0 %collective-permute-start.2 = (bf16[16,2432]{1,0:T(8,128)(2,1)S(1)}, bf16[16,2432]{1,0:T(8,128)(2,1)S(1)}, u32[]{:S(2)}, u32[]{:S(2)}) collective-permute-start(bf16[16,2432]{1,0:T(8,128)(2,1)S(1)} %get-tuple-element.33.pay_ref.own_ref), channel_id=1, source_target_pairs={{0,1},{1,0},{2,3},{3,2},{4,5},{5,4},{6,7},{7,6},{8,9},{9,8},{10,11... | collective-permute-start | bytes 233480 | tf_op jit(solution)/shard_map/ppermute | solution.py:504
  12.2 22.6 %all-to-all-start = ((bf16[64,8,128]{2,1,0:T(8,128)(2,1)}), bf16[64,8,128]{2,1,0:T(8,128)(2,1)S(1)}, u32[]{:S(2)}, u32[]{:S(2)}) async-start(bf16[64,8,128]{2,1,0:T(8,128)(2,1)} %get-tuple-element.42), calls=%async_computation | async-start | bytes 262144 | tf_op jit(solution)/shard_map/all_to_all | solution.py:510
  24.5 7.3 %collective-permute-start.3 = (bf16[16,128]{1,0:T(8,128)(2,1)S(1)}, bf16[16,128]{1,0:T(8,128)(2,1)S(1)}, u32[]{:S(2)}, u32[]{:S(2)}) collective-permute-start(bf16[16,128]{1,0:T(8,128)(2,1)S(1)} %get-tuple-element.41), channel_id=1, source_target_pairs={{0,4},{4,8},{8,12},{12,16},{16,20},{20,24},{24,28},{28,32},{32,36}... | collective-permute-start | bytes 12296 | tf_op jit(solution)/shard_map/ppermute | solution.py:515

commit v6 on v5

--- a/solution.py
+++ b/solution.py
@@ -81,7 +81,7 @@
 
 def upward_kernel(
     size_hbm, x_hbm, basis_hbm, transfer_hbm, near_hbm, nodes_hbm, links_hbm,
-    pay_ref, masked_ref, limits_ref, basis_ref, transfer_ref, near_ref, nodes_ref, links_ref,
+    pay_ref, small_ref, masked_ref, limits_ref, basis_ref, transfer_ref, near_ref, nodes_ref, links_ref,
     size_ref, x_ref, map_ref, sems,
 ):
     copies = start_all(
@@ -126,6 +126,7 @@
     pay_ref[:, COEFF : COEFF + 128] = jnp.concatenate([high, packed - high], axis=0).astype(BF16)
     pay_ref[:, COEFF + 128 : COEFF + 256] = tile(masked_ref, 0)
     pay_ref[:, COEFF + 256 : COEFF + 384] = tile(masked_ref, 15)
+    small_ref[...] = tile(pay_ref, 16)
     for n in range(32):
         limits_ref[n : n + 1, :] = jnp.full((1, 128), size_ref[n], I32)
     for copy in copies[4:]:
@@ -200,10 +201,13 @@
             node_rows[512 * (g + n) : 512 * (g + n) + 512, :] = node_raw[(g + n) % 4].astype(BF16)
 
 
-def message_kernel(share_ref, one_ref, two_ref, three_ref, out_ref, cross_ref, sides_ref):
+def message_kernel(
+    share_ref, one_ref, two_ref, three_ref, own_ref, out_ref, cross_ref, sides_ref, again_ref
+):
     total = share_ref[...].astype(F32)
-    for ref in (one_ref, two_ref, three_ref):
-        total = total + tile(ref, 16).astype(F32)
+    for ref, at in ((one_ref, 16), (two_ref, 0), (three_ref, 16)):
+        total = total + tile(ref, at).astype(F32)
+    again_ref[...] = own_ref[:, :COEFF]
     packed = (total[:8] + total[8:]).astype(BF16)
     for n in range(64):
         out_ref[n] = packed
@@ -411,10 +415,10 @@
     return call(
         upward_kernel, "upward",
         [
-            shape((16, PAYLOAD)), pinned((16, 2048)), pinned((32, 128), I32), pinned((4, 256, 128)),
+            shape((16, PAYLOAD)), shape((16, 128)), pinned((16, 2048)), pinned((32, 128), I32), pinned((4, 256, 128)),
             pinned((4, 256, 128)), pinned((3, 4, 256, 128)), pinned((14, 256, 128)), pinned((8, 32), I32),
         ],
-        [HBM] * 7, [VMEM] * 8,
+        [HBM] * 7, [VMEM] * 9,
         [
             pltpu.SMEM((32,), I32),
             pltpu.VMEM((16, 2048), BF16),
@@ -445,7 +449,8 @@
 
 def message(*args):
     return call(
-        message_kernel, "message", [shape((64, 8, 128)), shape((16, 128)), shape((2, 16, 128))], [VMEM] * 4, [VMEM] * 3, [],
+        message_kernel, "message", [shape((64, 8, 128)), shape((16, 128)), shape((2, 16, 128)), shape((16, COEFF))],
+        [VMEM] * 5, [VMEM] * 4, [],
         10**5, 4,
     )(*args)
 
@@ -498,15 +503,17 @@
             node_links.T,
         ),
     )
-    payload, *tables = upward(leaf_size, vectors, basis, transfer, near, nodes, links)
+    payload, small, *tables = upward(leaf_size, vectors, basis, transfer, near, nodes, links)
     kept_points, limits, basis, transfer, near, nodes, links = map(near_by, tables)
     others = [
-        lax.ppermute(payload, "sub", [(s, s ^ d) for s in range(4)]) for d in (1, 2, 3)
+        lax.ppermute(small if d == 2 else payload, "sub", [(s, s ^ d) for s in range(4)])
+        for d in (1, 2, 3)
     ]
     near_part, basis_p, carry, edge, share, nodes_p = near_field(
         kept_points, limits, near, basis, transfer, nodes, payload
     )
-    messages, cross, sides = message(share, *others)
+    messages, cross, sides, again = message(share, *others, payload)
+    opposite = lax.ppermute(again, "sub", [(s, s ^ 2) for s in range(4)])
     summed = lax.all_to_all(messages, "leaf", 0, 0)
 
     branches = lax.axis_size("leaf")
@@ -515,7 +522,7 @@
     cross = lax.ppermute(cross, ("leaf", "sub"), routes)
 
     coupled, field, turned, partners = middle(
-        node_coupled, links, node_links, coupling, near_by(nodes_p), payload, others[1], others[2], others[0],
+        node_coupled, links, node_links, coupling, near_by(nodes_p), payload, opposite, others[2], others[0],
         near_by(near_part), near_by(basis_p), near_by(carry),
     )
     return downward(

time: 36.8 us -> 36.9 us (level)
  starting transfers between devices: 20.4 us -> 23.5 us
  waiting for transfers between devices: 5.16 us -> 2.12 us
    ppermute x3 -> x4, waiting for transfers between devices: 2.11 us -> 0.51 us  [the longest x3 0.46 us: body(): lax.ppermute(small if d == 2 else payload, 'sub', [(s, s ^ d) for s in ra...]
    all_to_all x1, starting transfers between devices: 12.3 us -> 13.8 us  [body(): summed = lax.all_to_all(messages, 'leaf', 0, 0)]
    all_to_all x1, waiting for transfers between devices: 3.05 us -> 1.61 us  [body(): summed = lax.all_to_all(messages, 'leaf', 0, 0)]
    ppermute x3 -> x4, starting transfers between devices: 4.61 us -> 5.97 us  [the longest x3 4.83 us: body(): lax.ppermute(small if d == 2 else payload, 'sub', [(s, s ^ d) for s in ra...]
  transfers between devices with their start and end apart: 5 -> 6, of which waited for: 2 -> 2; matrix products, arithmetic and copies ran while one was open for 0% -> 0% of each run, Pallas kernels for 18% -> 18%
where the time goes in v6:
time: 36.9 us; the launch traced here: 36.7 us
  starting transfers between devices  23.5 us (64%)
  Pallas kernels  10.9 us (30%)
  waiting for transfers between devices  2.12 us (6%)
    all_to_all x1, starting transfers between devices, body(): summed = lax.all_to_all(messages, 'leaf', 0, 0)  13.8 us
    ppermute x3, starting transfers between devices, body(): lax.ppermute(small if d == 2 else payload, 'sub', [(s, s ^ d) for s in ra...  4.83 us
    ppermute x1, starting transfers between devices, body(): cross = lax.ppermute(cross, ('leaf', 'sub'), routes)  3.81 us
    pallas_call x1, Pallas kernels, middle(): call(middle_kernel, 'middle', [pinned((1024, 128)), pinned((16, 2048), F3...  3.74 us
    pallas_call x1, Pallas kernels, near_field(): call(near_kernel, 'near', [pinned((16, 2048), F32), pinned((1024, 128)),...  2.88 us
    pallas_call x1, Pallas kernels, upward(): call(upward_kernel, 'upward', [shape((16, PAYLOAD)), shape((16, 128)), pi...  1.9 us
    pallas_call x1, Pallas kernels, downward(): call(downward_kernel, 'downward', shape((16, 2048)), [SMEM] + [VMEM] * 8,...  1.77 us
    all_to_all x1, waiting for transfers between devices, body(): summed = lax.all_to_all(messages, 'leaf', 0, 0)  1.61 us
  transfers between devices with their start and end apart: 6, of which 2 were waited for; matrix products, arithmetic and copies ran while one was open for 0% of the time, Pallas kernels for 18%

profile of v6, /device:TPU:1, one launch (start us, length us, event | category | flops | bytes accessed | tf_op | source)
XLA Modules:
  0.0 36.7 jit_solution(14012763957656034635)
XLA Ops:
  0.0 1.9 %upward.1 = (bf16[16,2432]{1,0:T(8,128)(2,1)S(1)}, bf16[16,128]{1,0:T(8,128)(2,1)S(1)}, bf16[16,2048]{1,0:T(8,128)(2,1)S(1)}, s32[32,128]{1,0:T(8,128)S(1)}, bf1...) custom-call(s32[32]{0:T(128)} %size_hbm.1, ...), custom_call_target="tpu_custom_call" | custom-call | flops 1000000000 | bytes 1000000 | tf_op jit(solution)/shard_map/upward/pallas_call | solution.py:415
  1.9 2.2 %collective-permute-start = (bf16[16,2432]{1,0:T(8,128)(2,1)S(1)}, bf16[16,2432]{1,0:T(8,128)(2,1)S(1)}, u32[]{:S(2)}, u32[]{:S(2)}) collective-permute-start(bf16[16,2432]{1,0:T(8,128)(2,1)S(1)} %get-tuple-element.35.pay_ref.own_ref), channel_id=1, source_target_pairs={{0,1},{1,0},{2,3},{3,2},{4,5},{5,4},{6,7},{7,6},{8,9},{9,8},{10,11... | collective-permute-start | bytes 233480 | tf_op jit(solution)/shard_map/ppermute | solution.py:509
  4.1 1.9 %collective-permute-start.2 = (bf16[16,2432]{1,0:T(8,128)(2,1)S(1)}, bf16[16,2432]{1,0:T(8,128)(2,1)S(1)}, u32[]{:S(2)}, u32[]{:S(2)}) collective-permute-start(bf16[16,2432]{1,0:T(8,128)(2,1)S(1)} %get-tuple-element.35.pay_ref.own_ref), channel_id=1, source_target_pairs={{0,3},{1,2},{2,1},{3,0},{4,7},{5,6},{6,5},{7,4},{8,11},{9,10},{10,... | collective-permute-start | bytes 233480 | tf_op jit(solution)/shard_map/ppermute | solution.py:509
  6.0 0.7 %collective-permute-start.1 = (bf16[16,128]{1,0:T(8,128)(2,1)S(1)}, bf16[16,128]{1,0:T(8,128)(2,1)S(1)}, u32[]{:S(2)}, u32[]{:S(2)}) collective-permute-start(bf16[16,128]{1,0:T(8,128)(2,1)S(1)} %get-tuple-element.38), channel_id=1, source_target_pairs={{0,2},{1,3},{2,0},{3,1},{4,6},{5,7},{6,4},{7,5},{8,10},{9,11},{10,... | collective-permute-start | bytes 12296 | tf_op jit(solution)/shard_map/ppermute | solution.py:509
  6.7 2.9 %near.1 = (f32[16,2048]{1,0:T(8,128)S(1)}, bf16[1024,128]{1,0:T(8,128)(2,1)S(1)}, bf16[1024,128]{1,0:T(8,128)(2,1)S(1)}, bf16[2,128,128]{2,1,0:T(8,128)(2,1)S(1)...) custom-call(bf16[16,2048]{1,0:T(8,128)(2,1)S(1)} %get-tuple-element.29.kept_ref, ...), custom_call_target="tpu_custom_call" | custom-call | flops 1000000000 | bytes 3000000 | tf_op jit(solution)/shard_map/near/pallas_call | solution.py:433
  9.6 0.5 %collective-permute-done.1.two_ref = bf16[16,128]{1,0:T(8,128)(2,1)S(1)} collective-permute-done((bf16[16,128]{1,0:T(8,128)(2,1)S(1)}, bf16[16,128]{1,0:T(8,128)(2,1)S(1)}, u32[]{:S(2)}, u32[]{:S(2)}) %collective-permute-start.1) | collective-permute-done | bytes 4128 | tf_op jit(solution)/shard_map/ppermute | solution.py:509
  10.1 0.0 collective-permute-done.one_ref
  10.1 0.0 collective-permute-done.2.three_ref
  10.1 0.7 %message.1 = (bf16[64,8,128]{2,1,0:T(8,128)(2,1)}, bf16[16,128]{1,0:T(8,128)(2,1)S(1)}, bf16[2,16,128]{2,1,0:T(8,128)(2,1)S(1)}, bf16[16,2048]{1,0:T(8,128)(2,1)S(1)}) custom-call(bf16[16,128]{1,0:T(8,128)(2,1)S(1)} %get-tuple-element.37.share_ref, bf16[16,2432]{1,0:T(8,128)(2,1)S(1)} %collective-permute-done.one_ref, ...), custom_call_target="tpu_custom_call" | custom-call | flops 1000000000 | bytes 100000 | tf_op jit(solution)/shard_map/message/pallas_call | solution.py:451
  10.8 13.8 %all-to-all-start = ((bf16[64,8,128]{2,1,0:T(8,128)(2,1)}), bf16[64,8,128]{2,1,0:T(8,128)(2,1)S(1)}, u32[]{:S(2)}, u32[]{:S(2)}) async-start(bf16[64,8,128]{2,1,0:T(8,128)(2,1)} %get-tuple-element.46), calls=%async_computation | async-start | bytes 262144 | tf_op jit(solution)/shard_map/all_to_all | solution.py:517
  24.5 1.1 %collective-permute-start.3 = (bf16[16,2048]{1,0:T(8,128)(2,1)S(1)}, bf16[16,2048]{1,0:T(8,128)(2,1)S(1)}, u32[]{:S(2)}, u32[]{:S(2)}) collective-permute-start(bf16[16,2048]{1,0:T(8,128)(2,1)S(1)} %get-tuple-element.39), channel_id=1, source_target_pairs={{0,2},{1,3},{2,0},{3,1},{4,6},{5,7},{6,4},{7,5},{8,10},{9,11},{10,... | collective-permute-start | bytes 196616 | tf_op jit(solution)/shard_map/ppermute | solution.py:516
  25.7 3.8 %collective-permute-start.4 = (bf16[16,128]{1,0:T(8,128)(2,1)S(1)}, bf16[16,128]{1,0:T(8,128)(2,1)S(1)}, u32[]{:S(2)}, u32[]{:S(2)}) collective-permute-start(bf16[16,128]{1,0:T(8,128)(2,1)S(1)} %get-tuple-element.45), channel_id=1, source_target_pairs={{0,4},{4,8},{8,12},{12,16},{16,20},{20,24},{24,28},{28,32},{32,36}... | collective-permute-start | bytes 12296 | tf_op jit(solution)/shard_map/ppermute | solution.py:522
  29.5 0.0 collective-permute-done.3.two_ref
  29.5 3.7 %middle.1 = (bf16[1024,128]{1,0:T(8,128)(2,1)S(1)}, f32[16,2048]{1,0:T(8,128)S(1)}, bf16[64,2048]{1,0:T(8,128)(2,1)S(1)}, s32[3,128]{1,0:T(4,128)S(4)}) custom-call(bf16[3,16,256,128]{3,2,1,0:T(8,128)(2,1)} %bitcast.36, s32[8,32]{1,0:T(8,128)S(1)} %get-tuple-element.28.links_vmem, s32[3,128]{1,0:T(4,128)} %bitcast.38, ...), custom_call_target="tpu_custom_call", output_to_operand_aliasing={{1}: (9, {})} | custom-call | flops 1000000000 | bytes 6000000 | tf_op jit(solution)/shard_map/middle/pallas_call | solution.py:459
  33.3 0.0 collective-permute-done.4.cross_ref
  33.3 1.6 %all-to-all-done.message_ref = bf16[64,8,128]{2,1,0:T(8,128)(2,1)S(1)} async-done(((bf16[64,8,128]{2,1,0:T(8,128)(2,1)}), bf16[64,8,128]{2,1,0:T(8,128)(2,1)S(1)}, u32[]{:S(2)}, u32[]{:S(2)}) %all-to-all-start) | async-done | bytes 131104 | tf_op jit(solution)/shard_map/all_to_all | solution.py:517
  34.9 1.8 %downward.1 = bf16[16,2048]{1,0:T(8,128)(2,1)} custom-call(s32[3,128]{1,0:T(4,128)S(4)} %get-tuple-element.43.node_links_ref, bf16[2,16,128]{2,1,0:T(8,128)(2,1)S(1)} %get-tuple-element.44.sides_ref, bf16[16,128]{1,0:T(8,128)(2,1)S(1)} %collective-permute-done.4.cross_ref, bf16[64,8,128]{2,1,0:T(8,128)(2,1)S(1)} %all-to-all-done.message_ref, ...), custom_call_target="tpu_custom_call" | custom-call | flops 1000000000 | bytes 4000000 | tf_op jit(solution)/shard_map/downward/pallas_call | solution.py:477
Async XLA Ops:
  1.9 8.2 %collective-permute-start = (bf16[16,2432]{1,0:T(8,128)(2,1)S(1)}, bf16[16,2432]{1,0:T(8,128)(2,1)S(1)}, u32[]{:S(2)}, u32[]{:S(2)}) collective-permute-start(bf16[16,2432]{1,0:T(8,128)(2,1)S(1)} %get-tuple-element.35.pay_ref.own_ref), channel_id=1, source_target_pairs={{0,1},{1,0},{2,3},{3,2},{4,5},{5,4},{6,7},{7,6},{8,9},{9,8},{10,11... | collective-permute-start | bytes 233480 | tf_op jit(solution)/shard_map/ppermute | solution.py:509
  4.1 6.0 %collective-permute-start.2 = (bf16[16,2432]{1,0:T(8,128)(2,1)S(1)}, bf16[16,2432]{1,0:T(8,128)(2,1)S(1)}, u32[]{:S(2)}, u32[]{:S(2)}) collective-permute-start(bf16[16,2432]{1,0:T(8,128)(2,1)S(1)} %get-tuple-element.35.pay_ref.own_ref), channel_id=1, source_target_pairs={{0,3},{1,2},{2,1},{3,0},{4,7},{5,6},{6,5},{7,4},{8,11},{9,10},{10,... | collective-permute-start | bytes 233480 | tf_op jit(solution)/shard_map/ppermute | solution.py:509
  6.0 4.1 %collective-permute-start.1 = (bf16[16,128]{1,0:T(8,128)(2,1)S(1)}, bf16[16,128]{1,0:T(8,128)(2,1)S(1)}, u32[]{:S(2)}, u32[]{:S(2)}) collective-permute-start(bf16[16,128]{1,0:T(8,128)(2,1)S(1)} %get-tuple-element.38), channel_id=1, source_target_pairs={{0,2},{1,3},{2,0},{3,1},{4,6},{5,7},{6,4},{7,5},{8,10},{9,11},{10,... | collective-permute-start | bytes 12296 | tf_op jit(solution)/shard_map/ppermute | solution.py:509
  10.8 24.1 %all-to-all-start = ((bf16[64,8,128]{2,1,0:T(8,128)(2,1)}), bf16[64,8,128]{2,1,0:T(8,128)(2,1)S(1)}, u32[]{:S(2)}, u32[]{:S(2)}) async-start(bf16[64,8,128]{2,1,0:T(8,128)(2,1)} %get-tuple-element.46), calls=%async_computation | async-start | bytes 262144 | tf_op jit(solution)/shard_map/all_to_all | solution.py:517
  24.5 5.0 %collective-permute-start.3 = (bf16[16,2048]{1,0:T(8,128)(2,1)S(1)}, bf16[16,2048]{1,0:T(8,128)(2,1)S(1)}, u32[]{:S(2)}, u32[]{:S(2)}) collective-permute-start(bf16[16,2048]{1,0:T(8,128)(2,1)S(1)} %get-tuple-element.39), channel_id=1, source_target_pairs={{0,2},{1,3},{2,0},{3,1},{4,6},{5,7},{6,4},{7,5},{8,10},{9,11},{10,... | collective-permute-start | bytes 196616 | tf_op jit(solution)/shard_map/ppermute | solution.py:516
  25.7 7.6 %collective-permute-start.4 = (bf16[16,128]{1,0:T(8,128)(2,1)S(1)}, bf16[16,128]{1,0:T(8,128)(2,1)S(1)}, u32[]{:S(2)}, u32[]{:S(2)}) collective-permute-start(bf16[16,128]{1,0:T(8,128)(2,1)S(1)} %get-tuple-element.45), channel_id=1, source_target_pairs={{0,4},{4,8},{8,12},{12,16},{16,20},{20,24},{24,28},{28,32},{32,36}... | collective-permute-start | bytes 12296 | tf_op jit(solution)/shard_map/ppermute | solution.py:522

commit v7 on v5

--- a/solution.py
+++ b/solution.py
@@ -310,8 +310,8 @@
 def downward_kernel(
     node_links_ref, sides_ref, cross_ref, message_ref,
     field_ref, carry_ref, edge_ref, nodes_ref, coupled_ref,
-    out_ref,
-    table_ref,
+    out_hbm,
+    table_ref, out_ref, sems,
 ):
     branch, sub = lax.axis_index("leaf"), lax.axis_index("sub")
     lo = low_half(16)
@@ -357,6 +357,7 @@
     down = down[:16] + down[16:]
     down = (down + swap(down)).astype(BF16)
     shared = dot(down[:, :64], carry_ref[...])
+    sent = []
     left = jnp.where(lo, zeros, jnp.where(sub == 0, cross_ref[...], sides_ref[0]))
     right = jnp.where(lo, jnp.where(sub == 3, cross_ref[...], sides_ref[1]), zeros)
     for j in range(TILES):
@@ -366,6 +367,12 @@
         if j == 15:
             out = out + dot_t(right, edge_ref[1])
         out_ref[:, 128 * j : 128 * j + 128] = out.astype(BF16)
+        if j % 8 == 7:
+            half = pl.ds(128 * (j - 7), 1024)
+            sent.append(pltpu.make_async_copy(out_ref.at[:, half], out_hbm.at[:, half], sems.at[j // 8]))
+            sent[-1].start()
+    for copy in sent:
+        copy.wait()
 
 
 VMEM = pl.BlockSpec(memory_space=pltpu.VMEM)
@@ -470,8 +477,8 @@
 
 def downward(*args):
     return call(
-        downward_kernel, "downward", shape((16, 2048)), [SMEM] + [VMEM] * 8, VMEM,
-        [pltpu.VMEM((32, 32, 128), BF16)],
+        downward_kernel, "downward", shape((16, 2048)), [SMEM] + [VMEM] * 8, HBM,
+        [pltpu.VMEM((32, 32, 128), BF16), pltpu.VMEM((16, 2048), BF16), dma(2)],
         4 * 10**6, 8,
     )(*args)
 

time: 36.8 us -> 36.8 us (level)
  no operation moved by 1% of the time
where the time goes in v7:
time: 36.8 us; the launch traced here: 36.6 us
  starting transfers between devices  20.4 us (55%)
  Pallas kernels  11 us (30%)
  waiting for transfers between devices  5.16 us (14%)
    all_to_all x1, starting transfers between devices, body(): summed = lax.all_to_all(messages, 'leaf', 0, 0)  12.3 us
    ppermute x3, starting transfers between devices, body(): lax.ppermute(payload, 'sub', [(s, s ^ d) for s in range(4)])  4.61 us
    pallas_call x1, Pallas kernels, middle(): call(middle_kernel, 'middle', [pinned((1024, 128)), pinned((16, 2048), F3...  3.74 us
    ppermute x1, starting transfers between devices, body(): cross = lax.ppermute(cross, ('leaf', 'sub'), routes)  3.54 us
    all_to_all x1, waiting for transfers between devices, body(): summed = lax.all_to_all(messages, 'leaf', 0, 0)  3.05 us
    pallas_call x1, Pallas kernels, near_field(): call(near_kernel, 'near', [pinned((16, 2048), F32), pinned((1024, 128)),...  2.88 us
    ppermute x3, waiting for transfers between devices, body(): lax.ppermute(payload, 'sub', [(s, s ^ d) for s in range(4)])  2.11 us
    pallas_call x1, Pallas kernels, upward(): call(upward_kernel, 'upward', [shape((16, PAYLOAD)), pinned((16, 2048)),...  1.89 us
  transfers between devices with their start and end apart: 5, of which 2 were waited for; matrix products, arithmetic and copies ran while one was open for 0% of the time, Pallas kernels for 18%

profile of v7, /device:TPU:1, one launch (start us, length us, event | category | flops | bytes accessed | tf_op | source)
XLA Modules:
  0.0 36.6 jit_solution(5647417803413458336)
XLA Ops:
  0.0 1.9 %upward.1 = (bf16[16,2432]{1,0:T(8,128)(2,1)S(1)}, bf16[16,2048]{1,0:T(8,128)(2,1)S(1)}, s32[32,128]{1,0:T(8,128)S(1)}, bf16[4,256,128]{2,1,0:T(8,128)(2,1)S(1)}...) custom-call(s32[32]{0:T(128)} %size_hbm.1, ...), custom_call_target="tpu_custom_call" | custom-call | flops 1000000000 | bytes 1000000 | tf_op jit(solution)/shard_map/upward/pallas_call | solution.py:418
  1.9 3.8 %collective-permute-start = (bf16[16,2432]{1,0:T(8,128)(2,1)S(1)}, bf16[16,2432]{1,0:T(8,128)(2,1)S(1)}, u32[]{:S(2)}, u32[]{:S(2)}) collective-permute-start(bf16[16,2432]{1,0:T(8,128)(2,1)S(1)} %get-tuple-element.33.pay_ref.own_ref), channel_id=1, source_target_pairs={{0,2},{1,3},{2,0},{3,1},{4,6},{5,7},{6,4},{7,5},{8,10},{9,11},{10,... | collective-permute-start | bytes 233480 | tf_op jit(solution)/shard_map/ppermute | solution.py:511
  5.7 0.8 %collective-permute-start.1 = (bf16[16,2432]{1,0:T(8,128)(2,1)S(1)}, bf16[16,2432]{1,0:T(8,128)(2,1)S(1)}, u32[]{:S(2)}, u32[]{:S(2)}) collective-permute-start(bf16[16,2432]{1,0:T(8,128)(2,1)S(1)} %get-tuple-element.33.pay_ref.own_ref), channel_id=1, source_target_pairs={{0,3},{1,2},{2,1},{3,0},{4,7},{5,6},{6,5},{7,4},{8,11},{9,10},{10,... | collective-permute-start | bytes 233480 | tf_op jit(solution)/shard_map/ppermute | solution.py:511
  6.5 0.0 collective-permute-start.2
  6.5 2.9 %near.1 = (f32[16,2048]{1,0:T(8,128)S(1)}, bf16[1024,128]{1,0:T(8,128)(2,1)S(1)}, bf16[1024,128]{1,0:T(8,128)(2,1)S(1)}, bf16[2,128,128]{2,1,0:T(8,128)(2,1)S(1)...) custom-call(bf16[16,2048]{1,0:T(8,128)(2,1)S(1)} %get-tuple-element.27.kept_ref, ...), custom_call_target="tpu_custom_call" | custom-call | flops 1000000000 | bytes 3000000 | tf_op jit(solution)/shard_map/near/pallas_call | solution.py:436
  9.4 0.0 collective-permute-done.two_ref
  9.4 2.1 %collective-permute-done.1.three_ref = bf16[16,2432]{1,0:T(8,128)(2,1)S(1)} collective-permute-done((bf16[16,2432]{1,0:T(8,128)(2,1)S(1)}, bf16[16,2432]{1,0:T(8,128)(2,1)S(1)}, u32[]{:S(2)}, u32[]{:S(2)}) %collective-permute-start.1) | collective-permute-done | bytes 77856 | tf_op jit(solution)/shard_map/ppermute | solution.py:511
  11.5 0.0 collective-permute-done.2.one_ref
  11.5 0.7 %message.1 = (bf16[64,8,128]{2,1,0:T(8,128)(2,1)}, bf16[16,128]{1,0:T(8,128)(2,1)S(1)}, bf16[2,16,128]{2,1,0:T(8,128)(2,1)S(1)}) custom-call(bf16[16,128]{1,0:T(8,128)(2,1)S(1)} %get-tuple-element.39.share_ref, bf16[16,2432]{1,0:T(8,128)(2,1)S(1)} %collective-permute-done.2.one_ref, bf16[16,2432]{1,0:T(8,128)(2,1)S(1)} %collective-permute-done.two_ref, ...), custom_call_target="tpu_custom_call" | custom-call | flops 1000000000 | bytes 100000 | tf_op jit(solution)/shard_map/message/pallas_call | solution.py:454
  12.2 12.3 %all-to-all-start = ((bf16[64,8,128]{2,1,0:T(8,128)(2,1)}), bf16[64,8,128]{2,1,0:T(8,128)(2,1)S(1)}, u32[]{:S(2)}, u32[]{:S(2)}) async-start(bf16[64,8,128]{2,1,0:T(8,128)(2,1)} %get-tuple-element.42), calls=%async_computation | async-start | bytes 262144 | tf_op jit(solution)/shard_map/all_to_all | solution.py:517
  24.5 3.5 %collective-permute-start.3 = (bf16[16,128]{1,0:T(8,128)(2,1)S(1)}, bf16[16,128]{1,0:T(8,128)(2,1)S(1)}, u32[]{:S(2)}, u32[]{:S(2)}) collective-permute-start(bf16[16,128]{1,0:T(8,128)(2,1)S(1)} %get-tuple-element.41), channel_id=1, source_target_pairs={{0,4},{4,8},{8,12},{12,16},{16,20},{20,24},{24,28},{28,32},{32,36}... | collective-permute-start | bytes 12296 | tf_op jit(solution)/shard_map/ppermute | solution.py:522
  28.0 3.7 %middle.1 = (bf16[1024,128]{1,0:T(8,128)(2,1)S(1)}, f32[16,2048]{1,0:T(8,128)S(1)}, bf16[64,2048]{1,0:T(8,128)(2,1)S(1)}, s32[3,128]{1,0:T(4,128)S(4)}) custom-call(bf16[3,16,256,128]{3,2,1,0:T(8,128)(2,1)} %bitcast.36, s32[8,32]{1,0:T(8,128)S(1)} %get-tuple-element.26.links_vmem, s32[3,128]{1,0:T(4,128)} %bitcast.38, ...), custom_call_target="tpu_custom_call", output_to_operand_aliasing={{1}: (9, {})} | custom-call | flops 1000000000 | bytes 6000000 | tf_op jit(solution)/shard_map/middle/pallas_call | solution.py:461
  31.8 0.0 collective-permute-done.3.cross_ref
  31.8 3.1 %all-to-all-done.message_ref = bf16[64,8,128]{2,1,0:T(8,128)(2,1)S(1)} async-done(((bf16[64,8,128]{2,1,0:T(8,128)(2,1)}), bf16[64,8,128]{2,1,0:T(8,128)(2,1)S(1)}, u32[]{:S(2)}, u32[]{:S(2)}) %all-to-all-start) | async-done | bytes 131104 | tf_op jit(solution)/shard_map/all_to_all | solution.py:517
  34.8 1.8 %downward.1 = bf16[16,2048]{1,0:T(8,128)(2,1)} custom-call(s32[3,128]{1,0:T(4,128)S(4)} %get-tuple-element.38.node_links_ref, bf16[2,16,128]{2,1,0:T(8,128)(2,1)S(1)} %get-tuple-element.40.sides_ref, bf16[16,128]{1,0:T(8,128)(2,1)S(1)} %collective-permute-done.3.cross_ref, bf16[64,8,128]{2,1,0:T(8,128)(2,1)S(1)} %all-to-all-done.message_ref, ...), custom_call_target="tpu_custom_call" | custom-call | flops 1000000000 | bytes 4000000 | tf_op jit(solution)/shard_map/downward/pallas_call | solution.py:479
Async XLA Ops:
  1.9 7.5 %collective-permute-start = (bf16[16,2432]{1,0:T(8,128)(2,1)S(1)}, bf16[16,2432]{1,0:T(8,128)(2,1)S(1)}, u32[]{:S(2)}, u32[]{:S(2)}) collective-permute-start(bf16[16,2432]{1,0:T(8,128)(2,1)S(1)} %get-tuple-element.33.pay_ref.own_ref), channel_id=1, source_target_pairs={{0,2},{1,3},{2,0},{3,1},{4,6},{5,7},{6,4},{7,5},{8,10},{9,11},{10,... | collective-permute-start | bytes 233480 | tf_op jit(solution)/shard_map/ppermute | solution.py:511
  5.7 5.8 %collective-permute-start.1 = (bf16[16,2432]{1,0:T(8,128)(2,1)S(1)}, bf16[16,2432]{1,0:T(8,128)(2,1)S(1)}, u32[]{:S(2)}, u32[]{:S(2)}) collective-permute-start(bf16[16,2432]{1,0:T(8,128)(2,1)S(1)} %get-tuple-element.33.pay_ref.own_ref), channel_id=1, source_target_pairs={{0,3},{1,2},{2,1},{3,0},{4,7},{5,6},{6,5},{7,4},{8,11},{9,10},{10,... | collective-permute-start | bytes 233480 | tf_op jit(solution)/shard_map/ppermute | solution.py:511
  6.5 5.0 %collective-permute-start.2 = (bf16[16,2432]{1,0:T(8,128)(2,1)S(1)}, bf16[16,2432]{1,0:T(8,128)(2,1)S(1)}, u32[]{:S(2)}, u32[]{:S(2)}) collective-permute-start(bf16[16,2432]{1,0:T(8,128)(2,1)S(1)} %get-tuple-element.33.pay_ref.own_ref), channel_id=1, source_target_pairs={{0,1},{1,0},{2,3},{3,2},{4,5},{5,4},{6,7},{7,6},{8,9},{9,8},{10,11... | collective-permute-start | bytes 233480 | tf_op jit(solution)/shard_map/ppermute | solution.py:511
  12.2 22.6 %all-to-all-start = ((bf16[64,8,128]{2,1,0:T(8,128)(2,1)}), bf16[64,8,128]{2,1,0:T(8,128)(2,1)S(1)}, u32[]{:S(2)}, u32[]{:S(2)}) async-start(bf16[64,8,128]{2,1,0:T(8,128)(2,1)} %get-tuple-element.42), calls=%async_computation | async-start | bytes 262144 | tf_op jit(solution)/shard_map/all_to_all | solution.py:517
  24.5 7.3 %collective-permute-start.3 = (bf16[16,128]{1,0:T(8,128)(2,1)S(1)}, bf16[16,128]{1,0:T(8,128)(2,1)S(1)}, u32[]{:S(2)}, u32[]{:S(2)}) collective-permute-start(bf16[16,128]{1,0:T(8,128)(2,1)S(1)} %get-tuple-element.41), channel_id=1, source_target_pairs={{0,4},{4,8},{8,12},{12,16},{16,20},{20,24},{24,28},{28,32},{32,36}... | collective-permute-start | bytes 12296 | tf_op jit(solution)/shard_map/ppermute | solution.py:522
